TPU v7x, 32 devices: a whole 2x2x4 slice. The times are simulated.
32 devices in a mesh: groups: 2 (over x), dp: 16 (over z, y, core).
Axes of the slice: x: 2, y: 2, z: 4, core: 2. Of those that a mesh axis runs over, the one named last changes fastest.
Arguments:
- x_rows: bfloat16 [8192, 5120], P(('groups', 'dp')), parts along dimension 0, may hold values from -6 to 6
- query_rows: bfloat16 [8192, 4096], P(('groups', 'dp')), parts along dimension 0, may hold values from -160 to 160
- key_rows: bfloat16 [8192, 512], P(('groups', 'dp')), parts along dimension 0, may hold values from -6 to 6
- values_base: bfloat16 [8192, 512], P(('groups', 'dp')), parts along dimension 0, may hold values from -6 to 6
- grad_out: bfloat16 [8192, 4096], P(('groups', 'dp')), parts along dimension 0, may hold values from -6 to 6
- adapt_down: bfloat16 [16, 64, 5120], P('dp'), may hold values from -0.078125 to 0.078125
- adapt_up: bfloat16 [16, 64, 512], P('dp'), may hold values from -0.75 to 0.75
- block_tenant: int32 [64], P(('groups', 'dp')), parts along dimension 0, may hold values from 0 to 15
- owner_map: int32 [16], replicated, may hold values from 0 to 15, each once
- seq_ids: int32 [64, 128], P(('groups', 'dp')), parts along dimension 0, may hold values from 0 to 3, never falling along the last dimension, each value on 1 to 64 neighbouring positions
Outputs:
- grad_query: bfloat16 [8192, 4096], P(('groups', 'dp')), parts along dimension 0
- grad_input_t: bfloat16 [5120, 8192], P('dp', 'groups'), parts along dimension 1
- grad_down: bfloat16 [32, 64, 5120], P(('groups', 'dp')), parts along dimension 0
- grad_up: bfloat16 [32, 64, 512], P(('groups', 'dp')), parts along dimension 0
There are 2 independent parts, one for each index of `groups`. A program takes and returns all parts, laid end to end along the dimension named above; an argument that names none is the same for every part. Nothing has to cross between parts.
All inputs are finite; a program needn't handle non-finite values.
Results may differ from a plain program's by a relative error of at most 0.0071.
Values may be sent and summed in bfloat16 or wider, within the bound.
No kernel may reach another device: no remote copies, remote signals or barrier semaphores. Data moves between devices by JAX's collectives and lax.ppermute only.
A program may use at most 128 MiB of HBM per device.

v0:
```python
import math

import jax
import jax.numpy as jnp
from jax import lax
from jax.experimental import pallas as pl
from jax.experimental.pallas import tpu as pltpu
from jax.sharding import PartitionSpec as P

HD = 128
KVH = 4
GROUP = 8
CHIPS = 4
SPAN = 16


adapter_scale = 2.0
neg_fill = -1e30


def build_mask(seg_ids, block_len):
    position = jnp.arange(seg_ids.shape[0])
    block_ids = position // block_len
    same_block = block_ids[:, None] == block_ids[None, :]
    same_seq = seg_ids[:, None] == seg_ids[None, :]
    causal = position[None, :] <= position[:, None]
    return same_block & same_seq & causal


def first_pass(query_tile, key_tile, grad_tile, keep_mask):
    tile_rows = query_tile.shape[0]
    query_heads = query_tile.reshape(tile_rows, KVH, GROUP, HD)
    key_heads = key_tile.reshape(tile_rows, KVH, HD)
    scores = jnp.einsum(
        "tkgd,skd->kgts", query_heads, key_heads, preferred_element_type=jnp.float32
    ) / math.sqrt(HD)
    scores = jnp.where(keep_mask[None, None], scores, neg_fill)
    attn_probs = jax.nn.softmax(scores, axis=-1)
    probs_b = attn_probs.astype(jnp.bfloat16)
    grad_heads = grad_tile.reshape(tile_rows, KVH, GROUP, HD)
    value_gradient = jnp.einsum(
        "kgts,tkgd->skd", probs_b, grad_heads, preferred_element_type=jnp.float32
    )
    return (attn_probs, probs_b, value_gradient.reshape(tile_rows, KVH * HD).astype(jnp.bfloat16))


def second_pass(attn_probs, probs_b, value_tile, key_tile, grad_tile):
    tile_rows = value_tile.shape[0]
    value_heads = value_tile.reshape(tile_rows, KVH, HD)
    key_heads = key_tile.reshape(tile_rows, KVH, HD)
    grad_heads = grad_tile.reshape(tile_rows, KVH, GROUP, HD)
    out_attn = jnp.einsum(
        "kgts,skd->tkgd", probs_b, value_heads, preferred_element_type=jnp.float32
    )
    dprobs = jnp.einsum(
        "tkgd,skd->kgts", grad_heads, value_heads, preferred_element_type=jnp.float32
    )
    row_delta = jnp.transpose(
        jnp.sum(grad_heads.astype(jnp.float32) * out_attn, axis=-1), (1, 2, 0)
    )[..., None]
    dscores = (attn_probs * (dprobs - row_delta)).astype(jnp.bfloat16)
    grad_heads_q = jnp.einsum(
        "kgts,skd->tkgd", dscores, key_heads, preferred_element_type=jnp.float32
    ) / math.sqrt(HD)
    return grad_heads_q.reshape(tile_rows, KVH * GROUP * HD).astype(jnp.bfloat16)


def local(
    x_rows,
    query_rows,
    key_rows,
    values_base,
    grad_out,
    adapt_down,
    adapt_up,
    block_tenant,
    owner_map,
    seq_ids,
):
    tok_rows = x_rows.shape[0]
    blk_count = block_tenant.shape[0]
    block_len = tok_rows // blk_count
    width = x_rows.shape[1]
    value_width = key_rows.shape[1]
    adapter_count = owner_map.shape[0]
    sliced_down, sliced_up = (
        lax.all_to_all(adapt_down, "dp", split_axis=1, concat_axis=0, tiled=True),
        lax.all_to_all(adapt_up, "dp", split_axis=1, concat_axis=0, tiled=True),
    )
    tenants = lax.all_gather(block_tenant, "dp", axis=0, tiled=True)
    lookup = tenants[:, None] == jnp.arange(adapter_count)[None, :]
    store_rows = jnp.sum(jnp.where(lookup, owner_map[None, :], 0), axis=1)
    picked_down = jnp.take(sliced_down, store_rows, axis=0)
    picked_up = jnp.take(sliced_up, store_rows, axis=0)
    my_down, tenant_up_weight = (
        lax.all_to_all(picked_down, "dp", split_axis=0, concat_axis=1, tiled=True),
        lax.all_to_all(picked_up, "dp", split_axis=0, concat_axis=1, tiled=True),
    )
    tile_rows = min(tok_rows, 512)
    tile_count = tok_rows // tile_rows
    query_tiles = query_rows.reshape(tile_count, tile_rows, -1)
    key_tiles = key_rows.reshape(tile_count, tile_rows, -1)
    grad_tiles = grad_out.reshape(tile_count, tile_rows, -1)
    seq_tiles = seq_ids.reshape(tile_count, tile_rows)
    keep_masks = jax.vmap(lambda ids: build_mask(ids, block_len))(seq_tiles)
    attn_probs, probs_b, value_gradient = jax.vmap(first_pass)(
        query_tiles, key_tiles, grad_tiles, keep_masks
    )
    dvalue_blocks = value_gradient.reshape(blk_count, block_len, value_width)
    x_blocks = x_rows.reshape(blk_count, block_len, width)
    hidden_rows = jnp.einsum(
        "btd,brd->btr", x_blocks, my_down, preferred_element_type=jnp.float32
    ).astype(jnp.bfloat16)
    adapter_values = jnp.einsum(
        "uzd,udv->uzv", hidden_rows, tenant_up_weight, preferred_element_type=jnp.float32
    )
    frozen_value_blocks = values_base.reshape(blk_count, block_len, value_width).astype(jnp.float32)
    value_rows = (frozen_value_blocks + adapter_scale * adapter_values).astype(jnp.bfloat16)
    hidden_gradient = (
        adapter_scale
        * jnp.einsum(
            "bte,bre->btr", dvalue_blocks, tenant_up_weight, preferred_element_type=jnp.float32
        )
    ).astype(jnp.bfloat16)
    part_down = jnp.einsum(
        "btr,btd->brd", hidden_gradient, x_blocks, preferred_element_type=jnp.float32
    )
    partial_up_weight = adapter_scale * jnp.einsum(
        "btr,bte->bre", hidden_rows, dvalue_blocks, preferred_element_type=jnp.float32
    )
    back_down, back_up = (
        lax.all_to_all(part_down, "dp", split_axis=1, concat_axis=0, tiled=True),
        lax.all_to_all(partial_up_weight, "dp", split_axis=1, concat_axis=0, tiled=True),
    )
    selector = (jnp.arange(adapter_count)[:, None] == store_rows[None, :]).astype(jnp.float32)
    sum_down = jnp.einsum("ab,brc->arc", selector, back_down, precision=lax.Precision.HIGHEST)
    sum_up = jnp.einsum("ab,brc->arc", selector, back_up, precision=lax.Precision.HIGHEST)
    grad_down, grad_up = (
        lax.all_to_all(
            sum_down.astype(jnp.bfloat16), "dp", split_axis=0, concat_axis=1, tiled=True
        ),
        lax.all_to_all(sum_up.astype(jnp.bfloat16), "dp", split_axis=0, concat_axis=1, tiled=True),
    )
    local_grad = jnp.einsum(
        "brd,btr->dbt", my_down, hidden_gradient, preferred_element_type=jnp.float32
    )
    local_grad = local_grad.reshape(width, tok_rows).astype(jnp.bfloat16)
    grad_input_t = lax.all_to_all(local_grad, "dp", split_axis=0, concat_axis=1, tiled=True)
    value_tiles = value_rows.reshape(tile_count, tile_rows, value_width)
    grad_query = jax.vmap(second_pass)(attn_probs, probs_b, value_tiles, key_tiles, grad_tiles)
    grad_query = grad_query.reshape(tok_rows, -1)
    return (grad_query, grad_input_t, grad_down, grad_up)


def cost(micros):
    return pl.CostEstimate(flops=0, bytes_accessed=int(micros * 3.3e4), transcendentals=0)


def eighth_of(device):
    return 4 * ((device >> 3) ^ (device & 1)) + ((device >> 1) & 3)


def run_copies(pairs, sems):
    copies = [pltpu.make_async_copy(src, dst, sems.at[k]) for k, (src, dst) in enumerate(pairs)]
    for copy in copies:
        copy.start()
    return copies


def columns(part, span):
    return pl.ds(pl.multiple_of(part * span, 128), span)


def pack_kernel(x_ref, down_ref, down_out, *refs):
    outs, (x_buf, down_buf, sems) = refs[: CHIPS - 1], refs[CHIPS - 1 :]
    me, group = lax.axis_index("dp"), lax.axis_index("groups")
    half, span = down_out.shape[1:]
    ranks = pl.ds(pl.multiple_of(group * half, 16), half)
    pairs = []
    for k in range(CHIPS - 1):
        chip = ((me >> 1) & 3) ^ (k + 1)
        for side in range(2):
            part = 4 * ((me >> 3) ^ side) + chip
            pairs.append((x_ref.at[:, columns(part, span)], x_buf.at[k, :, pl.ds(side * span, span)]))
    pairs.append((down_ref.at[0, ranks, :], down_buf))
    loads = run_copies(pairs, sems)
    pairs = [(x_buf.at[k], outs[k]) for k in range(CHIPS - 1)]
    for dest in range(SPAN):
        pairs.append((down_buf.at[:, pl.ds(eighth_of(dest) * span, span)], down_out.at[dest]))
    stores = [
        pltpu.make_async_copy(src, dst, sems.at[len(loads) + k])
        for k, (src, dst) in enumerate(pairs)
    ]
    for k in range(CHIPS - 1):
        loads[2 * k].wait()
        loads[2 * k + 1].wait()
        stores[k].start()
    loads[-1].wait()
    for copy in stores[CHIPS - 1 :]:
        copy.start()
    for copy in stores:
        copy.wait()


def store_kernel(tenant_ref, owner_ref, slot_ref, row_ref, wide):
    for k in range(2):
        slot_ref[k] = owner_ref[tenant_ref[k]]
    lane = lax.broadcasted_iota(jnp.int32, wide.shape, 1)
    wide[...] = jnp.where(
        lane < wide.shape[1] // 2, slot_ref[0].astype(jnp.float32), slot_ref[1].astype(jnp.float32)
    )
    row_ref[...] = wide[...].astype(jnp.bfloat16)


def heads_in_rows(ref):
    return jnp.concatenate([ref[:, h * HD : (h + 1) * HD] for h in range(GROUP)], axis=0)


def probabilities(ids, keys, queries):
    length = ids.shape[1]
    across = jnp.broadcast_to(ids.astype(jnp.float32), (length, length))
    later = lax.broadcasted_iota(jnp.int32, (length, length), 1)
    earlier = lax.broadcasted_iota(jnp.int32, (length, length), 0)
    keep = (across == across.T) & (earlier <= later)
    scores = lax.dot_general(
        keys, queries, (((1,), (1,)), ((), ())), preferred_element_type=jnp.float32
    ) * (1.0 / math.sqrt(HD))
    scores = jnp.where(jnp.concatenate([keep] * GROUP, axis=1), scores, neg_fill)
    weights = jnp.exp(scores - jnp.max(scores, axis=0, keepdims=True))
    return weights * (1.0 / jnp.sum(weights, axis=0, keepdims=True))


def first_kernel(ids_ref, query_ref, key_ref, grad_ref, dval_ref):
    ids = ids_ref[pl.ds(pl.program_id(0), 1), :]
    probs = probabilities(ids, key_ref[...], heads_in_rows(query_ref)).astype(jnp.bfloat16)
    out = jnp.dot(probs, heads_in_rows(grad_ref), preferred_element_type=jnp.float32)
    dval_ref[...] = out.astype(jnp.bfloat16)


def second_kernel(ids_ref, query_ref, key_ref, value_ref, grad_ref, out_ref):
    ids = ids_ref[pl.ds(pl.program_id(0), 1), :]
    keys = key_ref[...]
    probs = probabilities(ids, keys, heads_in_rows(query_ref))
    dprobs = lax.dot_general(
        value_ref[...],
        heads_in_rows(grad_ref),
        (((1,), (1,)), ((), ())),
        preferred_element_type=jnp.float32,
    )
    rounded = probs.astype(jnp.bfloat16).astype(jnp.float32)
    delta = jnp.sum(rounded * dprobs, axis=0, keepdims=True)
    dscores = (probs * (dprobs - delta)).astype(jnp.bfloat16)
    turned = keys.astype(jnp.float32).T.astype(jnp.bfloat16)
    out = jnp.dot(turned, dscores, preferred_element_type=jnp.float32) * (1.0 / math.sqrt(HD))
    for head in range(GROUP):
        lanes = slice(head * HD, (head + 1) * HD)
        out_ref[:, lanes] = out[:, lanes].T.astype(jnp.bfloat16)


def grad_hidden_kernel(slot_ref, dval_ref, up_ref, *refs):
    out_ref = refs[-1]
    rank = out_ref.shape[0]
    out = lax.dot_general(
        up_ref[0],
        dval_ref[...],
        (((1,), (1,)), ((), ())),
        preferred_element_type=jnp.float32,
    )
    out_ref[...] = (adapter_scale * out).astype(jnp.bfloat16)


def x_copies(x_ref, near, rows):
    me = lax.axis_index("dp")
    chip = (me >> 1) & 3
    span = rows.shape[2] // 2
    pairs = []
    for side in range(2):
        part = 4 * ((me >> 3) ^ side) + chip
        pairs.append((x_ref.at[:, columns(part, span)], rows.at[0, :, pl.ds(side * span, span)]))
    for k, ref in enumerate(near):
        pairs.append((ref, rows.at[k + 1]))
    return pairs


def hidden_kernel(store_ref, x_ref, *refs):
    near, downs, outs, (rows, down, sems) = refs[:3], refs[3:7], refs[7:11], refs[11:]
    me, group = lax.axis_index("dp"), lax.axis_index("groups")
    core = me & 1
    span, half = downs[0].shape[2], downs[0].shape[1]
    block = x_ref.shape[0] // 2
    pairs = x_copies(x_ref, near, rows)
    for slot in range(CHIPS):
        for k in range(2):
            store = store_ref[slot, k]
            for kind, ref in enumerate(downs):
                ranks = pl.ds(pl.multiple_of((group ^ (kind & 1)) * half, 16), half)
                lanes = columns(core ^ (kind >> 1), span)
                pairs.append((ref.at[store], down.at[2 * slot + k, ranks, lanes]))
    for copy in run_copies(pairs, sems):
        copy.wait()
    for slot in range(CHIPS):
        for k in range(2):
            out = lax.dot_general(
                down[2 * slot + k],
                rows[slot, pl.ds(k * block, block), :],
                (((1,), (1,)), ((), ())),
                preferred_element_type=jnp.float32,
            )
            outs[slot][:, pl.ds(k * block, block)] = out.astype(jnp.bfloat16)


def grad_down_kernel(store_ref, x_ref, grad_ref, *refs):
    near, (keep_ref, send_ref, rows, total, sems) = refs[:3], refs[5:]
    me = lax.axis_index("dp")
    core = me & 1
    span = keep_ref.shape[2]
    block = x_ref.shape[0] // 2
    copies = run_copies(x_copies(x_ref, near, rows), sems)
    total[...] = jnp.zeros_like(total)
    for copy in copies:
        copy.wait()
    for slot in range(CHIPS):
        for k in range(2):
            store = store_ref[slot, k]
            total[store] += jnp.dot(
                grad_ref[slot, :, pl.ds(k * block, block)],
                rows[slot, pl.ds(k * block, block), :],
                preferred_element_type=jnp.float32,
            )
    keep_ref[...] = total[:, :, columns(core, span)].astype(jnp.bfloat16)
    send_ref[...] = total[:, :, columns(1 - core, span)].astype(jnp.bfloat16)


def sum_kernel(one_ref, two_ref, out_ref):
    out = one_ref[0].astype(jnp.float32) + two_ref[0].astype(jnp.float32)
    out_ref[0] = out.astype(jnp.bfloat16)


def values_kernel(slot_ref, up_slot_ref, base_ref, dval_ref, up_ref, *refs):
    hidden_refs, (val_ref, keep_ref, send_ref) = refs[:CHIPS], refs[CHIPS:]
    rank = keep_ref.shape[1]
    block = base_ref.shape[0] // 2
    hidden = hidden_refs[0][...].astype(jnp.float32)
    for ref in hidden_refs[1:]:
        hidden = hidden + ref[...].astype(jnp.float32)
    hidden = hidden.astype(jnp.bfloat16)
    keep_ref[...] = jnp.zeros_like(keep_ref)
    send_ref[...] = jnp.zeros_like(send_ref)
    terms = []
    for k in range(2):
        rows = pl.ds(k * block, block)
        part = hidden[:, k * block : (k + 1) * block]
        added = lax.dot_general(
            part,
            up_ref[up_slot_ref[k]],
            (((0,), (0,)), ((), ())),
            preferred_element_type=jnp.float32,
        )
        val_ref[rows, :] = (base_ref[rows, :].astype(jnp.float32) + adapter_scale * added).astype(
            jnp.bfloat16
        )
        terms.append(
            adapter_scale * jnp.dot(part, dval_ref[rows, :], preferred_element_type=jnp.float32)
        )
    same = (slot_ref[0] == slot_ref[1]).astype(jnp.float32)
    terms[1] = terms[1] + same * terms[0]
    for k in range(2):
        for side, ref in enumerate((keep_ref, send_ref)):

            @pl.when((slot_ref[k] & 1) == side)
            def _():
                ref[slot_ref[k] >> 1] = terms[k].astype(ref.dtype)


def halve_kernel(kept_ref, came_ref, *outs):
    for k in range(kept_ref.shape[0]):
        ref = outs[k % len(outs)]
        ref[k // len(outs)] = (kept_ref[k] + came_ref[k].astype(jnp.float32)).astype(ref.dtype)


def grad_input_kernel(store_ref, grad_ref, *refs):
    downs, (out_ref, down, wide, turned, sems) = refs[:4], refs[4:]
    me, group = lax.axis_index("dp"), lax.axis_index("groups")
    core = me & 1
    block = grad_ref.shape[2] // 2
    feats, span = out_ref.shape[0], down.shape[2]
    half = down.shape[1] // 2
    window = wide.shape[0]

    def places(kind):
        ranks = pl.ds(pl.multiple_of((group ^ kind) * half, 16), half)
        return down.at[:, ranks, :]

    for side in range(2):

        @pl.when(core == side)
        def _():
            for kind in range(2):
                src = downs[2 * side + kind]
                pltpu.make_async_copy(src, places(kind), sems.at[kind]).start()

    for kind in range(2):
        pltpu.make_async_copy(downs[kind], places(kind), sems.at[kind]).wait()
    lanes = pl.ds(pl.multiple_of(core * (span - window), 128), window)
    skip = pl.ds(pl.multiple_of(core * (window - feats), 16), feats)
    for store in range(SPAN):
        wide[...] = down[store, :, lanes].astype(jnp.float32).T
        turned[store] = wide[skip, :].astype(jnp.bfloat16)
    for mask in range(SPAN):
        for k in range(2):
            out = jnp.dot(
                turned[store_ref[mask, k]],
                grad_ref[mask, :, pl.ds(k * block, block)],
                preferred_element_type=jnp.float32,
            )
            at = pl.multiple_of(((mask ^ me) * 2 + k) * block, 128)
            out_ref[:, pl.ds(at, block)] = out.astype(jnp.bfloat16)


def together(*values):
    return lax.optimization_barrier(values)


def swap(value, mask):
    return lax.ppermute(value, "dp", [(i, i ^ mask) for i in range(SPAN)])


def spread(value, masks, done=()):
    for mask in masks:
        axis = sum(other > mask for other in done)
        value = jnp.stack([value, swap(value, mask)], axis=axis)
        done = done + (mask,)
    return value


def local_clustered(
    x_rows,
    query_rows,
    key_rows,
    values_base,
    grad_out,
    adapt_down,
    adapt_up,
    block_tenant,
    owner_map,
    seq_ids,
):
    tok_rows, width = x_rows.shape
    value_width = key_rows.shape[1]
    query_width = query_rows.shape[1]
    rank = adapt_down.shape[1]
    blocks, block = seq_ids.shape
    heads = value_width // HD
    span = width // (2 * CHIPS)
    group_width = GROUP * HD
    bf16, f32 = jnp.bfloat16, jnp.float32
    any_spec = pl.BlockSpec(memory_space=pltpu.HBM)
    smem_spec = pl.BlockSpec(memory_space=pltpu.SMEM)
    vmem_spec = pl.BlockSpec(memory_space=pltpu.VMEM)
    shape = jax.ShapeDtypeStruct
    params = pltpu.CompilerParams(vmem_limit_bytes=32 * 1024 * 1024)
    big = pltpu.CompilerParams(vmem_limit_bytes=60 * 1024 * 1024)
    wide_spec = pl.BlockSpec((block, group_width), lambda b, h: (b, h))
    head_spec = pl.BlockSpec((block, HD), lambda b, h: (b, h))

    down_pack, *x_packs = pl.pallas_call(
        pack_kernel,
        in_specs=[any_spec] * 2,
        out_specs=[any_spec] * CHIPS,
        out_shape=[shape((SPAN, rank // 2, span), bf16)]
        + [shape((tok_rows, 2 * span), bf16)] * (CHIPS - 1),
        scratch_shapes=[
            pltpu.VMEM((CHIPS - 1, tok_rows, 2 * span), bf16),
            pltpu.VMEM((rank // 2, width), bf16),
            pltpu.SemaphoreType.DMA((SPAN + 3 * CHIPS,)),
        ],
        compiler_params=big,
        cost_estimate=cost(2.5),
        name="pack",
    )(x_rows, adapt_down)

    slots, slot_rows = pl.pallas_call(
        store_kernel,
        in_specs=[smem_spec] * 2,
        out_specs=[smem_spec, vmem_spec],
        out_shape=[shape((blocks,), jnp.int32), shape((16, value_width), bf16)],
        scratch_shapes=[pltpu.VMEM((16, value_width), f32)],
        compiler_params=params,
        name="store_rows",
    )(block_tenant, owner_map)

    dvalues = pl.pallas_call(
        first_kernel,
        grid=(blocks, heads),
        in_specs=[vmem_spec, wide_spec, head_spec, wide_spec],
        out_specs=head_spec,
        out_shape=shape((tok_rows, value_width), bf16),
        compiler_params=params,
        cost_estimate=cost(7),
        name="first_pass",
    )(seq_ids, query_rows, key_rows, grad_out)

    up_pair = jnp.concatenate(
        [jnp.concatenate([value, swap(value, 8)]) for value in (adapt_up[0], slot_rows)]
    )
    x_packs[0], x_packs[1], x_packs[2], up_pair = together(*x_packs, up_pair)
    near_up = jnp.stack([up_pair] + [swap(up_pair, 2 * k) for k in range(1, CHIPS)])
    down_pack, near_up = together(down_pack, near_up)
    near = [swap(x_packs[k], 2 * (k + 1)) for k in range(CHIPS - 1)]
    down_own = lax.all_to_all(down_pack, "dp", split_axis=0, concat_axis=0, tiled=True)
    all_up = jnp.stack([near_up, swap(near_up, 1)])
    stores = all_up[:, :, 2 * rank :].reshape(2, CHIPS, 2, 16, 2, -1)[:, :, :, 0, :, 0]
    stores = stores.astype(jnp.int32)
    near_stores = stores[0, :, 0]
    stores = stores.transpose(2, 1, 0, 3).reshape(SPAN, blocks)
    all_up = all_up[:, :, : 2 * rank].reshape((SPAN,) + adapt_up.shape[1:])
    down_other = lax.ppermute(down_own, "groups", [(0, 1), (1, 0)])
    me = lax.axis_index("dp")
    slots = slots ^ me
    up_slots = 8 * (slots & 1) + 2 * ((slots >> 1) & 3) + (slots >> 3)

    hidden_gradient = pl.pallas_call(
        grad_hidden_kernel,
        grid_spec=pltpu.PrefetchScalarGridSpec(
            num_scalar_prefetch=1,
            grid=(blocks,),
            in_specs=[
                pl.BlockSpec((block, value_width), lambda b, slot: (b, 0)),
                pl.BlockSpec((1, rank, value_width), lambda b, slot: (slot[b], 0, 0)),
                any_spec,
                any_spec,
            ],
            out_specs=pl.BlockSpec((rank, block), lambda b, slot: (0, b)),
        ),
        out_shape=shape((rank, tok_rows), bf16),
        compiler_params=params,
        cost_estimate=cost(1),
        name="grad_hidden",
    )(up_slots, dvalues, all_up, *near[:2])
    far_gradient = swap(hidden_gradient, 8)
    near_grad, far_grad = [
        jnp.stack([grad] + [swap(grad, 2 * k) for k in range(1, CHIPS)])
        for grad in (hidden_gradient, far_gradient)
    ]
    all_grad = jnp.stack([near_grad, far_grad])
    all_grad = jnp.stack([all_grad, swap(all_grad, 1)], axis=2)
    all_grad = all_grad.reshape((SPAN,) + hidden_gradient.shape)

    downs = [down_own, down_other, swap(down_own, 1), swap(down_other, 1)]

    down_keep, down_send = pl.pallas_call(
        grad_down_kernel,
        in_specs=[smem_spec, any_spec, vmem_spec] + [any_spec] * (CHIPS + 1),
        out_specs=[vmem_spec] * 2,
        out_shape=[shape((SPAN, rank, span), bf16)] * 2,
        scratch_shapes=[
            pltpu.VMEM((CHIPS, tok_rows, 2 * span), bf16),
            pltpu.VMEM((SPAN, rank, 2 * span), f32),
            pltpu.SemaphoreType.DMA((CHIPS + 1,)),
        ],
        compiler_params=params,
        cost_estimate=cost(3),
        name="grad_down",
    )(near_stores, x_rows, near_grad, *near, down_other, downs[2])
    hidden_parts = pl.pallas_call(
        hidden_kernel,
        in_specs=[smem_spec] + [any_spec] * (CHIPS + 4),
        out_specs=[vmem_spec] * CHIPS,
        out_shape=[shape((rank, tok_rows), bf16)] * CHIPS,
        scratch_shapes=[
            pltpu.VMEM((CHIPS, tok_rows, 2 * span), bf16),
            pltpu.VMEM((2 * CHIPS, rank, 2 * span), bf16),
            pltpu.SemaphoreType.DMA((9 * CHIPS + 1,)),
        ],
        compiler_params=params,
        cost_estimate=cost(3),
        name="hidden",
    )(near_stores, x_rows, *near, *downs)
    own_part = hidden_parts[0]
    hidden_parts = [own_part] + [swap(hidden_parts[k], 2 * k) for k in range(1, CHIPS)]

    down_parts = (down_keep.astype(f32) + swap(down_send, 1).astype(f32)).astype(bf16)
    down_parts = lax.all_to_all(down_parts, "dp", split_axis=0, concat_axis=0, tiled=True)

    value_rows, kept, sent = pl.pallas_call(
        values_kernel,
        in_specs=[smem_spec] * 2 + [vmem_spec] * (3 + CHIPS),
        out_specs=[vmem_spec] * 3,
        out_shape=[
            shape((tok_rows, value_width), bf16),
            shape((SPAN // 2, rank, value_width), f32),
            shape((SPAN // 2, rank, value_width), bf16),
        ],
        compiler_params=params,
        cost_estimate=cost(1),
        name="values",
    )(slots, up_slots, values_base, dvalues, all_up, *hidden_parts)

    grad_query = pl.pallas_call(
        second_kernel,
        grid=(blocks, heads),
        in_specs=[vmem_spec, wide_spec, head_spec, head_spec, wide_spec],
        out_specs=wide_spec,
        out_shape=shape((tok_rows, query_width), bf16),
        compiler_params=params,
        cost_estimate=cost(9),
        name="second_pass",
    )(seq_ids, query_rows, key_rows, value_rows, grad_out)

    feats = width // SPAN
    window = -(-feats // 128) * 128
    grad_input_t = pl.pallas_call(
        grad_input_kernel,
        in_specs=[smem_spec, vmem_spec] + [any_spec] * 4,
        out_specs=vmem_spec,
        out_shape=shape((feats, SPAN * tok_rows), bf16),
        scratch_shapes=[
            pltpu.VMEM((SPAN, rank, span), bf16),
            pltpu.VMEM((window, rank), f32),
            pltpu.VMEM((SPAN, feats, rank), bf16),
            pltpu.SemaphoreType.DMA((2,)),
        ],
        compiler_params=params,
        cost_estimate=cost(7),
        name="grad_input",
    )(stores, all_grad, *downs)

    for mask in (1, 2, 4, 8):
        if mask == 4:
            sent, grad_query = together(sent, grad_query)
        if mask == 8:
            sent, down_parts, grad_input_t = together(sent, down_parts, grad_input_t)
        came = swap(sent, mask)
        count = max(came.shape[0] // 2, 1)
        outs = [shape((count,) + came.shape[1:], bf16)]
        if mask < 8:
            outs = [shape(outs[0].shape, f32)] + outs
        halves = pl.pallas_call(
            halve_kernel,
            in_specs=[vmem_spec] * 2,
            out_specs=[vmem_spec] * len(outs),
            out_shape=outs,
            compiler_params=params,
            cost_estimate=cost(1),
            name="halve",
        )(kept, came)
        kept, sent = halves[0], halves[-1]
    grad_up = sent

    grad_down = pl.pallas_call(
        sum_kernel,
        grid=(2 * CHIPS,),
        in_specs=[
            pl.BlockSpec((1, rank, span), lambda p: (p // CHIPS * 8 + p % CHIPS * 2, 0, 0)),
            pl.BlockSpec((1, rank, span), lambda p: (8 - p // CHIPS * 8 + p % CHIPS * 2 + 1, 0, 0)),
        ],
        out_specs=pl.BlockSpec((1, rank, span), lambda p: (0, 0, p)),
        out_shape=shape((1, rank, width), bf16),
        compiler_params=params,
        cost_estimate=cost(2),
        name="sum_down",
    )(down_parts, down_parts)
    return (grad_query, grad_input_t, grad_down, grad_up)


def solution(mesh):
    clustered = mesh.shape["dp"] == SPAN and mesh.shape["groups"] == 2
    in_specs = (
        P(("groups", "dp"), None),
        P(("groups", "dp"), None),
        P(("groups", "dp"), None),
        P(("groups", "dp"), None),
        P(("groups", "dp"), None),
        P("dp", None, None),
        P("dp", None, None),
        P(("groups", "dp")),
        P(),
        P(("groups", "dp"), None),
    )
    out_specs = (
        P(("groups", "dp"), None),
        P("dp", "groups"),
        P(("groups", "dp"), None, None),
        P(("groups", "dp"), None, None),
    )
    return jax.shard_map(
        local_clustered if clustered else local, mesh=mesh, in_specs=in_specs, out_specs=out_specs, check_vma=False
    )
```

profile of v0, /device:TPU:0, one launch (start us, length us, event | category | flops | bytes accessed | tf_op | source)
XLA Modules:
  0.0 151.1 jit_solution(11339079548860645901)
XLA Ops:
  0.6 4.1 %collective-permute-start = (bf16[64,512]{1,0:T(8,128)(2,1)}, bf16[64,512]{1,0:T(8,128)(2,1)S(1)}, u32[]{:S(2)}, u32[]{:S(2)}) collective-permute-start(bf16[64,512]{1,0:T(8,128)(2,1)} %bitcast.47), channel_id=1, source_target_pairs={{0,8},{1,9},{2,10},{3,11},{4,12},{5,13},{6,14},{7,15},{8,0},{9,1},... | collective-permute-start | bytes 196616 | tf_op jit(solution)/shard_map/ppermute | solution.py:425
  4.7 0.7 copy-done.13
  5.4 0.7 copy-done.14
  6.0 1.1 store_rows.1
  7.3 2.8 %pack.1 = (bf16[16,32,640]{2,1,0:T(8,128)(2,1)}, bf16[256,1280]{1,0:T(8,128)(2,1)}, bf16[256,1280]{1,0:T(8,128)(2,1)}, bf16[256,1280]{1,0:T(8,128)(2,1)}) custom-call(bf16[256,5120]{1,0:T(8,128)(2,1)} %x_ref.5, bf16[1,64,5120]{2,1,0:T(8,128)(2,1)} %down_ref.1), custom_call_target="tpu_custom_call" | custom-call | bytes 82500 | tf_op jit(solution)/shard_map/pack/pallas_call | solution.py:466
  10.1 1.8 %collective-permute-done.1 = bf16[16,512]{1,0:T(8,128)(2,1)S(1)} collective-permute-done((bf16[16,512]{1,0:T(8,128)(2,1)S(1)}, bf16[16,512]{1,0:T(8,128)(2,1)S(1)}, u32[]{:S(2)}, u32[]{:S(2)}) %collective-permute-start.1) | collective-permute-done | bytes 16416 | tf_op jit(solution)/shard_map/ppermute | solution.py:425
  11.9 2.6 %collective-permute-start.4 = (bf16[160,512]{1,0:T(8,128)(2,1)S(1)}, bf16[160,512]{1,0:T(8,128)(2,1)S(1)}, u32[]{:S(2)}, u32[]{:S(2)}) collective-permute-start(bf16[160,512]{1,0:T(8,128)(2,1)S(1)} %pad_maximum_fusion.4), channel_id=1, source_target_pairs={{0,6},{1,7},{2,4},{3,5},{4,2},{5,3},{6,0},{7,1},{8,14},{9,15},{10,... | collective-permute-start | bytes 491528 | tf_op jit(solution)/shard_map/ppermute | solution.py:425
  14.5 0.4 collective-permute-start.3
  15.0 0.5 collective-permute-start.2
  15.5 3.7 %collective-permute-done.4 = bf16[160,512]{1,0:T(8,128)(2,1)S(1)} collective-permute-done((bf16[160,512]{1,0:T(8,128)(2,1)S(1)}, bf16[160,512]{1,0:T(8,128)(2,1)S(1)}, u32[]{:S(2)}, u32[]{:S(2)}) %collective-permute-start.4) | collective-permute-done | bytes 163872 | tf_op jit(solution)/shard_map/ppermute | solution.py:425
  19.2 1.7 %collective-permute-done.3 = bf16[160,512]{1,0:T(8,128)(2,1)S(1)} collective-permute-done((bf16[160,512]{1,0:T(8,128)(2,1)S(1)}, bf16[160,512]{1,0:T(8,128)(2,1)S(1)}, u32[]{:S(2)}, u32[]{:S(2)}) %collective-permute-start.3) | collective-permute-done | bytes 163872 | tf_op jit(solution)/shard_map/ppermute | solution.py:425
  21.0 0.9 pad_maximum_fusion
  21.9 5.4 %all-to-all-start = ((bf16[16,32,640]{2,1,0:T(8,128)(2,1)}), bf16[16,32,640]{2,1,0:T(8,128)(2,1)S(1)}, u32[]{:S(2)}, u32[]{:S(2)}) async-start(bf16[16,32,640]{2,1,0:T(8,128)(2,1)} %get-tuple-element.47), calls=%async_computation | async-start | bytes 1310720 | tf_op jit(solution)/shard_map/all_to_all | solution.py:510
  27.3 0.4 collective-permute-start.5
  27.7 1.7 %collective-permute-start.6 = (bf16[256,1280]{1,0:T(8,128)(2,1)}, bf16[256,1280]{1,0:T(8,128)(2,1)}, u32[]{:S(2)}, u32[]{:S(2)}) collective-permute-start(bf16[256,1280]{1,0:T(8,128)(2,1)} %get-tuple-element.44), channel_id=1, source_target_pairs={{0,2},{1,3},{2,0},{3,1},{4,6},{5,7},{6,4},{7,5},{8,10},{9,11},{10,... | collective-permute-start | bytes 1966088 | tf_op jit(solution)/shard_map/ppermute | solution.py:425
  29.4 1.5 collective-permute-start.7
  30.9 1.6 %copy-done.5 = bf16[256,4096]{1,0:T(8,128)(2,1)S(1)} copy-done((bf16[256,4096]{1,0:T(8,128)(2,1)S(1)}, bf16[256,4096]{1,0:T(8,128)(2,1)}, u32[]{:S(2)}) %copy-start.5) | copy-done | bytes 2097176
  32.5 4.7 %first_pass.1.dval_ref = bf16[256,512]{1,0:T(8,128)(2,1)S(1)} custom-call(s32[2,128]{1,0:T(2,128)S(1)} %copy-done.12, bf16[256,4096]{1,0:T(8,128)(2,1)S(1)} %copy-done.3, bf16[256,512]{1,0:T(8,128)(2,1)S(1)} %copy-done.9, bf16[256,4096]{1,0:T(8,128)(2,1)S(1)} %copy-done.5), custom_call_target="tpu_custom_call" | custom-call | bytes 231000 | tf_op jit(solution)/shard_map/first_pass/pallas_call | solution.py:492
  37.2 0.4 collective-permute-start.8
  37.6 1.1 fusion
  38.7 12.9 %collective-permute-done.6.refs_0_ = bf16[256,1280]{1,0:T(8,128)(2,1)} collective-permute-done((bf16[256,1280]{1,0:T(8,128)(2,1)}, bf16[256,1280]{1,0:T(8,128)(2,1)}, u32[]{:S(2)}, u32[]{:S(2)}) %collective-permute-start.6) | collective-permute-done | bytes 655392 | tf_op jit(solution)/shard_map/ppermute | solution.py:425
  51.6 4.0 %collective-permute-done.7.refs_1_ = bf16[256,1280]{1,0:T(8,128)(2,1)} collective-permute-done((bf16[256,1280]{1,0:T(8,128)(2,1)}, bf16[256,1280]{1,0:T(8,128)(2,1)}, u32[]{:S(2)}, u32[]{:S(2)}) %collective-permute-start.7) | collective-permute-done | bytes 655392 | tf_op jit(solution)/shard_map/ppermute | solution.py:425
  55.6 1.5 %grad_hidden.1 = bf16[64,256]{1,0:T(8,128)(2,1)} custom-call(s32[2]{0:T(128)S(1)} %get-tuple-element.68.up_slot_ref.slot_ref, bf16[256,512]{1,0:T(8,128)(2,1)S(1)} %first_pass.1.dval_ref, bf16[16,64,512]{2,1,0:T(8,128)(2,1)S(1)} %bitcast.36, bf16[256,1280]{1,0:T(8,128)(2,1)} %collective-permute-done.6.refs_0_, bf16[256,1280]{1,0:T(8,128)(2,1)} %collective-permute-done.7.refs_1_), custom_call_target="tpu_custom_call" | custom-call | bytes 33000 | tf_op jit(solution)/shard_map/grad_hidden/pallas_call | solution.py:522
  57.1 1.5 collective-permute-start.20
  58.6 1.4 collective-permute-start.19
  60.0 1.5 collective-permute-start.9
  61.5 1.7 %pad_maximum_fusion.2 = bf16[2,4,32,512]{3,2,1,0:T(8,128)(2,1)} fusion(bf16[1,4,160,512]{3,2,1,0:T(8,128)(2,1)} %bitcast.6, bf16[1,4,160,512]{3,2,1,0:T(8,128)(2,1)} %bitcast.40), kind=kLoop, calls=%fused_computation.6 | loop fusion | flops 524288 | bytes 1572864 | tf_op jit(solution)/shard_map/stack | solution.py:511
  63.2 1.7 %reshape.23 = bf16[2,4,2,16,2,256]{5,4,3,2,1,0:T(2,128)(2,1)} reshape(bf16[2,4,32,512]{3,2,1,0:T(8,128)(2,1)} %pad_maximum_fusion.2) | data formatting | bytes 524288 | tf_op jit(solution)/shard_map/reshape | solution.py:512
  64.9 1.3 slice.18
  66.2 0.8 copy.28
  67.1 0.6 fusion.1
  67.7 3.4 %collective-permute-done.20 = bf16[64,256]{1,0:T(8,128)(2,1)} collective-permute-done((bf16[64,256]{1,0:T(8,128)(2,1)}, bf16[64,256]{1,0:T(8,128)(2,1)}, u32[]{:S(2)}, u32[]{:S(2)}) %collective-permute-start.20) | collective-permute-done | bytes 32800 | tf_op jit(solution)/shard_map/ppermute | solution.py:425
  71.1 0.6 collective-permute-start.18
  71.7 0.6 slice_bitcast_fusion
  72.2 0.8 copy.21.store_ref
  73.0 2.3 %collective-permute-done.18 = bf16[64,256]{1,0:T(8,128)(2,1)} collective-permute-done((bf16[64,256]{1,0:T(8,128)(2,1)}, bf16[64,256]{1,0:T(8,128)(2,1)}, u32[]{:S(2)}, u32[]{:S(2)}) %collective-permute-start.18) | collective-permute-done | bytes 32800 | tf_op jit(solution)/shard_map/ppermute | solution.py:425
  75.3 1.5 fusion.3
  76.9 3.0 %grad_down.1 = (bf16[16,64,640]{2,1,0:T(8,128)(2,1)S(1)}, bf16[16,64,640]{2,1,0:T(8,128)(2,1)S(1)}) custom-call(s32[4,2]{1,0:T(4,128)S(1)} %copy.21.store_ref, bf16[256,5120]{1,0:T(8,128)(2,1)S(1)} %copy-done, bf16[4,64,256]{2,1,0:T(8,128)(2,1)S(1)} %get-tuple-element.73.grad_ref, bf16[256,1280]{1,0:T(8,128)(2,1)} %collective-permute-done.6.refs_0_, ...), custom_call_target="tpu_custom_call" | custom-call | bytes 99000 | tf_op jit(solution)/shard_map/grad_down/pallas_call | solution.py:551
  79.9 3.0 %collective-permute-done.21 = bf16[16,64,640]{2,1,0:T(8,128)(2,1)S(1)} collective-permute-done((bf16[16,64,640]{2,1,0:T(8,128)(2,1)S(1)}, bf16[16,64,640]{2,1,0:T(8,128)(2,1)S(1)}, u32[]{:S(2)}, u32[]{:S(2)}) %collective-permute-start.21) | collective-permute-done | bytes 1310752 | tf_op jit(solution)/shard_map/ppermute | solution.py:425
  83.0 1.5 add_convert_fusion
  84.4 4.4 %all-to-all-start.1 = ((bf16[16,64,640]{2,1,0:T(8,128)(2,1)}), bf16[16,64,640]{2,1,0:T(8,128)(2,1)}, u32[]{:S(2)}, u32[]{:S(2)}) async-start(bf16[16,64,640]{2,1,0:T(8,128)(2,1)} %add_convert_fusion), calls=%async_computation.1 | async-start | bytes 2621440 | tf_op jit(solution)/shard_map/all_to_all | solution.py:583
  89.1 2.1 %collective-permute-done.11.refs_6_.refs_3_ = bf16[16,32,640]{2,1,0:T(8,128)(2,1)S(1)} collective-permute-done((bf16[16,32,640]{2,1,0:T(8,128)(2,1)}, bf16[16,32,640]{2,1,0:T(8,128)(2,1)S(1)}, u32[]{:S(2)}, u32[]{:S(2)}) %collective-permute-start.11) | collective-permute-done | bytes 655392 | tf_op jit(solution)/shard_map/ppermute | solution.py:425
  91.2 3.6 %hidden.1 = (bf16[64,256]{1,0:T(8,128)(2,1)S(1)}, bf16[64,256]{1,0:T(8,128)(2,1)S(1)}, bf16[64,256]{1,0:T(8,128)(2,1)S(1)}, bf16[64,256]{1,0:T(8,128)(2,1)S(1)}) custom-call(s32[4,2]{1,0:T(4,128)S(1)} %copy.21.store_ref, bf16[256,5120]{1,0:T(8,128)(2,1)S(1)} %copy-done, bf16[256,1280]{1,0:T(8,128)(2,1)} %collective-permute-done.6.refs_0_, ...), custom_call_target="tpu_custom_call" | custom-call | bytes 99000 | tf_op jit(solution)/shard_map/hidden/pallas_call | solution.py:565
  94.8 1.8 %collective-permute-start.12 = (bf16[64,256]{1,0:T(8,128)(2,1)S(1)}, bf16[64,256]{1,0:T(8,128)(2,1)S(1)}, u32[]{:S(2)}, u32[]{:S(2)}) collective-permute-start(bf16[64,256]{1,0:T(8,128)(2,1)S(1)} %get-tuple-element.49), channel_id=1, source_target_pairs={{0,2},{1,3},{2,0},{3,1},{4,6},{5,7},{6,4},{7,5},{8,10},{9,11},{10,... | collective-permute-start | bytes 98312 | tf_op jit(solution)/shard_map/ppermute | solution.py:425
  96.6 1.5 collective-permute-start.13
  98.4 0.7 collective-permute-done.12.refs_1_
  99.1 12.8 %collective-permute-done.13.refs_2_ = bf16[64,256]{1,0:T(8,128)(2,1)S(1)} collective-permute-done((bf16[64,256]{1,0:T(8,128)(2,1)S(1)}, bf16[64,256]{1,0:T(8,128)(2,1)S(1)}, u32[]{:S(2)}, u32[]{:S(2)}) %collective-permute-start.13) | collective-permute-done | bytes 32800 | tf_op jit(solution)/shard_map/ppermute | solution.py:425
  111.9 0.4 collective-permute-done.14.refs_3_
  112.3 0.9 values.1
  113.3 5.5 %collective-permute-start.22 = (bf16[64,256]{1,0:T(8,128)(2,1)}, bf16[64,256]{1,0:T(8,128)(2,1)S(1)}, u32[]{:S(2)}, u32[]{:S(2)}) collective-permute-start(bf16[64,256]{1,0:T(8,128)(2,1)} %grad_hidden.1), channel_id=1, source_target_pairs={{0,8},{1,9},{2,10},{3,11},{4,12},{5,13},{6,14},{7,15},{8,0},{9,1},... | collective-permute-start | bytes 98312 | tf_op jit(solution)/shard_map/ppermute | solution.py:425
  118.9 3.4 %collective-permute-done.22 = bf16[64,256]{1,0:T(8,128)(2,1)S(1)} collective-permute-done((bf16[64,256]{1,0:T(8,128)(2,1)}, bf16[64,256]{1,0:T(8,128)(2,1)S(1)}, u32[]{:S(2)}, u32[]{:S(2)}) %collective-permute-start.22) | collective-permute-done | bytes 32800 | tf_op jit(solution)/shard_map/ppermute | solution.py:425
  122.3 3.0 %collective-permute-start.24 = (bf16[64,256]{1,0:T(8,128)(2,1)S(1)}, bf16[64,256]{1,0:T(8,128)(2,1)S(1)}, u32[]{:S(2)}, u32[]{:S(2)}) collective-permute-start(bf16[64,256]{1,0:T(8,128)(2,1)S(1)} %collective-permute-done.22), channel_id=1, source_target_pairs={{0,4},{1,5},{2,6},{3,7},{4,0},{5,1},{6,2},{7,3},{8,12},{9,13},{10,... | collective-permute-start | bytes 98312 | tf_op jit(solution)/shard_map/ppermute | solution.py:425
  125.3 0.5 collective-permute-start.23
  125.8 1.4 collective-permute-done.25
  127.2 0.3 collective-permute-done.24
  127.5 1.7 %collective-permute-done.23 = bf16[64,256]{1,0:T(8,128)(2,1)S(1)} collective-permute-done((bf16[64,256]{1,0:T(8,128)(2,1)S(1)}, bf16[64,256]{1,0:T(8,128)(2,1)S(1)}, u32[]{:S(2)}, u32[]{:S(2)}) %collective-permute-start.23) | collective-permute-done | bytes 32800 | tf_op jit(solution)/shard_map/ppermute | solution.py:425
  129.3 0.6 collective-permute-start.16
  130.0 0.8 copy-done.4
  130.8 6.9 %second_pass.1 = bf16[256,4096]{1,0:T(8,128)(2,1)} custom-call(s32[2,128]{1,0:T(2,128)S(1)} %copy-done.12, bf16[256,4096]{1,0:T(8,128)(2,1)S(1)} %copy-done.4, bf16[256,512]{1,0:T(8,128)(2,1)S(1)} %copy-done.10, bf16[256,512]{1,0:T(8,128)(2,1)S(1)} %get-tuple-element.57.value_ref, bf16[256,4096]{1,0:T(8,128)(2,1)S(1)} %copy-done.6), custom_call_target="tpu_custom_call" | custom-call | bytes 297000 | tf_op jit(solution)/shard_map/second_pass/pallas_call | solution.py:599
  138.0 0.7 copy-done.8
  138.8 5.4 %grad_input.1 = bf16[320,4096]{1,0:T(8,128)(2,1)} custom-call(s32[16,2]{1,0:T(8,128)S(1)} %bitcast.39, bf16[16,64,256]{2,1,0:T(8,128)(2,1)S(1)} %bitcast.38, bf16[16,32,640]{2,1,0:T(8,128)(2,1)S(1)} %all-to-all-done.refs_3_.refs_0_, bf16[16,32,640]{2,1,0:T(8,128)(2,1)} %collective-permute-done.9.refs_4_.refs_3_.refs_1_, ...), custom_call_target="tpu_custom_call" | custom-call | bytes 231000 | tf_op jit(solution)/shard_map/grad_input/pallas_call | solution.py:612
  144.3 1.0 collective-permute-start.27
  145.2 5.2 %sum_down.1 = bf16[1,64,5120]{2,1,0:T(8,128)(2,1)} custom-call(bf16[16,64,640]{2,1,0:T(8,128)(2,1)} %all-to-all-done.1.one_ref.two_ref, bf16[16,64,640]{2,1,0:T(8,128)(2,1)} %all-to-all-done.1.one_ref.two_ref), custom_call_target="tpu_custom_call" | custom-call | bytes 66000 | tf_op jit(solution)/shard_map/sum_down/pallas_call | solution.py:650
  150.5 0.6 halve.7
  (66 shorter events, 1.4 us)
Async XLA Ops:
  0.6 11.3 %collective-permute-start = (bf16[64,512]{1,0:T(8,128)(2,1)}, bf16[64,512]{1,0:T(8,128)(2,1)S(1)}, u32[]{:S(2)}, u32[]{:S(2)}) collective-permute-start(bf16[64,512]{1,0:T(8,128)(2,1)} %bitcast.47), channel_id=1, source_target_pairs={{0,8},{1,9},{2,10},{3,11},{4,12},{5,13},{6,14},{7,15},{8,0},{9,1},... | collective-permute-start | bytes 196616 | tf_op jit(solution)/shard_map/ppermute | solution.py:425
  4.7 0.7 copy-start.13
  5.4 0.7 copy-start.14
  7.2 4.7 %copy-start.17 = (bf16[1,64,512]{2,1,0:T(8,128)(2,1)S(1)}, bf16[1,64,512]{2,1,0:T(8,128)(2,1)}, u32[]{:S(2)}) copy-start(bf16[1,64,512]{2,1,0:T(8,128)(2,1)} %param.16) | copy-start | bytes 196612
  7.2 4.7 %collective-permute-start.1 = (bf16[16,512]{1,0:T(8,128)(2,1)S(1)}, bf16[16,512]{1,0:T(8,128)(2,1)S(1)}, u32[]{:S(2)}, u32[]{:S(2)}) collective-permute-start(bf16[16,512]{1,0:T(8,128)(2,1)S(1)} %get-tuple-element.41), channel_id=1, source_target_pairs={{0,8},{1,9},{2,10},{3,11},{4,12},{5,13},{6,14},{7,15},{8,0},{9,1},... | collective-permute-start | bytes 49160 | tf_op jit(solution)/shard_map/ppermute | solution.py:425
  11.9 7.3 %collective-permute-start.4 = (bf16[160,512]{1,0:T(8,128)(2,1)S(1)}, bf16[160,512]{1,0:T(8,128)(2,1)S(1)}, u32[]{:S(2)}, u32[]{:S(2)}) collective-permute-start(bf16[160,512]{1,0:T(8,128)(2,1)S(1)} %pad_maximum_fusion.4), channel_id=1, source_target_pairs={{0,6},{1,7},{2,4},{3,5},{4,2},{5,3},{6,0},{7,1},{8,14},{9,15},{10,... | collective-permute-start | bytes 491528 | tf_op jit(solution)/shard_map/ppermute | solution.py:425
  14.5 6.4 %collective-permute-start.3 = (bf16[160,512]{1,0:T(8,128)(2,1)S(1)}, bf16[160,512]{1,0:T(8,128)(2,1)S(1)}, u32[]{:S(2)}, u32[]{:S(2)}) collective-permute-start(bf16[160,512]{1,0:T(8,128)(2,1)S(1)} %pad_maximum_fusion.4), channel_id=1, source_target_pairs={{0,4},{1,5},{2,6},{3,7},{4,0},{5,1},{6,2},{7,3},{8,12},{9,13},{10,... | collective-permute-start | bytes 491528 | tf_op jit(solution)/shard_map/ppermute | solution.py:425
  15.0 6.0 %collective-permute-start.2 = (bf16[160,512]{1,0:T(8,128)(2,1)S(1)}, bf16[160,512]{1,0:T(8,128)(2,1)S(1)}, u32[]{:S(2)}, u32[]{:S(2)}) collective-permute-start(bf16[160,512]{1,0:T(8,128)(2,1)S(1)} %pad_maximum_fusion.4), channel_id=1, source_target_pairs={{0,2},{1,3},{2,0},{3,1},{4,6},{5,7},{6,4},{7,5},{8,10},{9,11},{10,... | collective-permute-start | bytes 491528 | tf_op jit(solution)/shard_map/ppermute | solution.py:425
  21.0 9.9 %copy-start.3 = (bf16[256,4096]{1,0:T(8,128)(2,1)S(1)}, bf16[256,4096]{1,0:T(8,128)(2,1)}, u32[]{:S(2)}) copy-start(bf16[256,4096]{1,0:T(8,128)(2,1)} %query_ref.3) | copy-start | bytes 6291460
  21.0 9.9 %copy-start.9 = (bf16[256,512]{1,0:T(8,128)(2,1)S(1)}, bf16[256,512]{1,0:T(8,128)(2,1)}, u32[]{:S(2)}) copy-start(bf16[256,512]{1,0:T(8,128)(2,1)} %key_ref.3) | copy-start | bytes 786436
  21.0 9.9 %copy-start.12 = (s32[2,128]{1,0:T(2,128)S(1)}, s32[2,128]{1,0:T(2,128)}, u32[]{:S(2)}) copy-start(s32[2,128]{1,0:T(2,128)} %ids_ref.3) | copy-start | bytes 3076
  21.9 38.1 %all-to-all-start = ((bf16[16,32,640]{2,1,0:T(8,128)(2,1)}), bf16[16,32,640]{2,1,0:T(8,128)(2,1)S(1)}, u32[]{:S(2)}, u32[]{:S(2)}) async-start(bf16[16,32,640]{2,1,0:T(8,128)(2,1)} %get-tuple-element.47), calls=%async_computation | async-start | bytes 1310720 | tf_op jit(solution)/shard_map/all_to_all | solution.py:510
  27.3 10.3 %collective-permute-start.5 = (bf16[4,160,512]{2,1,0:T(8,128)(2,1)}, bf16[4,160,512]{2,1,0:T(8,128)(2,1)}, u32[]{:S(2)}, u32[]{:S(2)}) collective-permute-start(bf16[4,160,512]{2,1,0:T(8,128)(2,1)} %pad_maximum_fusion), channel_id=1, source_target_pairs={{0,1},{1,0},{2,3},{3,2},{4,5},{5,4},{6,7},{7,6},{8,9},{9,8},{10,11... | collective-permute-start | bytes 1966088 | tf_op jit(solution)/shard_map/ppermute | solution.py:425
  27.7 23.9 %collective-permute-start.6 = (bf16[256,1280]{1,0:T(8,128)(2,1)}, bf16[256,1280]{1,0:T(8,128)(2,1)}, u32[]{:S(2)}, u32[]{:S(2)}) collective-permute-start(bf16[256,1280]{1,0:T(8,128)(2,1)} %get-tuple-element.44), channel_id=1, source_target_pairs={{0,2},{1,3},{2,0},{3,1},{4,6},{5,7},{6,4},{7,5},{8,10},{9,11},{10,... | collective-permute-start | bytes 1966088 | tf_op jit(solution)/shard_map/ppermute | solution.py:425
  29.4 26.2 %collective-permute-start.7 = (bf16[256,1280]{1,0:T(8,128)(2,1)}, bf16[256,1280]{1,0:T(8,128)(2,1)}, u32[]{:S(2)}, u32[]{:S(2)}) collective-permute-start(bf16[256,1280]{1,0:T(8,128)(2,1)} %get-tuple-element.45), channel_id=1, source_target_pairs={{0,4},{1,5},{2,6},{3,7},{4,0},{5,1},{6,2},{7,3},{8,12},{9,13},{10,... | collective-permute-start | bytes 1966088 | tf_op jit(solution)/shard_map/ppermute | solution.py:425
  30.9 1.6 %copy-start.5 = (bf16[256,4096]{1,0:T(8,128)(2,1)S(1)}, bf16[256,4096]{1,0:T(8,128)(2,1)}, u32[]{:S(2)}) copy-start(bf16[256,4096]{1,0:T(8,128)(2,1)} %grad_ref.3) | copy-start | bytes 6291460
  32.5 5.1 %copy-start.15 = (bf16[4,160,512]{2,1,0:T(8,128)(2,1)S(1)}, bf16[4,160,512]{2,1,0:T(8,128)(2,1)}, u32[]{:S(2)}) copy-start(bf16[4,160,512]{2,1,0:T(8,128)(2,1)} %pad_maximum_fusion) | copy-start | bytes 1966084
  37.2 39.7 %collective-permute-start.8 = (bf16[256,1280]{1,0:T(8,128)(2,1)}, bf16[256,1280]{1,0:T(8,128)(2,1)}, u32[]{:S(2)}, u32[]{:S(2)}) collective-permute-start(bf16[256,1280]{1,0:T(8,128)(2,1)} %get-tuple-element.46), channel_id=1, source_target_pairs={{0,6},{1,7},{2,4},{3,5},{4,2},{5,3},{6,0},{7,1},{8,14},{9,15},{10,... | collective-permute-start | bytes 1966088 | tf_op jit(solution)/shard_map/ppermute | solution.py:425
  38.7 18.4 %copy-start.1 = (bf16[2,4,128,512]{3,2,1,0:T(8,128)(2,1)}, bf16[2,4,128,512]{3,2,1,0:T(8,128)(2,1)S(1)}, u32[]{:S(2)}) copy-start(bf16[2,4,128,512]{3,2,1,0:T(8,128)(2,1)S(1)} %fusion) | copy-start | bytes 3145732
  55.6 21.3 %copy-start = (bf16[256,5120]{1,0:T(8,128)(2,1)S(1)}, bf16[256,5120]{1,0:T(8,128)(2,1)}, u32[]{:S(2)}) copy-start(bf16[256,5120]{1,0:T(8,128)(2,1)} %x_ref.5) | copy-start | bytes 7864324
  57.1 14.0 %collective-permute-start.20 = (bf16[64,256]{1,0:T(8,128)(2,1)}, bf16[64,256]{1,0:T(8,128)(2,1)}, u32[]{:S(2)}, u32[]{:S(2)}) collective-permute-start(bf16[64,256]{1,0:T(8,128)(2,1)} %grad_hidden.1), channel_id=1, source_target_pairs={{0,6},{1,7},{2,4},{3,5},{4,2},{5,3},{6,0},{7,1},{8,14},{9,15},{10,... | collective-permute-start | bytes 98312 | tf_op jit(solution)/shard_map/ppermute | solution.py:425
  58.6 14.4 %collective-permute-start.19 = (bf16[64,256]{1,0:T(8,128)(2,1)}, bf16[64,256]{1,0:T(8,128)(2,1)}, u32[]{:S(2)}, u32[]{:S(2)}) collective-permute-start(bf16[64,256]{1,0:T(8,128)(2,1)} %grad_hidden.1), channel_id=1, source_target_pairs={{0,4},{1,5},{2,6},{3,7},{4,0},{5,1},{6,2},{7,3},{8,12},{9,13},{10,... | collective-permute-start | bytes 98312 | tf_op jit(solution)/shard_map/ppermute | solution.py:425
  60.0 16.8 %collective-permute-start.9 = (bf16[16,32,640]{2,1,0:T(8,128)(2,1)S(1)}, bf16[16,32,640]{2,1,0:T(8,128)(2,1)}, u32[]{:S(2)}, u32[]{:S(2)}) collective-permute-start(bf16[16,32,640]{2,1,0:T(8,128)(2,1)S(1)} %all-to-all-done.refs_3_.refs_0_), channel_id=1, source_target_pairs={{0,16},{16,0},{1,17},{17,1},{2,18},{18,2},{3,19},{19,3},{4,20},{20... | collective-permute-start | bytes 1966088 | tf_op jit(solution)/shard_map/ppermute | solution.py:517
  61.5 15.3 %collective-permute-start.10 = (bf16[16,32,640]{2,1,0:T(8,128)(2,1)S(1)}, bf16[16,32,640]{2,1,0:T(8,128)(2,1)}, u32[]{:S(2)}, u32[]{:S(2)}) collective-permute-start(bf16[16,32,640]{2,1,0:T(8,128)(2,1)S(1)} %all-to-all-done.refs_3_.refs_0_), channel_id=1, source_target_pairs={{0,1},{1,0},{2,3},{3,2},{4,5},{5,4},{6,7},{7,6},{8,9},{9,8},{10,11... | collective-permute-start | bytes 1966088 | tf_op jit(solution)/shard_map/ppermute | solution.py:425
  71.1 4.2 %collective-permute-start.18 = (bf16[64,256]{1,0:T(8,128)(2,1)}, bf16[64,256]{1,0:T(8,128)(2,1)}, u32[]{:S(2)}, u32[]{:S(2)}) collective-permute-start(bf16[64,256]{1,0:T(8,128)(2,1)} %grad_hidden.1), channel_id=1, source_target_pairs={{0,2},{1,3},{2,0},{3,1},{4,6},{5,7},{6,4},{7,5},{8,10},{9,11},{10,... | collective-permute-start | bytes 98312 | tf_op jit(solution)/shard_map/ppermute | solution.py:425
  79.9 3.1 %collective-permute-start.21 = (bf16[16,64,640]{2,1,0:T(8,128)(2,1)S(1)}, bf16[16,64,640]{2,1,0:T(8,128)(2,1)S(1)}, u32[]{:S(2)}, u32[]{:S(2)}) collective-permute-start(bf16[16,64,640]{2,1,0:T(8,128)(2,1)S(1)} %get-tuple-element.63), channel_id=1, source_target_pairs={{0,1},{1,0},{2,3},{3,2},{4,5},{5,4},{6,7},{7,6},{8,9},{9,8},{10,11... | collective-permute-start | bytes 3932168 | tf_op jit(solution)/shard_map/ppermute | solution.py:425
  84.4 59.8 %all-to-all-start.1 = ((bf16[16,64,640]{2,1,0:T(8,128)(2,1)}), bf16[16,64,640]{2,1,0:T(8,128)(2,1)}, u32[]{:S(2)}, u32[]{:S(2)}) async-start(bf16[16,64,640]{2,1,0:T(8,128)(2,1)} %add_convert_fusion), calls=%async_computation.1 | async-start | bytes 2621440 | tf_op jit(solution)/shard_map/all_to_all | solution.py:583
  88.8 23.5 %copy-start.2 = (bf16[2,4,128,512]{3,2,1,0:T(8,128)(2,1)S(1)}, bf16[2,4,128,512]{3,2,1,0:T(8,128)(2,1)}, u32[]{:S(2)}) copy-start(bf16[2,4,128,512]{3,2,1,0:T(8,128)(2,1)} %copy-done.1) | copy-start | bytes 3145732
  88.8 23.5 %copy-start.11 = (bf16[256,512]{1,0:T(8,128)(2,1)S(1)}, bf16[256,512]{1,0:T(8,128)(2,1)}, u32[]{:S(2)}) copy-start(bf16[256,512]{1,0:T(8,128)(2,1)} %base_ref.1) | copy-start | bytes 786436
  88.8 2.4 %collective-permute-start.11 = (bf16[16,32,640]{2,1,0:T(8,128)(2,1)}, bf16[16,32,640]{2,1,0:T(8,128)(2,1)S(1)}, u32[]{:S(2)}, u32[]{:S(2)}) collective-permute-start(bf16[16,32,640]{2,1,0:T(8,128)(2,1)} %collective-permute-done.9.refs_4_.refs_3_.refs_1_), channel_id=1, source_target_pairs={{0,1},{1,0},{2,3},{3,2},{4,5},{5,4},{6,7},{7,6},{8,9},{9,8},{10,11... | collective-permute-start | bytes 1966088 | tf_op jit(solution)/shard_map/ppermute | solution.py:425
  91.2 3.6 %copy-start.7 = (bf16[16,32,640]{2,1,0:T(8,128)(2,1)}, bf16[16,32,640]{2,1,0:T(8,128)(2,1)S(1)}, u32[]{:S(2)}) copy-start(bf16[16,32,640]{2,1,0:T(8,128)(2,1)S(1)} %collective-permute-done.11.refs_6_.refs_3_) | copy-start | bytes 1966084
  91.2 38.8 %copy-start.10 = (bf16[256,512]{1,0:T(8,128)(2,1)S(1)}, bf16[256,512]{1,0:T(8,128)(2,1)}, u32[]{:S(2)}) copy-start(bf16[256,512]{1,0:T(8,128)(2,1)} %key_ref.3) | copy-start | bytes 786436
  94.8 4.2 %collective-permute-start.12 = (bf16[64,256]{1,0:T(8,128)(2,1)S(1)}, bf16[64,256]{1,0:T(8,128)(2,1)S(1)}, u32[]{:S(2)}, u32[]{:S(2)}) collective-permute-start(bf16[64,256]{1,0:T(8,128)(2,1)S(1)} %get-tuple-element.49), channel_id=1, source_target_pairs={{0,2},{1,3},{2,0},{3,1},{4,6},{5,7},{6,4},{7,5},{8,10},{9,11},{10,... | collective-permute-start | bytes 98312 | tf_op jit(solution)/shard_map/ppermute | solution.py:425
  96.6 15.3 %collective-permute-start.13 = (bf16[64,256]{1,0:T(8,128)(2,1)S(1)}, bf16[64,256]{1,0:T(8,128)(2,1)S(1)}, u32[]{:S(2)}, u32[]{:S(2)}) collective-permute-start(bf16[64,256]{1,0:T(8,128)(2,1)S(1)} %get-tuple-element.50), channel_id=1, source_target_pairs={{0,4},{1,5},{2,6},{3,7},{4,0},{5,1},{6,2},{7,3},{8,12},{9,13},{10,... | collective-permute-start | bytes 98312 | tf_op jit(solution)/shard_map/ppermute | solution.py:425
  98.1 14.2 %collective-permute-start.14 = (bf16[64,256]{1,0:T(8,128)(2,1)S(1)}, bf16[64,256]{1,0:T(8,128)(2,1)S(1)}, u32[]{:S(2)}, u32[]{:S(2)}) collective-permute-start(bf16[64,256]{1,0:T(8,128)(2,1)S(1)} %get-tuple-element.51), channel_id=1, source_target_pairs={{0,6},{1,7},{2,4},{3,5},{4,2},{5,3},{6,0},{7,1},{8,14},{9,15},{10,... | collective-permute-start | bytes 98312 | tf_op jit(solution)/shard_map/ppermute | solution.py:425
  112.3 17.7 %copy-start.6 = (bf16[256,4096]{1,0:T(8,128)(2,1)S(1)}, bf16[256,4096]{1,0:T(8,128)(2,1)}, u32[]{:S(2)}) copy-start(bf16[256,4096]{1,0:T(8,128)(2,1)} %grad_ref.3) | copy-start | bytes 6291460
  113.3 16.6 %copy-start.16 = (bf16[1,4,64,256]{3,2,1,0:T(8,128)(2,1)S(1)}, bf16[1,4,64,256]{3,2,1,0:T(8,128)(2,1)}, u32[]{:S(2)}) copy-start(bf16[1,4,64,256]{3,2,1,0:T(8,128)(2,1)} %get-tuple-element.72) | copy-start | bytes 393220
  113.3 16.0 %collective-permute-start.15 = (bf16[8,64,512]{2,1,0:T(8,128)(2,1)S(1)}, bf16[8,64,512]{2,1,0:T(8,128)(2,1)S(1)}, u32[]{:S(2)}, u32[]{:S(2)}) collective-permute-start(bf16[8,64,512]{2,1,0:T(8,128)(2,1)S(1)} %get-tuple-element.53), channel_id=1, source_target_pairs={{0,1},{1,0},{2,3},{3,2},{4,5},{5,4},{6,7},{7,6},{8,9},{9,8},{10,11... | collective-permute-start | bytes 1572872 | tf_op jit(solution)/shard_map/ppermute | solution.py:425
  113.3 9.0 %collective-permute-start.22 = (bf16[64,256]{1,0:T(8,128)(2,1)}, bf16[64,256]{1,0:T(8,128)(2,1)S(1)}, u32[]{:S(2)}, u32[]{:S(2)}) collective-permute-start(bf16[64,256]{1,0:T(8,128)(2,1)} %grad_hidden.1), channel_id=1, source_target_pairs={{0,8},{1,9},{2,10},{3,11},{4,12},{5,13},{6,14},{7,15},{8,0},{9,1},... | collective-permute-start | bytes 98312 | tf_op jit(solution)/shard_map/ppermute | solution.py:425
  122.3 4.9 %collective-permute-start.25 = (bf16[64,256]{1,0:T(8,128)(2,1)S(1)}, bf16[64,256]{1,0:T(8,128)(2,1)S(1)}, u32[]{:S(2)}, u32[]{:S(2)}) collective-permute-start(bf16[64,256]{1,0:T(8,128)(2,1)S(1)} %collective-permute-done.22), channel_id=1, source_target_pairs={{0,6},{1,7},{2,4},{3,5},{4,2},{5,3},{6,0},{7,1},{8,14},{9,15},{10,... | collective-permute-start | bytes 98312 | tf_op jit(solution)/shard_map/ppermute | solution.py:425
  122.3 5.2 %collective-permute-start.24 = (bf16[64,256]{1,0:T(8,128)(2,1)S(1)}, bf16[64,256]{1,0:T(8,128)(2,1)S(1)}, u32[]{:S(2)}, u32[]{:S(2)}) collective-permute-start(bf16[64,256]{1,0:T(8,128)(2,1)S(1)} %collective-permute-done.22), channel_id=1, source_target_pairs={{0,4},{1,5},{2,6},{3,7},{4,0},{5,1},{6,2},{7,3},{8,12},{9,13},{10,... | collective-permute-start | bytes 98312 | tf_op jit(solution)/shard_map/ppermute | solution.py:425
  125.3 3.9 %collective-permute-start.23 = (bf16[64,256]{1,0:T(8,128)(2,1)S(1)}, bf16[64,256]{1,0:T(8,128)(2,1)S(1)}, u32[]{:S(2)}, u32[]{:S(2)}) collective-permute-start(bf16[64,256]{1,0:T(8,128)(2,1)S(1)} %collective-permute-done.22), channel_id=1, source_target_pairs={{0,2},{1,3},{2,0},{3,1},{4,6},{5,7},{6,4},{7,5},{8,10},{9,11},{10,... | collective-permute-start | bytes 98312 | tf_op jit(solution)/shard_map/ppermute | solution.py:425
  129.2 1.6 %copy-start.4 = (bf16[256,4096]{1,0:T(8,128)(2,1)S(1)}, bf16[256,4096]{1,0:T(8,128)(2,1)}, u32[]{:S(2)}) copy-start(bf16[256,4096]{1,0:T(8,128)(2,1)} %query_ref.3) | copy-start | bytes 6291460
  129.3 8.3 %collective-permute-start.16 = (bf16[4,64,512]{2,1,0:T(8,128)(2,1)S(1)}, bf16[4,64,512]{2,1,0:T(8,128)(2,1)S(1)}, u32[]{:S(2)}, u32[]{:S(2)}) collective-permute-start(bf16[4,64,512]{2,1,0:T(8,128)(2,1)S(1)} %get-tuple-element.55), channel_id=1, source_target_pairs={{0,2},{1,3},{2,0},{3,1},{4,6},{5,7},{6,4},{7,5},{8,10},{9,11},{10,... | collective-permute-start | bytes 786440 | tf_op jit(solution)/shard_map/ppermute | solution.py:425
  129.9 8.0 %collective-permute-start.26 = (bf16[2,4,64,256]{3,2,1,0:T(8,128)(2,1)S(1)}, bf16[2,4,64,256]{3,2,1,0:T(8,128)(2,1)S(1)}, u32[]{:S(2)}, u32[]{:S(2)}) collective-permute-start(bf16[2,4,64,256]{3,2,1,0:T(8,128)(2,1)S(1)} %get-tuple-element.71), channel_id=1, source_target_pairs={{0,1},{1,0},{2,3},{3,2},{4,5},{5,4},{6,7},{7,6},{8,9},{9,8},{10,11... | collective-permute-start | bytes 786440 | tf_op jit(solution)/shard_map/ppermute | solution.py:425
  130.8 7.0 %copy-start.18 = (s32[2,4,2,2]{1,3,0,2:T(2,128)S(1)}, s32[2,4,2,2]{1,3,0,2:T(2,128)}, u32[]{:S(2)}) copy-start(s32[2,4,2,2]{1,3,0,2:T(2,128)} %get-tuple-element.74) | copy-start | bytes 388
  137.7 1.1 copy-start.8
  137.7 6.5 %collective-permute-start.17 = (bf16[2,64,512]{2,1,0:T(8,128)(2,1)S(1)}, bf16[2,64,512]{2,1,0:T(8,128)(2,1)S(1)}, u32[]{:S(2)}, u32[]{:S(2)}) collective-permute-start(bf16[2,64,512]{2,1,0:T(8,128)(2,1)S(1)} %get-tuple-element.60), channel_id=1, source_target_pairs={{0,4},{1,5},{2,6},{3,7},{4,0},{5,1},{6,2},{7,3},{8,12},{9,13},{10,... | collective-permute-start | bytes 393224 | tf_op jit(solution)/shard_map/ppermute | solution.py:425
  144.3 6.2 %collective-permute-start.27 = (bf16[1,64,512]{2,1,0:T(8,128)(2,1)S(1)}, bf16[1,64,512]{2,1,0:T(8,128)(2,1)S(1)}, u32[]{:S(2)}, u32[]{:S(2)}) collective-permute-start(bf16[1,64,512]{2,1,0:T(8,128)(2,1)S(1)} %get-tuple-element.67), channel_id=1, source_target_pairs={{0,8},{1,9},{2,10},{3,11},{4,12},{5,13},{6,14},{7,15},{8,0},{9,1},... | collective-permute-start | bytes 196616 | tf_op jit(solution)/shard_map/ppermute | solution.py:425
where the time goes:
time: 152 us; the launch traced here: 151 us
  waiting for transfers between devices  55.8 us (37%)
  starting transfers between devices  41.2 us (27%)
  Pallas kernels  36 us (24%)
  local copies, waits for them, and re-layouts  9.78 us (6%)
  other arithmetic  7.41 us (5%)
    ppermute x27, waiting for transfers between devices, swap(): return lax.ppermute(value, 'dp', [(i, i ^ mask) for i in range(SPAN)])  55.8 us
    ppermute x27, starting transfers between devices, swap(): return lax.ppermute(value, 'dp', [(i, i ^ mask) for i in range(SPAN)])  29.9 us
    pallas_call x1, Pallas kernels, local_clustered(): pl.pallas_call(second_kernel, grid=(blocks, heads), in_specs=[vmem_spec,...  6.88 us
    pallas_call x1, Pallas kernels, local_clustered(): pl.pallas_call(grad_input_kernel, in_specs=[smem_spec, vmem_spec] + [any_...  5.44 us
    all_to_all x1, starting transfers between devices, local_clustered(): lax.all_to_all(down_pack, 'dp', split_axis=0, concat_axis=0, tiled=True)  5.39 us
    unnamed x39, local copies, waits for them, and re-layouts  5.29 us
    pallas_call x1, Pallas kernels, local_clustered(): pl.pallas_call(sum_kernel, grid=(2 * CHIPS,), in_specs=[pl.BlockSpec((1,...  5.23 us
    pallas_call x1, Pallas kernels, local_clustered(): pl.pallas_call(first_kernel, grid=(blocks, heads), in_specs=[vmem_spec, w...  4.67 us
  transfers between devices with their start and end apart: 30, of which 16 were waited for; matrix products, arithmetic and copies ran while one was open for 7% of the time, Pallas kernels for 21%

commit v1 on v0

--- a/solution.py
+++ b/solution.py
@@ -306,11 +306,11 @@
                 (((1,), (1,)), ((), ())),
                 preferred_element_type=jnp.float32,
             )
-            outs[slot][:, pl.ds(k * block, block)] = out.astype(jnp.bfloat16)
-
-
-def grad_down_kernel(store_ref, x_ref, grad_ref, *refs):
-    near, (keep_ref, send_ref, rows, total, sems) = refs[:3], refs[5:]
+            outs[slot][:, pl.ds(k * block, block)] = out
+
+
+def grad_down_kernel(store_ref, x_ref, *refs):
+    grads, near, (keep_ref, send_ref, rows, total, sems) = refs[:4], refs[4:7], refs[8:]
     me = lax.axis_index("dp")
     core = me & 1
     span = keep_ref.shape[2]
@@ -323,7 +323,7 @@
         for k in range(2):
             store = store_ref[slot, k]
             total[store] += jnp.dot(
-                grad_ref[slot, :, pl.ds(k * block, block)],
+                grads[slot][0, :, pl.ds(k * block, block)],
                 rows[slot, pl.ds(k * block, block), :],
                 preferred_element_type=jnp.float32,
             )
@@ -331,18 +331,21 @@
     send_ref[...] = total[:, :, columns(1 - core, span)].astype(jnp.bfloat16)
 
 
-def sum_kernel(one_ref, two_ref, out_ref):
-    out = one_ref[0].astype(jnp.float32) + two_ref[0].astype(jnp.float32)
-    out_ref[0] = out.astype(jnp.bfloat16)
+def sum_kernel(part_ref, out_ref):
+    span = part_ref.shape[2]
+    for part in range(2 * CHIPS):
+        one, two = [i for i in range(SPAN) if eighth_of(i) == part]
+        out = part_ref[one].astype(jnp.float32) + part_ref[two].astype(jnp.float32)
+        out_ref[0, :, pl.ds(part * span, span)] = out.astype(jnp.bfloat16)
 
 
 def values_kernel(slot_ref, up_slot_ref, base_ref, dval_ref, up_ref, *refs):
     hidden_refs, (val_ref, keep_ref, send_ref) = refs[:CHIPS], refs[CHIPS:]
     rank = keep_ref.shape[1]
     block = base_ref.shape[0] // 2
-    hidden = hidden_refs[0][...].astype(jnp.float32)
+    hidden = hidden_refs[0][...]
     for ref in hidden_refs[1:]:
-        hidden = hidden + ref[...].astype(jnp.float32)
+        hidden = hidden + ref[...]
     hidden = hidden.astype(jnp.bfloat16)
     keep_ref[...] = jnp.zeros_like(keep_ref)
     send_ref[...] = jnp.zeros_like(send_ref)
@@ -458,7 +461,7 @@
     smem_spec = pl.BlockSpec(memory_space=pltpu.SMEM)
     vmem_spec = pl.BlockSpec(memory_space=pltpu.VMEM)
     shape = jax.ShapeDtypeStruct
-    params = pltpu.CompilerParams(vmem_limit_bytes=32 * 1024 * 1024)
+    params = pltpu.CompilerParams(vmem_limit_bytes=16 * 1024 * 1024)
     big = pltpu.CompilerParams(vmem_limit_bytes=60 * 1024 * 1024)
     wide_spec = pl.BlockSpec((block, group_width), lambda b, h: (b, h))
     head_spec = pl.BlockSpec((block, HD), lambda b, h: (b, h))
@@ -500,21 +503,20 @@
         name="first_pass",
     )(seq_ids, query_rows, key_rows, grad_out)
 
-    up_pair = jnp.concatenate(
-        [jnp.concatenate([value, swap(value, 8)]) for value in (adapt_up[0], slot_rows)]
-    )
-    x_packs[0], x_packs[1], x_packs[2], up_pair = together(*x_packs, up_pair)
+    up_pair = jnp.concatenate([adapt_up[0], swap(adapt_up[0], 8), slot_rows])
+    x_packs[0], x_packs[1], x_packs[2], down_pack, up_pair = together(*x_packs, down_pack, up_pair)
     near_up = jnp.stack([up_pair] + [swap(up_pair, 2 * k) for k in range(1, CHIPS)])
-    down_pack, near_up = together(down_pack, near_up)
     near = [swap(x_packs[k], 2 * (k + 1)) for k in range(CHIPS - 1)]
     down_own = lax.all_to_all(down_pack, "dp", split_axis=0, concat_axis=0, tiled=True)
+    near[0], near[1], down_own, near_up, dvalues = together(
+        near[0], near[1], down_own, near_up, dvalues
+    )
+    down_other = lax.ppermute(down_own, "groups", [(0, 1), (1, 0)])
+    near_stores = near_up[:, 2 * rank].reshape(CHIPS, 2, -1)[:, :, 0].astype(jnp.int32)
     all_up = jnp.stack([near_up, swap(near_up, 1)])
-    stores = all_up[:, :, 2 * rank :].reshape(2, CHIPS, 2, 16, 2, -1)[:, :, :, 0, :, 0]
-    stores = stores.astype(jnp.int32)
-    near_stores = stores[0, :, 0]
-    stores = stores.transpose(2, 1, 0, 3).reshape(SPAN, blocks)
+    stores = jnp.stack([near_stores, swap(near_stores, 1)], axis=1).reshape(2 * CHIPS, blocks)
+    stores = jnp.concatenate([stores, swap(stores, 8)])
     all_up = all_up[:, :, : 2 * rank].reshape((SPAN,) + adapt_up.shape[1:])
-    down_other = lax.ppermute(down_own, "groups", [(0, 1), (1, 0)])
     me = lax.axis_index("dp")
     slots = slots ^ me
     up_slots = 8 * (slots & 1) + 2 * ((slots >> 1) & 3) + (slots >> 3)
@@ -527,8 +529,6 @@
             in_specs=[
                 pl.BlockSpec((block, value_width), lambda b, slot: (b, 0)),
                 pl.BlockSpec((1, rank, value_width), lambda b, slot: (slot[b], 0, 0)),
-                any_spec,
-                any_spec,
             ],
             out_specs=pl.BlockSpec((rank, block), lambda b, slot: (0, b)),
         ),
@@ -536,21 +536,36 @@
         compiler_params=params,
         cost_estimate=cost(1),
         name="grad_hidden",
-    )(up_slots, dvalues, all_up, *near[:2])
+    )(up_slots, dvalues, all_up)
     far_gradient = swap(hidden_gradient, 8)
-    near_grad, far_grad = [
-        jnp.stack([grad] + [swap(grad, 2 * k) for k in range(1, CHIPS)])
-        for grad in (hidden_gradient, far_gradient)
-    ]
-    all_grad = jnp.stack([near_grad, far_grad])
-    all_grad = jnp.stack([all_grad, swap(all_grad, 1)], axis=2)
-    all_grad = all_grad.reshape((SPAN,) + hidden_gradient.shape)
+    hidden_gradient, far_gradient, near[2], near_stores, stores, down_other = together(
+        hidden_gradient, far_gradient, near[2], near_stores, stores, down_other
+    )
+    both = jnp.stack([hidden_gradient, far_gradient])
+    near_grad = [both] + [swap(both, 2 * k) for k in range(1, CHIPS)]
 
     downs = [down_own, down_other, swap(down_own, 1), swap(down_other, 1)]
+
+    hidden_parts = pl.pallas_call(
+        hidden_kernel,
+        in_specs=[smem_spec] + [any_spec] * (CHIPS + 4),
+        out_specs=[vmem_spec] * CHIPS,
+        out_shape=[shape((rank, tok_rows), f32)] * CHIPS,
+        scratch_shapes=[
+            pltpu.VMEM((CHIPS, tok_rows, 2 * span), bf16),
+            pltpu.VMEM((2 * CHIPS, rank, 2 * span), bf16),
+            pltpu.SemaphoreType.DMA((9 * CHIPS + 1,)),
+        ],
+        compiler_params=params,
+        cost_estimate=cost(3),
+        name="hidden",
+    )(near_stores, x_rows, *near, *downs)
+    own_part = hidden_parts[0]
+    hidden_parts = [own_part] + [swap(hidden_parts[k], 2 * k) for k in range(1, CHIPS)]
 
     down_keep, down_send = pl.pallas_call(
         grad_down_kernel,
-        in_specs=[smem_spec, any_spec, vmem_spec] + [any_spec] * (CHIPS + 1),
+        in_specs=[smem_spec, any_spec] + [vmem_spec] * CHIPS + [any_spec] * CHIPS,
         out_specs=[vmem_spec] * 2,
         out_shape=[shape((SPAN, rank, span), bf16)] * 2,
         scratch_shapes=[
@@ -561,27 +576,7 @@
         compiler_params=params,
         cost_estimate=cost(3),
         name="grad_down",
-    )(near_stores, x_rows, near_grad, *near, down_other, downs[2])
-    hidden_parts = pl.pallas_call(
-        hidden_kernel,
-        in_specs=[smem_spec] + [any_spec] * (CHIPS + 4),
-        out_specs=[vmem_spec] * CHIPS,
-        out_shape=[shape((rank, tok_rows), bf16)] * CHIPS,
-        scratch_shapes=[
-            pltpu.VMEM((CHIPS, tok_rows, 2 * span), bf16),
-            pltpu.VMEM((2 * CHIPS, rank, 2 * span), bf16),
-            pltpu.SemaphoreType.DMA((9 * CHIPS + 1,)),
-        ],
-        compiler_params=params,
-        cost_estimate=cost(3),
-        name="hidden",
-    )(near_stores, x_rows, *near, *downs)
-    own_part = hidden_parts[0]
-    hidden_parts = [own_part] + [swap(hidden_parts[k], 2 * k) for k in range(1, CHIPS)]
-
-    down_parts = (down_keep.astype(f32) + swap(down_send, 1).astype(f32)).astype(bf16)
-    down_parts = lax.all_to_all(down_parts, "dp", split_axis=0, concat_axis=0, tiled=True)
-
+    )(near_stores, x_rows, *near_grad, *near, own_part)
     value_rows, kept, sent = pl.pallas_call(
         values_kernel,
         in_specs=[smem_spec] * 2 + [vmem_spec] * (3 + CHIPS),
@@ -595,6 +590,14 @@
         cost_estimate=cost(1),
         name="values",
     )(slots, up_slots, values_base, dvalues, all_up, *hidden_parts)
+
+    down_parts = (down_keep.astype(f32) + swap(down_send, 1).astype(f32)).astype(bf16)
+    down_parts, value_rows, kept, sent = together(down_parts, value_rows, kept, sent)
+    all_grad = jnp.stack(near_grad, axis=1)
+    all_grad = jnp.stack([all_grad, swap(all_grad, 1)], axis=2)
+    all_grad = all_grad.reshape((SPAN,) + hidden_gradient.shape)
+    down_parts = lax.all_to_all(down_parts, "dp", split_axis=0, concat_axis=0, tiled=True)
+
 
     grad_query = pl.pallas_call(
         second_kernel,
@@ -649,17 +652,13 @@
 
     grad_down = pl.pallas_call(
         sum_kernel,
-        grid=(2 * CHIPS,),
-        in_specs=[
-            pl.BlockSpec((1, rank, span), lambda p: (p // CHIPS * 8 + p % CHIPS * 2, 0, 0)),
-            pl.BlockSpec((1, rank, span), lambda p: (8 - p // CHIPS * 8 + p % CHIPS * 2 + 1, 0, 0)),
-        ],
-        out_specs=pl.BlockSpec((1, rank, span), lambda p: (0, 0, p)),
+        in_specs=[vmem_spec],
+        out_specs=vmem_spec,
         out_shape=shape((1, rank, width), bf16),
         compiler_params=params,
         cost_estimate=cost(2),
         name="sum_down",
-    )(down_parts, down_parts)
+    )(down_parts)
     return (grad_query, grad_input_t, grad_down, grad_up)
 
 

time: 152 us -> 139 us (0.914)
  waiting for transfers between devices: 55.8 us -> 41.5 us
  Pallas kernels: 36 us -> 33.2 us
  other arithmetic: 7.41 us -> 9.94 us
    ppermute x27 -> x25, waiting for transfers between devices: 55.8 us -> 40.5 us  [swap(): return lax.ppermute(value, 'dp', [(i, i ^ mask) for i in range(SPAN)])]
    another operation x2, other arithmetic: 0.09 us -> 2.68 us  [local_clustered(): all_grad = jnp.stack([all_grad, swap(all_grad, 1)], axis=2)]
    pallas_call x2, Pallas kernels: 8.24 us -> 5.79 us  [the longest x1 3.49 us: local_clustered(): pl.pallas_call(grad_down_kernel, in_specs=[smem_spec, any_spec] + [vmem_s...]
    another operation x2 -> x1, other arithmetic: 2.83 us -> 1.27 us  [local_clustered(): all_up = jnp.stack([near_up, swap(near_up, 1)])]
    unnamed x39 -> x41, local copies, waits for them, and re-layouts: 5.29 us -> 6.22 us
    ppermute x27 -> x25, starting transfers between devices: 29.9 us -> 30.3 us  [swap(): return lax.ppermute(value, 'dp', [(i, i ^ mask) for i in range(SPAN)])]
  transfers between devices with their start and end apart: 30 -> 28, of which waited for: 16 -> 15; matrix products, arithmetic and copies ran while one was open for 7% -> 10% of each run, Pallas kernels for 21% -> 21%
where the time goes in v1:
time: 139 us; the launch traced here: 138 us
  starting transfers between devices  41.9 us (30%)
  waiting for transfers between devices  41.5 us (30%)
  Pallas kernels  33.2 us (24%)
  local copies, waits for them, and re-layouts  10.6 us (8%)
  other arithmetic  9.94 us (7%)
    ppermute x25, waiting for transfers between devices, swap(): return lax.ppermute(value, 'dp', [(i, i ^ mask) for i in range(SPAN)])  40.5 us
    ppermute x25, starting transfers between devices, swap(): return lax.ppermute(value, 'dp', [(i, i ^ mask) for i in range(SPAN)])  30.3 us
    pallas_call x1, Pallas kernels, local_clustered(): pl.pallas_call(second_kernel, grid=(blocks, heads), in_specs=[vmem_spec,...  6.9 us
    unnamed x41, local copies, waits for them, and re-layouts  6.22 us
    all_to_all x1, starting transfers between devices, local_clustered(): lax.all_to_all(down_pack, 'dp', split_axis=0, concat_axis=0, tiled=True)  5.61 us
    pallas_call x1, Pallas kernels, local_clustered(): pl.pallas_call(grad_input_kernel, in_specs=[smem_spec, vmem_spec] + [any_...  5.44 us
    pallas_call x1, Pallas kernels, local_clustered(): pl.pallas_call(first_kernel, grid=(blocks, heads), in_specs=[vmem_spec, w...  4.67 us
    all_to_all x1, starting transfers between devices, local_clustered(): lax.all_to_all(down_parts, 'dp', split_axis=0, concat_axis=0, tiled=True)  4.53 us
  transfers between devices with their start and end apart: 28, of which 15 were waited for; matrix products, arithmetic and copies ran while one was open for 10% of the time, Pallas kernels for 21%

profile of v1, /device:TPU:0, one launch (start us, length us, event | category | flops | bytes accessed | tf_op | source)
XLA Modules:
  0.0 138.1 jit_solution(8897211442297796224)
XLA Ops:
  0.7 4.1 %collective-permute-start = (bf16[64,512]{1,0:T(8,128)(2,1)}, bf16[64,512]{1,0:T(8,128)(2,1)S(1)}, u32[]{:S(2)}, u32[]{:S(2)}) collective-permute-start(bf16[64,512]{1,0:T(8,128)(2,1)} %bitcast.32), channel_id=1, source_target_pairs={{0,8},{1,9},{2,10},{3,11},{4,12},{5,13},{6,14},{7,15},{8,0},{9,1},... | collective-permute-start | bytes 196616 | tf_op jit(solution)/shard_map/ppermute | solution.py:428
  4.8 2.8 %pack.1 = (bf16[16,32,640]{2,1,0:T(8,128)(2,1)}, bf16[256,1280]{1,0:T(8,128)(2,1)}, bf16[256,1280]{1,0:T(8,128)(2,1)}, bf16[256,1280]{1,0:T(8,128)(2,1)}) custom-call(bf16[256,5120]{1,0:T(8,128)(2,1)} %x_ref.5, bf16[1,64,5120]{2,1,0:T(8,128)(2,1)} %down_ref.1), custom_call_target="tpu_custom_call" | custom-call | bytes 82500 | tf_op jit(solution)/shard_map/pack/pallas_call | solution.py:469
  7.6 1.1 store_rows.1
  8.8 5.6 %all-to-all-start = ((bf16[16,32,640]{2,1,0:T(8,128)(2,1)}), bf16[16,32,640]{2,1,0:T(8,128)(2,1)S(1)}, u32[]{:S(2)}, u32[]{:S(2)}) async-start(bf16[16,32,640]{2,1,0:T(8,128)(2,1)} %get-tuple-element.58), calls=%async_computation | async-start | bytes 1310720 | tf_op jit(solution)/shard_map/all_to_all | solution.py:510
  14.4 1.9 %collective-permute-start.1 = (bf16[256,1280]{1,0:T(8,128)(2,1)}, bf16[256,1280]{1,0:T(8,128)(2,1)}, u32[]{:S(2)}, u32[]{:S(2)}) collective-permute-start(bf16[256,1280]{1,0:T(8,128)(2,1)} %get-tuple-element.56), channel_id=1, source_target_pairs={{0,2},{1,3},{2,0},{3,1},{4,6},{5,7},{6,4},{7,5},{8,10},{9,11},{10,... | collective-permute-start | bytes 1966088 | tf_op jit(solution)/shard_map/ppermute | solution.py:428
  16.3 1.5 %collective-permute-start.2 = (bf16[256,1280]{1,0:T(8,128)(2,1)}, bf16[256,1280]{1,0:T(8,128)(2,1)}, u32[]{:S(2)}, u32[]{:S(2)}) collective-permute-start(bf16[256,1280]{1,0:T(8,128)(2,1)} %get-tuple-element.57), channel_id=1, source_target_pairs={{0,4},{1,5},{2,6},{3,7},{4,0},{5,1},{6,2},{7,3},{8,12},{9,13},{10,... | collective-permute-start | bytes 1966088 | tf_op jit(solution)/shard_map/ppermute | solution.py:428
  17.8 0.6 collective-permute-start.3
  18.5 2.8 %collective-permute-start.5 = (bf16[144,512]{1,0:T(8,128)(2,1)S(1)}, bf16[144,512]{1,0:T(8,128)(2,1)}, u32[]{:S(2)}, u32[]{:S(2)}) collective-permute-start(bf16[144,512]{1,0:T(8,128)(2,1)S(1)} %pad_maximum_fusion.4), channel_id=1, source_target_pairs={{0,6},{1,7},{2,4},{3,5},{4,2},{5,3},{6,0},{7,1},{8,14},{9,15},{10,... | collective-permute-start | bytes 442376 | tf_op jit(solution)/shard_map/ppermute | solution.py:428
  21.3 1.6 %copy-done.5 = bf16[256,4096]{1,0:T(8,128)(2,1)S(1)} copy-done((bf16[256,4096]{1,0:T(8,128)(2,1)S(1)}, bf16[256,4096]{1,0:T(8,128)(2,1)}, u32[]{:S(2)}) %copy-start.5) | copy-done | bytes 2097176
  22.9 4.7 %first_pass.1.dval_ref = bf16[256,512]{1,0:T(8,128)(2,1)S(1)} custom-call(s32[2,128]{1,0:T(2,128)S(1)} %copy-done.12, bf16[256,4096]{1,0:T(8,128)(2,1)S(1)} %copy-done.3, bf16[256,512]{1,0:T(8,128)(2,1)S(1)} %copy-done.7, bf16[256,4096]{1,0:T(8,128)(2,1)S(1)} %copy-done.5), custom_call_target="tpu_custom_call" | custom-call | bytes 231000 | tf_op jit(solution)/shard_map/first_pass/pallas_call | solution.py:495
  27.6 14.3 %collective-permute-done.3 = bf16[144,512]{1,0:T(8,128)(2,1)} collective-permute-done((bf16[144,512]{1,0:T(8,128)(2,1)S(1)}, bf16[144,512]{1,0:T(8,128)(2,1)}, u32[]{:S(2)}, u32[]{:S(2)}) %collective-permute-start.3) | collective-permute-done | bytes 147488 | tf_op jit(solution)/shard_map/ppermute | solution.py:428
  41.9 4.0 %collective-permute-done.4 = bf16[144,512]{1,0:T(8,128)(2,1)} collective-permute-done((bf16[144,512]{1,0:T(8,128)(2,1)S(1)}, bf16[144,512]{1,0:T(8,128)(2,1)}, u32[]{:S(2)}, u32[]{:S(2)}) %collective-permute-start.4) | collective-permute-done | bytes 147488 | tf_op jit(solution)/shard_map/ppermute | solution.py:428
  45.9 3.6 %collective-permute-done.5 = bf16[144,512]{1,0:T(8,128)(2,1)} collective-permute-done((bf16[144,512]{1,0:T(8,128)(2,1)S(1)}, bf16[144,512]{1,0:T(8,128)(2,1)}, u32[]{:S(2)}, u32[]{:S(2)}) %collective-permute-start.5) | collective-permute-done | bytes 147488 | tf_op jit(solution)/shard_map/ppermute | solution.py:428
  49.4 1.9 %pad_maximum_fusion.1 = bf16[4,144,512]{2,1,0:T(8,128)(2,1)} fusion(bf16[1,144,512]{2,1,0:T(8,128)(2,1)} %bitcast.4, bf16[1,144,512]{2,1,0:T(8,128)(2,1)} %bitcast.3, bf16[1,144,512]{2,1,0:T(8,128)(2,1)} %bitcast.2, bf16[1,144,512]{2,1,0:T(8,128)(2,1)S(1)} %bitcast.31), kind=kLoop, calls=%fused_computation.2 | loop fusion | flops 884736 | bytes 1179648 | tf_op jit(solution)/shard_map/stack | solution.py:508
  51.5 0.5 collective-permute-start.8
  52.0 1.5 %collective-permute-start.11 = (bf16[16,32,640]{2,1,0:T(8,128)(2,1)S(1)}, bf16[16,32,640]{2,1,0:T(8,128)(2,1)}, u32[]{:S(2)}, u32[]{:S(2)}) collective-permute-start(bf16[16,32,640]{2,1,0:T(8,128)(2,1)S(1)} %all-to-all-done.refs_3_.refs_0_), channel_id=1, source_target_pairs={{0,16},{16,0},{1,17},{17,1},{2,18},{18,2},{3,19},{19,3},{4,20},{20... | collective-permute-start | bytes 1966088 | tf_op jit(solution)/shard_map/ppermute | solution.py:514
  53.5 0.8 slice_reduce_fusion
  54.3 0.6 reshape_squeeze.3
  54.9 0.7 slice.12
  55.6 0.6 copy.42
  56.2 0.7 convert_bitcast_fusion
  56.9 0.5 collective-permute-start.9
  57.4 0.8 collective-permute-done.9
  58.2 0.6 pad_add_fusion
  58.8 0.8 copy.37
  59.6 0.6 reshape.32
  60.2 2.5 %collective-permute-start.10 = (s32[8,2]{0,1:T(2,128)}, s32[8,2]{0,1:T(2,128)S(1)}, u32[]{:S(2)}, u32[]{:S(2)}) collective-permute-start(s32[8,2]{0,1:T(2,128)} %reshape.32), channel_id=1, source_target_pairs={{0,8},{1,9},{2,10},{3,11},{4,12},{5,13},{6,14},{7,15},{8,0},{9,1},... | collective-permute-start | bytes 200 | tf_op jit(solution)/shard_map/ppermute | solution.py:428
  62.7 1.3 pad_maximum_fusion
  64.0 0.9 grad_hidden.1
  64.9 1.0 copy-done.1
  66.3 0.9 collective-permute-done.10
  67.3 0.6 pad_add_fusion.1
  67.9 2.0 %collective-permute-done.8.refs_2_.refs_6_ = bf16[256,1280]{1,0:T(8,128)(2,1)} collective-permute-done((bf16[256,1280]{1,0:T(8,128)(2,1)}, bf16[256,1280]{1,0:T(8,128)(2,1)}, u32[]{:S(2)}, u32[]{:S(2)}) %collective-permute-start.8) | collective-permute-done | bytes 655392 | tf_op jit(solution)/shard_map/ppermute | solution.py:428
  69.9 1.0 collective-permute-done.7
  70.9 0.7 fusion
  71.5 1.5 %collective-permute-start.12 = (bf16[2,64,256]{2,1,0:T(8,128)(2,1)}, bf16[2,64,256]{2,1,0:T(8,128)(2,1)}, u32[]{:S(2)}, u32[]{:S(2)}) collective-permute-start(bf16[2,64,256]{2,1,0:T(8,128)(2,1)} %get-tuple-element.101.refs_0_), channel_id=1, source_target_pairs={{0,2},{1,3},{2,0},{3,1},{4,6},{5,7},{6,4},{7,5},{8,10},{9,11},{10,... | collective-permute-start | bytes 196616 | tf_op jit(solution)/shard_map/ppermute | solution.py:428
  73.0 1.6 %collective-permute-start.13 = (bf16[2,64,256]{2,1,0:T(8,128)(2,1)}, bf16[2,64,256]{2,1,0:T(8,128)(2,1)}, u32[]{:S(2)}, u32[]{:S(2)}) collective-permute-start(bf16[2,64,256]{2,1,0:T(8,128)(2,1)} %get-tuple-element.101.refs_0_), channel_id=1, source_target_pairs={{0,4},{1,5},{2,6},{3,7},{4,0},{5,1},{6,2},{7,3},{8,12},{9,13},{10,... | collective-permute-start | bytes 196616 | tf_op jit(solution)/shard_map/ppermute | solution.py:428
  75.0 0.8 copy.39.store_ref
  75.8 3.8 %hidden.1 = (f32[64,256]{1,0:T(8,128)S(1)}, f32[64,256]{1,0:T(8,128)S(1)}, f32[64,256]{1,0:T(8,128)S(1)}, f32[64,256]{1,0:T(8,128)S(1)}) custom-call(s32[4,2]{1,0:T(4,128)S(1)} %copy.39.store_ref, bf16[256,5120]{1,0:T(8,128)(2,1)S(1)} %copy-done, bf16[256,1280]{1,0:T(8,128)(2,1)} %collective-permute-done.1.refs_0_.refs_4_, ...), custom_call_target="tpu_custom_call" | custom-call | bytes 99000 | tf_op jit(solution)/shard_map/hidden/pallas_call | solution.py:549
  80.1 3.5 %grad_down.1 = (bf16[16,64,640]{2,1,0:T(8,128)(2,1)S(1)}, bf16[16,64,640]{2,1,0:T(8,128)(2,1)S(1)}) custom-call(s32[4,2]{1,0:T(4,128)S(1)} %copy.39.store_ref, bf16[256,5120]{1,0:T(8,128)(2,1)S(1)} %copy-done, bf16[2,64,256]{2,1,0:T(8,128)(2,1)} %get-tuple-element.101.refs_0_, bf16[2,64,256]{2,1,0:T(8,128)(2,1)} %collective-permute-done.12.refs_1_, ...), custom_call_target="tpu_custom_call" | custom-call | bytes 99000 | tf_op jit(solution)/shard_map/grad_down/pallas_call | solution.py:566
  83.6 1.2 collective-permute-start.18
  84.8 1.6 %collective-permute-start.19 = (f32[64,256]{1,0:T(8,128)S(1)}, f32[64,256]{1,0:T(8,128)S(1)}, u32[]{:S(2)}, u32[]{:S(2)}) collective-permute-start(f32[64,256]{1,0:T(8,128)S(1)} %get-tuple-element.75), channel_id=1, source_target_pairs={{0,4},{1,5},{2,6},{3,7},{4,0},{5,1},{6,2},{7,3},{8,12},{9,13},{10,... | collective-permute-start | bytes 196616 | tf_op jit(solution)/shard_map/ppermute | solution.py:428
  86.4 0.8 collective-permute-start.20
  87.2 1.0 collective-permute-done.18.refs_1_
  88.1 1.2 collective-permute-done.19.refs_2_
  89.4 2.1 %collective-permute-done.20.refs_3_ = f32[64,256]{1,0:T(8,128)S(1)} collective-permute-done((f32[64,256]{1,0:T(8,128)S(1)}, f32[64,256]{1,0:T(8,128)S(1)}, u32[]{:S(2)}, u32[]{:S(2)}) %collective-permute-start.20) | collective-permute-done | bytes 65568 | tf_op jit(solution)/shard_map/ppermute | solution.py:428
  91.5 0.9 values.1
  92.5 1.0 copy-done.9
  93.5 0.8 copy-done.13
  94.2 1.5 %add_convert_fusion = bf16[16,64,640]{2,1,0:T(8,128)(2,1)} fusion(bf16[16,64,640]{2,1,0:T(8,128)(2,1)S(1)} %collective-permute-done.17, bf16[16,64,640]{2,1,0:T(8,128)(2,1)S(1)} %get-tuple-element.72), kind=kLoop, calls=%fused_computation | loop fusion | flops 2621440 | bytes 3932160 | tf_op jit(solution)/shard_map/convert_element_type | solution.py:594
  95.7 4.5 %all-to-all-start.1 = ((bf16[16,64,640]{2,1,0:T(8,128)(2,1)}), bf16[16,64,640]{2,1,0:T(8,128)(2,1)}, u32[]{:S(2)}, u32[]{:S(2)}) async-start(bf16[16,64,640]{2,1,0:T(8,128)(2,1)} %add_convert_fusion), calls=%async_computation.1 | async-start | bytes 2621440 | tf_op jit(solution)/shard_map/all_to_all | solution.py:599
  100.6 1.9 %collective-permute-done.21.came_ref = bf16[8,64,512]{2,1,0:T(8,128)(2,1)S(1)} collective-permute-done((bf16[8,64,512]{2,1,0:T(8,128)(2,1)}, bf16[8,64,512]{2,1,0:T(8,128)(2,1)S(1)}, u32[]{:S(2)}, u32[]{:S(2)}) %collective-permute-start.21) | collective-permute-done | bytes 524320 | tf_op jit(solution)/shard_map/ppermute | solution.py:428
  102.5 1.2 copy-done.10
  103.8 1.8 %collective-permute-start.22 = (bf16[4,64,512]{2,1,0:T(8,128)(2,1)S(1)}, bf16[4,64,512]{2,1,0:T(8,128)(2,1)S(1)}, u32[]{:S(2)}, u32[]{:S(2)}) collective-permute-start(bf16[4,64,512]{2,1,0:T(8,128)(2,1)S(1)} %get-tuple-element.83), channel_id=1, source_target_pairs={{0,2},{1,3},{2,0},{3,1},{4,6},{5,7},{6,4},{7,5},{8,10},{9,11},{10,... | collective-permute-start | bytes 786440 | tf_op jit(solution)/shard_map/ppermute | solution.py:428
  105.6 1.7 %fusion.1 = (bf16[2,4,1,64,256]{4,3,0,1,2:T(8,128)(2,1)S(1)}, bf16[2,4,64,256]{3,2,0,1:T(8,128)(2,1)}) fusion(bf16[2,1,64,256]{3,2,0,1:T(8,128)(2,1)} %bitcast.16, bf16[2,1,64,256]{3,2,0,1:T(8,128)(2,1)} %bitcast.15, bf16[2,1,64,256]{3,2,0,1:T(8,128)(2,1)} %bitcast.14, bf16[2,1,64,256]{3,2,0,1:T(8,128)(2,1)} %get-tuple-element.100), kind=kLoop, calls=%fused_computation.15 | loop fusion | flops 393216 | bytes 786432 | tf_op jit(solution)/shard_map/stack | solution.py:597
  107.3 6.9 %second_pass.1 = bf16[256,4096]{1,0:T(8,128)(2,1)} custom-call(s32[2,128]{1,0:T(2,128)S(1)} %copy-done.12, bf16[256,4096]{1,0:T(8,128)(2,1)S(1)} %copy-done.4, bf16[256,512]{1,0:T(8,128)(2,1)S(1)} %copy-done.8, bf16[256,512]{1,0:T(8,128)(2,1)S(1)} %get-tuple-element.85.value_ref, bf16[256,4096]{1,0:T(8,128)(2,1)S(1)} %copy-done.6), custom_call_target="tpu_custom_call" | custom-call | bytes 297000 | tf_op jit(solution)/shard_map/second_pass/pallas_call | solution.py:602
  114.2 5.9 %collective-permute-done.22.came_ref = bf16[4,64,512]{2,1,0:T(8,128)(2,1)S(1)} collective-permute-done((bf16[4,64,512]{2,1,0:T(8,128)(2,1)S(1)}, bf16[4,64,512]{2,1,0:T(8,128)(2,1)S(1)}, u32[]{:S(2)}, u32[]{:S(2)}) %collective-permute-start.22) | collective-permute-done | bytes 262176 | tf_op jit(solution)/shard_map/ppermute | solution.py:428
  120.4 1.0 pad_maximum_fusion.2
  121.4 5.4 %grad_input.1 = bf16[320,4096]{1,0:T(8,128)(2,1)} custom-call(s32[16,2]{1,0:T(8,128)S(1)} %copy.41.store_ref, bf16[16,64,256]{2,1,0:T(8,128)(2,1)S(1)} %bitcast.28, bf16[16,32,640]{2,1,0:T(8,128)(2,1)S(1)} %all-to-all-done.refs_3_.refs_0_, bf16[16,32,640]{2,1,0:T(8,128)(2,1)} %collective-permute-done.11.refs_4_.refs_1_, ...), custom_call_target="tpu_custom_call" | custom-call | bytes 231000 | tf_op jit(solution)/shard_map/grad_input/pallas_call | solution.py:615
  126.9 1.0 all-to-all-done.1.part_ref
  127.9 6.0 %collective-permute-start.25 = (bf16[1,64,512]{2,1,0:T(8,128)(2,1)S(1)}, bf16[1,64,512]{2,1,0:T(8,128)(2,1)S(1)}, u32[]{:S(2)}, u32[]{:S(2)}) collective-permute-start(bf16[1,64,512]{2,1,0:T(8,128)(2,1)S(1)} %get-tuple-element.95), channel_id=1, source_target_pairs={{0,8},{1,9},{2,10},{3,11},{4,12},{5,13},{6,14},{7,15},{8,0},{9,1},... | collective-permute-start | bytes 196616 | tf_op jit(solution)/shard_map/ppermute | solution.py:428
  133.8 2.3 %sum_down.1 = bf16[1,64,5120]{2,1,0:T(8,128)(2,1)} custom-call(bf16[16,64,640]{2,1,0:T(8,128)(2,1)} %all-to-all-done.1.part_ref), custom_call_target="tpu_custom_call" | custom-call | bytes 66000 | tf_op jit(solution)/shard_map/sum_down/pallas_call | solution.py:653
  136.2 1.3 collective-permute-done.25.came_ref
  137.5 0.6 halve.7
  (66 shorter events, 2.4 us)
Async XLA Ops:
  0.6 8.1 %copy-start.16 = (bf16[1,64,512]{2,1,0:T(8,128)(2,1)S(1)}, bf16[1,64,512]{2,1,0:T(8,128)(2,1)}, u32[]{:S(2)}) copy-start(bf16[1,64,512]{2,1,0:T(8,128)(2,1)} %param.16) | copy-start | bytes 196612
  0.6 6.9 %copy-start.14 = (s32[2]{0:T(128)S(1)}, s32[2]{0:T(128)}, u32[]{:S(2)}) copy-start(s32[2]{0:T(128)} %tenant_ref.1) | copy-start | bytes 28
  0.7 6.9 %copy-start.15 = (s32[16]{0:T(128)S(1)}, s32[16]{0:T(128)}, u32[]{:S(2)}) copy-start(s32[16]{0:T(128)} %owner_ref.1) | copy-start | bytes 196
  0.7 20.6 %copy-start.3 = (bf16[256,4096]{1,0:T(8,128)(2,1)S(1)}, bf16[256,4096]{1,0:T(8,128)(2,1)}, u32[]{:S(2)}) copy-start(bf16[256,4096]{1,0:T(8,128)(2,1)} %query_ref.3) | copy-start | bytes 6291460
  0.7 20.6 %copy-start.7 = (bf16[256,512]{1,0:T(8,128)(2,1)S(1)}, bf16[256,512]{1,0:T(8,128)(2,1)}, u32[]{:S(2)}) copy-start(bf16[256,512]{1,0:T(8,128)(2,1)} %key_ref.3) | copy-start | bytes 786436
  0.7 20.6 %copy-start.12 = (s32[2,128]{1,0:T(2,128)S(1)}, s32[2,128]{1,0:T(2,128)}, u32[]{:S(2)}) copy-start(s32[2,128]{1,0:T(2,128)} %ids_ref.3) | copy-start | bytes 3076
  0.7 8.1 %collective-permute-start = (bf16[64,512]{1,0:T(8,128)(2,1)}, bf16[64,512]{1,0:T(8,128)(2,1)S(1)}, u32[]{:S(2)}, u32[]{:S(2)}) collective-permute-start(bf16[64,512]{1,0:T(8,128)(2,1)} %bitcast.32), channel_id=1, source_target_pairs={{0,8},{1,9},{2,10},{3,11},{4,12},{5,13},{6,14},{7,15},{8,0},{9,1},... | collective-permute-start | bytes 196616 | tf_op jit(solution)/shard_map/ppermute | solution.py:428
  8.8 42.6 %all-to-all-start = ((bf16[16,32,640]{2,1,0:T(8,128)(2,1)}), bf16[16,32,640]{2,1,0:T(8,128)(2,1)S(1)}, u32[]{:S(2)}, u32[]{:S(2)}) async-start(bf16[16,32,640]{2,1,0:T(8,128)(2,1)} %get-tuple-element.58), calls=%async_computation | async-start | bytes 1310720 | tf_op jit(solution)/shard_map/all_to_all | solution.py:510
  14.4 37.0 %collective-permute-start.1 = (bf16[256,1280]{1,0:T(8,128)(2,1)}, bf16[256,1280]{1,0:T(8,128)(2,1)}, u32[]{:S(2)}, u32[]{:S(2)}) collective-permute-start(bf16[256,1280]{1,0:T(8,128)(2,1)} %get-tuple-element.56), channel_id=1, source_target_pairs={{0,2},{1,3},{2,0},{3,1},{4,6},{5,7},{6,4},{7,5},{8,10},{9,11},{10,... | collective-permute-start | bytes 1966088 | tf_op jit(solution)/shard_map/ppermute | solution.py:428
  16.3 35.1 %collective-permute-start.2 = (bf16[256,1280]{1,0:T(8,128)(2,1)}, bf16[256,1280]{1,0:T(8,128)(2,1)}, u32[]{:S(2)}, u32[]{:S(2)}) collective-permute-start(bf16[256,1280]{1,0:T(8,128)(2,1)} %get-tuple-element.57), channel_id=1, source_target_pairs={{0,4},{1,5},{2,6},{3,7},{4,0},{5,1},{6,2},{7,3},{8,12},{9,13},{10,... | collective-permute-start | bytes 1966088 | tf_op jit(solution)/shard_map/ppermute | solution.py:428
  17.8 24.1 %collective-permute-start.3 = (bf16[144,512]{1,0:T(8,128)(2,1)S(1)}, bf16[144,512]{1,0:T(8,128)(2,1)}, u32[]{:S(2)}, u32[]{:S(2)}) collective-permute-start(bf16[144,512]{1,0:T(8,128)(2,1)S(1)} %pad_maximum_fusion.4), channel_id=1, source_target_pairs={{0,2},{1,3},{2,0},{3,1},{4,6},{5,7},{6,4},{7,5},{8,10},{9,11},{10,... | collective-permute-start | bytes 442376 | tf_op jit(solution)/shard_map/ppermute | solution.py:428
  18.4 27.5 %collective-permute-start.4 = (bf16[144,512]{1,0:T(8,128)(2,1)S(1)}, bf16[144,512]{1,0:T(8,128)(2,1)}, u32[]{:S(2)}, u32[]{:S(2)}) collective-permute-start(bf16[144,512]{1,0:T(8,128)(2,1)S(1)} %pad_maximum_fusion.4), channel_id=1, source_target_pairs={{0,4},{1,5},{2,6},{3,7},{4,0},{5,1},{6,2},{7,3},{8,12},{9,13},{10,... | collective-permute-start | bytes 442376 | tf_op jit(solution)/shard_map/ppermute | solution.py:428
  18.5 30.9 %collective-permute-start.5 = (bf16[144,512]{1,0:T(8,128)(2,1)S(1)}, bf16[144,512]{1,0:T(8,128)(2,1)}, u32[]{:S(2)}, u32[]{:S(2)}) collective-permute-start(bf16[144,512]{1,0:T(8,128)(2,1)S(1)} %pad_maximum_fusion.4), channel_id=1, source_target_pairs={{0,6},{1,7},{2,4},{3,5},{4,2},{5,3},{6,0},{7,1},{8,14},{9,15},{10,... | collective-permute-start | bytes 442376 | tf_op jit(solution)/shard_map/ppermute | solution.py:428
  21.3 1.6 %copy-start.5 = (bf16[256,4096]{1,0:T(8,128)(2,1)S(1)}, bf16[256,4096]{1,0:T(8,128)(2,1)}, u32[]{:S(2)}) copy-start(bf16[256,4096]{1,0:T(8,128)(2,1)} %grad_ref.3) | copy-start | bytes 6291460
  51.4 24.4 %copy-start = (bf16[256,5120]{1,0:T(8,128)(2,1)S(1)}, bf16[256,5120]{1,0:T(8,128)(2,1)}, u32[]{:S(2)}) copy-start(bf16[256,5120]{1,0:T(8,128)(2,1)} %x_ref.5) | copy-start | bytes 7864324
  51.4 11.3 %collective-permute-start.6 = (bf16[4,144,512]{2,1,0:T(8,128)(2,1)}, bf16[4,144,512]{2,1,0:T(8,128)(2,1)}, u32[]{:S(2)}, u32[]{:S(2)}) collective-permute-start(bf16[4,144,512]{2,1,0:T(8,128)(2,1)} %pad_maximum_fusion.1), channel_id=1, source_target_pairs={{0,1},{1,0},{2,3},{3,2},{4,5},{5,4},{6,7},{7,6},{8,9},{9,8},{10,11... | collective-permute-start | bytes 1769480 | tf_op jit(solution)/shard_map/ppermute | solution.py:428
  51.5 18.4 %collective-permute-start.8 = (bf16[256,1280]{1,0:T(8,128)(2,1)}, bf16[256,1280]{1,0:T(8,128)(2,1)}, u32[]{:S(2)}, u32[]{:S(2)}) collective-permute-start(bf16[256,1280]{1,0:T(8,128)(2,1)} %get-tuple-element.62), channel_id=1, source_target_pairs={{0,6},{1,7},{2,4},{3,5},{4,2},{5,3},{6,0},{7,1},{8,14},{9,15},{10,... | collective-permute-start | bytes 1966088 | tf_op jit(solution)/shard_map/ppermute | solution.py:428
  52.0 18.9 %collective-permute-start.11 = (bf16[16,32,640]{2,1,0:T(8,128)(2,1)S(1)}, bf16[16,32,640]{2,1,0:T(8,128)(2,1)}, u32[]{:S(2)}, u32[]{:S(2)}) collective-permute-start(bf16[16,32,640]{2,1,0:T(8,128)(2,1)S(1)} %all-to-all-done.refs_3_.refs_0_), channel_id=1, source_target_pairs={{0,16},{16,0},{1,17},{17,1},{2,18},{18,2},{3,19},{19,3},{4,20},{20... | collective-permute-start | bytes 1966088 | tf_op jit(solution)/shard_map/ppermute | solution.py:514
  53.5 22.3 %collective-permute-start.15 = (bf16[16,32,640]{2,1,0:T(8,128)(2,1)S(1)}, bf16[16,32,640]{2,1,0:T(8,128)(2,1)}, u32[]{:S(2)}, u32[]{:S(2)}) collective-permute-start(bf16[16,32,640]{2,1,0:T(8,128)(2,1)S(1)} %all-to-all-done.refs_3_.refs_0_), channel_id=1, source_target_pairs={{0,1},{1,0},{2,3},{3,2},{4,5},{5,4},{6,7},{7,6},{8,9},{9,8},{10,11... | collective-permute-start | bytes 1966088 | tf_op jit(solution)/shard_map/ppermute | solution.py:428
  56.9 1.3 copy-start.19
  56.9 1.3 collective-permute-start.9
  60.2 7.0 %copy-start.18 = (s32[8,2]{0,1:T(2,128)S(1)}, s32[8,2]{0,1:T(2,128)}, u32[]{:S(2)}) copy-start(s32[8,2]{0,1:T(2,128)} %reshape.32) | copy-start | bytes 196
  60.2 7.0 %collective-permute-start.10 = (s32[8,2]{0,1:T(2,128)}, s32[8,2]{0,1:T(2,128)S(1)}, u32[]{:S(2)}, u32[]{:S(2)}) collective-permute-start(s32[8,2]{0,1:T(2,128)} %reshape.32), channel_id=1, source_target_pairs={{0,8},{1,9},{2,10},{3,11},{4,12},{5,13},{6,14},{7,15},{8,0},{9,1},... | collective-permute-start | bytes 200 | tf_op jit(solution)/shard_map/ppermute | solution.py:428
  64.9 1.0 copy-start.1
  65.9 5.0 %collective-permute-start.7 = (bf16[64,256]{1,0:T(8,128)(2,1)S(1)}, bf16[64,256]{1,0:T(8,128)(2,1)S(1)}, u32[]{:S(2)}, u32[]{:S(2)}) collective-permute-start(bf16[64,256]{1,0:T(8,128)(2,1)S(1)} %grad_hidden.1), channel_id=1, source_target_pairs={{0,8},{1,9},{2,10},{3,11},{4,12},{5,13},{6,14},{7,15},{8,0},{9,1},... | collective-permute-start | bytes 98312 | tf_op jit(solution)/shard_map/ppermute | solution.py:428
  70.9 4.9 %collective-permute-start.16 = (bf16[16,32,640]{2,1,0:T(8,128)(2,1)}, bf16[16,32,640]{2,1,0:T(8,128)(2,1)}, u32[]{:S(2)}, u32[]{:S(2)}) collective-permute-start(bf16[16,32,640]{2,1,0:T(8,128)(2,1)} %collective-permute-done.11.refs_4_.refs_1_), channel_id=1, source_target_pairs={{0,1},{1,0},{2,3},{3,2},{4,5},{5,4},{6,7},{7,6},{8,9},{9,8},{10,11... | collective-permute-start | bytes 1966088 | tf_op jit(solution)/shard_map/ppermute | solution.py:428
  71.5 8.1 %collective-permute-start.12 = (bf16[2,64,256]{2,1,0:T(8,128)(2,1)}, bf16[2,64,256]{2,1,0:T(8,128)(2,1)}, u32[]{:S(2)}, u32[]{:S(2)}) collective-permute-start(bf16[2,64,256]{2,1,0:T(8,128)(2,1)} %get-tuple-element.101.refs_0_), channel_id=1, source_target_pairs={{0,2},{1,3},{2,0},{3,1},{4,6},{5,7},{6,4},{7,5},{8,10},{9,11},{10,... | collective-permute-start | bytes 196616 | tf_op jit(solution)/shard_map/ppermute | solution.py:428
  73.0 6.6 %collective-permute-start.13 = (bf16[2,64,256]{2,1,0:T(8,128)(2,1)}, bf16[2,64,256]{2,1,0:T(8,128)(2,1)}, u32[]{:S(2)}, u32[]{:S(2)}) collective-permute-start(bf16[2,64,256]{2,1,0:T(8,128)(2,1)} %get-tuple-element.101.refs_0_), channel_id=1, source_target_pairs={{0,4},{1,5},{2,6},{3,7},{4,0},{5,1},{6,2},{7,3},{8,12},{9,13},{10,... | collective-permute-start | bytes 196616 | tf_op jit(solution)/shard_map/ppermute | solution.py:428
  74.6 5.5 %collective-permute-start.14 = (bf16[2,64,256]{2,1,0:T(8,128)(2,1)}, bf16[2,64,256]{2,1,0:T(8,128)(2,1)}, u32[]{:S(2)}, u32[]{:S(2)}) collective-permute-start(bf16[2,64,256]{2,1,0:T(8,128)(2,1)} %get-tuple-element.101.refs_0_), channel_id=1, source_target_pairs={{0,6},{1,7},{2,4},{3,5},{4,2},{5,3},{6,0},{7,1},{8,14},{9,15},{10,... | collective-permute-start | bytes 196616 | tf_op jit(solution)/shard_map/ppermute | solution.py:428
  80.1 11.5 %copy-start.2 = (bf16[2,4,128,512]{3,2,1,0:T(8,128)(2,1)S(1)}, bf16[2,4,128,512]{3,2,1,0:T(8,128)(2,1)}, u32[]{:S(2)}) copy-start(bf16[2,4,128,512]{3,2,1,0:T(8,128)(2,1)} %copy-done.1) | copy-start | bytes 3145732
  80.1 11.5 %copy-start.11 = (bf16[256,512]{1,0:T(8,128)(2,1)S(1)}, bf16[256,512]{1,0:T(8,128)(2,1)}, u32[]{:S(2)}) copy-start(bf16[256,512]{1,0:T(8,128)(2,1)} %base_ref.1) | copy-start | bytes 786436
  83.6 10.7 %collective-permute-start.17 = (bf16[16,64,640]{2,1,0:T(8,128)(2,1)S(1)}, bf16[16,64,640]{2,1,0:T(8,128)(2,1)S(1)}, u32[]{:S(2)}, u32[]{:S(2)}) collective-permute-start(bf16[16,64,640]{2,1,0:T(8,128)(2,1)S(1)} %get-tuple-element.73), channel_id=1, source_target_pairs={{0,1},{1,0},{2,3},{3,2},{4,5},{5,4},{6,7},{7,6},{8,9},{9,8},{10,11... | collective-permute-start | bytes 3932168 | tf_op jit(solution)/shard_map/ppermute | solution.py:428
  83.6 4.5 %collective-permute-start.18 = (f32[64,256]{1,0:T(8,128)S(1)}, f32[64,256]{1,0:T(8,128)S(1)}, u32[]{:S(2)}, u32[]{:S(2)}) collective-permute-start(f32[64,256]{1,0:T(8,128)S(1)} %get-tuple-element.74), channel_id=1, source_target_pairs={{0,2},{1,3},{2,0},{3,1},{4,6},{5,7},{6,4},{7,5},{8,10},{9,11},{10,... | collective-permute-start | bytes 196616 | tf_op jit(solution)/shard_map/ppermute | solution.py:428
  84.8 4.6 %collective-permute-start.19 = (f32[64,256]{1,0:T(8,128)S(1)}, f32[64,256]{1,0:T(8,128)S(1)}, u32[]{:S(2)}, u32[]{:S(2)}) collective-permute-start(f32[64,256]{1,0:T(8,128)S(1)} %get-tuple-element.75), channel_id=1, source_target_pairs={{0,4},{1,5},{2,6},{3,7},{4,0},{5,1},{6,2},{7,3},{8,12},{9,13},{10,... | collective-permute-start | bytes 196616 | tf_op jit(solution)/shard_map/ppermute | solution.py:428
  86.4 5.2 %collective-permute-start.20 = (f32[64,256]{1,0:T(8,128)S(1)}, f32[64,256]{1,0:T(8,128)S(1)}, u32[]{:S(2)}, u32[]{:S(2)}) collective-permute-start(f32[64,256]{1,0:T(8,128)S(1)} %get-tuple-element.76), channel_id=1, source_target_pairs={{0,6},{1,7},{2,4},{3,5},{4,2},{5,3},{6,0},{7,1},{8,14},{9,15},{10,... | collective-permute-start | bytes 196616 | tf_op jit(solution)/shard_map/ppermute | solution.py:428
  92.5 1.0 copy-start.9
  93.5 0.8 copy-start.13
  95.7 11.6 %copy-start.4 = (bf16[256,4096]{1,0:T(8,128)(2,1)S(1)}, bf16[256,4096]{1,0:T(8,128)(2,1)}, u32[]{:S(2)}) copy-start(bf16[256,4096]{1,0:T(8,128)(2,1)} %query_ref.3) | copy-start | bytes 6291460
  95.7 11.6 %copy-start.8 = (bf16[256,512]{1,0:T(8,128)(2,1)S(1)}, bf16[256,512]{1,0:T(8,128)(2,1)}, u32[]{:S(2)}) copy-start(bf16[256,512]{1,0:T(8,128)(2,1)} %key_ref.3) | copy-start | bytes 786436
  95.7 32.1 %all-to-all-start.1 = ((bf16[16,64,640]{2,1,0:T(8,128)(2,1)}), bf16[16,64,640]{2,1,0:T(8,128)(2,1)}, u32[]{:S(2)}, u32[]{:S(2)}) async-start(bf16[16,64,640]{2,1,0:T(8,128)(2,1)} %add_convert_fusion), calls=%async_computation.1 | async-start | bytes 2621440 | tf_op jit(solution)/shard_map/all_to_all | solution.py:599
  100.3 7.0 %copy-start.6 = (bf16[256,4096]{1,0:T(8,128)(2,1)S(1)}, bf16[256,4096]{1,0:T(8,128)(2,1)}, u32[]{:S(2)}) copy-start(bf16[256,4096]{1,0:T(8,128)(2,1)} %grad_ref.3) | copy-start | bytes 6291460
  100.3 2.2 %collective-permute-start.21 = (bf16[8,64,512]{2,1,0:T(8,128)(2,1)}, bf16[8,64,512]{2,1,0:T(8,128)(2,1)S(1)}, u32[]{:S(2)}, u32[]{:S(2)}) collective-permute-start(bf16[8,64,512]{2,1,0:T(8,128)(2,1)} %copy-done.13), channel_id=1, source_target_pairs={{0,1},{1,0},{2,3},{3,2},{4,5},{5,4},{6,7},{7,6},{8,9},{9,8},{10,11... | collective-permute-start | bytes 1572872 | tf_op jit(solution)/shard_map/ppermute | solution.py:428
  102.5 1.2 copy-start.10
  103.8 16.4 %collective-permute-start.22 = (bf16[4,64,512]{2,1,0:T(8,128)(2,1)S(1)}, bf16[4,64,512]{2,1,0:T(8,128)(2,1)S(1)}, u32[]{:S(2)}, u32[]{:S(2)}) collective-permute-start(bf16[4,64,512]{2,1,0:T(8,128)(2,1)S(1)} %get-tuple-element.83), channel_id=1, source_target_pairs={{0,2},{1,3},{2,0},{3,1},{4,6},{5,7},{6,4},{7,5},{8,10},{9,11},{10,... | collective-permute-start | bytes 786440 | tf_op jit(solution)/shard_map/ppermute | solution.py:428
  107.3 13.0 %copy-start.17 = (s32[16,2]{0,1:T(2,128)S(1)}, s32[16,2]{0,1:T(2,128)}, u32[]{:S(2)}) copy-start(s32[16,2]{0,1:T(2,128)} %pad_add_fusion.1) | copy-start | bytes 388
  107.3 13.1 %collective-permute-start.24 = (bf16[2,4,64,256]{3,2,0,1:T(8,128)(2,1)}, bf16[2,4,64,256]{3,2,0,1:T(8,128)(2,1)}, u32[]{:S(2)}, u32[]{:S(2)}) collective-permute-start(bf16[2,4,64,256]{3,2,0,1:T(8,128)(2,1)} %get-tuple-element.99), channel_id=1, source_target_pairs={{0,1},{1,0},{2,3},{3,2},{4,5},{5,4},{6,7},{7,6},{8,9},{9,8},{10,11... | collective-permute-start | bytes 786440 | tf_op jit(solution)/shard_map/ppermute | solution.py:428
  120.2 6.7 %collective-permute-start.23 = (bf16[2,64,512]{2,1,0:T(8,128)(2,1)S(1)}, bf16[2,64,512]{2,1,0:T(8,128)(2,1)S(1)}, u32[]{:S(2)}, u32[]{:S(2)}) collective-permute-start(bf16[2,64,512]{2,1,0:T(8,128)(2,1)S(1)} %get-tuple-element.88), channel_id=1, source_target_pairs={{0,4},{1,5},{2,6},{3,7},{4,0},{5,1},{6,2},{7,3},{8,12},{9,13},{10,... | collective-permute-start | bytes 393224 | tf_op jit(solution)/shard_map/ppermute | solution.py:428
  127.9 9.6 %collective-permute-start.25 = (bf16[1,64,512]{2,1,0:T(8,128)(2,1)S(1)}, bf16[1,64,512]{2,1,0:T(8,128)(2,1)S(1)}, u32[]{:S(2)}, u32[]{:S(2)}) collective-permute-start(bf16[1,64,512]{2,1,0:T(8,128)(2,1)S(1)} %get-tuple-element.95), channel_id=1, source_target_pairs={{0,8},{1,9},{2,10},{3,11},{4,12},{5,13},{6,14},{7,15},{8,0},{9,1},... | collective-permute-start | bytes 196616 | tf_op jit(solution)/shard_map/ppermute | solution.py:428

commit v2 on v1

--- a/solution.py
+++ b/solution.py
@@ -1,3 +1,4 @@
+import functools
 import math
 
 import jax
@@ -202,14 +203,9 @@
         copy.wait()
 
 
-def store_kernel(tenant_ref, owner_ref, slot_ref, row_ref, wide):
+def store_kernel(tenant_ref, owner_ref, out_ref):
     for k in range(2):
-        slot_ref[k] = owner_ref[tenant_ref[k]]
-    lane = lax.broadcasted_iota(jnp.int32, wide.shape, 1)
-    wide[...] = jnp.where(
-        lane < wide.shape[1] // 2, slot_ref[0].astype(jnp.float32), slot_ref[1].astype(jnp.float32)
-    )
-    row_ref[...] = wide[...].astype(jnp.bfloat16)
+        out_ref[k] = owner_ref[tenant_ref[k]]
 
 
 def heads_in_rows(ref):
@@ -257,16 +253,24 @@
         out_ref[:, lanes] = out[:, lanes].T.astype(jnp.bfloat16)
 
 
-def grad_hidden_kernel(slot_ref, dval_ref, up_ref, *refs):
-    out_ref = refs[-1]
-    rank = out_ref.shape[0]
+def grad_hidden_kernel(slot_ref, store_ref, dval_ref, up_ref, out_ref):
+    rank = up_ref.shape[1]
     out = lax.dot_general(
-        up_ref[0],
-        dval_ref[...],
-        (((1,), (1,)), ((), ())),
-        preferred_element_type=jnp.float32,
-    )
-    out_ref[...] = (adapter_scale * out).astype(jnp.bfloat16)
+        up_ref[0], dval_ref[...], (((1,), (1,)), ((), ())), preferred_element_type=jnp.float32
+    )
+    out_ref[pl.ds(0, rank), :] = (adapter_scale * out).astype(jnp.bfloat16)
+    store = store_ref[pl.program_id(0)].astype(jnp.float32)
+    below = jnp.full((16, out_ref.shape[1]), store, jnp.float32)
+    out_ref[pl.ds(rank, 16), :] = below.astype(jnp.bfloat16)
+
+
+def read_stores(values, rank, wide, stores, sem):
+    for k, value in enumerate(values):
+        row = value[pl.ds(rank, 16), :].astype(jnp.float32)[0:1, :]
+        wide[pl.ds(k, 1), :] = row.astype(jnp.int32)
+    copy = pltpu.make_async_copy(wide, stores, sem)
+    copy.start()
+    copy.wait()
 
 
 def x_copies(x_ref, near, rows):
@@ -282,21 +286,27 @@
     return pairs
 
 
-def hidden_kernel(store_ref, x_ref, *refs):
-    near, downs, outs, (rows, down, sems) = refs[:3], refs[3:7], refs[7:11], refs[11:]
+def hidden_kernel(x_ref, *refs):
+    grads, near, downs, outs = refs[:4], refs[4:7], refs[7:11], refs[11:15]
+    rows, down, wide, stores, sems = refs[15:]
     me, group = lax.axis_index("dp"), lax.axis_index("groups")
     core = me & 1
     span, half = downs[0].shape[2], downs[0].shape[1]
     block = x_ref.shape[0] // 2
-    pairs = x_copies(x_ref, near, rows)
+    copies = run_copies(x_copies(x_ref, near, rows), sems)
+    read_stores(grads, 2 * half, wide, stores, sems.at[len(copies)])
     for slot in range(CHIPS):
         for k in range(2):
-            store = store_ref[slot, k]
+            store = stores[slot, k * block]
             for kind, ref in enumerate(downs):
                 ranks = pl.ds(pl.multiple_of((group ^ (kind & 1)) * half, 16), half)
                 lanes = columns(core ^ (kind >> 1), span)
-                pairs.append((ref.at[store], down.at[2 * slot + k, ranks, lanes]))
-    for copy in run_copies(pairs, sems):
+                copy = pltpu.make_async_copy(
+                    ref.at[store], down.at[2 * slot + k, ranks, lanes], sems.at[len(copies) + 1]
+                )
+                copy.start()
+                copies.append(copy)
+    for copy in copies:
         copy.wait()
     for slot in range(CHIPS):
         for k in range(2):
@@ -309,21 +319,20 @@
             outs[slot][:, pl.ds(k * block, block)] = out
 
 
-def grad_down_kernel(store_ref, x_ref, *refs):
-    grads, near, (keep_ref, send_ref, rows, total, sems) = refs[:4], refs[4:7], refs[8:]
-    me = lax.axis_index("dp")
-    core = me & 1
-    span = keep_ref.shape[2]
+def grad_down_kernel(x_ref, *refs):
+    grads, near, (keep_ref, send_ref, rows, total, wide, stores, sems) = refs[:4], refs[4:7], refs[7:]
+    core = lax.axis_index("dp") & 1
+    rank, span = keep_ref.shape[1:]
     block = x_ref.shape[0] // 2
     copies = run_copies(x_copies(x_ref, near, rows), sems)
+    read_stores(grads, rank, wide, stores, sems.at[len(copies)])
     total[...] = jnp.zeros_like(total)
     for copy in copies:
         copy.wait()
     for slot in range(CHIPS):
         for k in range(2):
-            store = store_ref[slot, k]
-            total[store] += jnp.dot(
-                grads[slot][0, :, pl.ds(k * block, block)],
+            total[stores[slot, k * block]] += jnp.dot(
+                grads[slot][pl.ds(0, rank), pl.ds(k * block, block)],
                 rows[slot, pl.ds(k * block, block), :],
                 preferred_element_type=jnp.float32,
             )
@@ -340,7 +349,7 @@
 
 
 def values_kernel(slot_ref, up_slot_ref, base_ref, dval_ref, up_ref, *refs):
-    hidden_refs, (val_ref, keep_ref, send_ref) = refs[:CHIPS], refs[CHIPS:]
+    hidden_refs, (val_ref, keep_ref, send_ref) = refs[:CHIPS], refs[CHIPS + 1 :]
     rank = keep_ref.shape[1]
     block = base_ref.shape[0] // 2
     hidden = hidden_refs[0][...]
@@ -375,14 +384,15 @@
                 ref[slot_ref[k] >> 1] = terms[k].astype(ref.dtype)
 
 
-def halve_kernel(kept_ref, came_ref, *outs):
+def halve_kernel(kept_ref, came_ref, *outs, extra=0):
+    outs = outs[extra:]
     for k in range(kept_ref.shape[0]):
         ref = outs[k % len(outs)]
         ref[k // len(outs)] = (kept_ref[k] + came_ref[k].astype(jnp.float32)).astype(ref.dtype)
 
 
-def grad_input_kernel(store_ref, grad_ref, *refs):
-    downs, (out_ref, down, wide, turned, sems) = refs[:4], refs[4:]
+def grad_input_kernel(grad_ref, *refs):
+    downs, (out_ref, down, wide, turned, marks, stores, sems) = refs[:4], refs[4:]
     me, group = lax.axis_index("dp"), lax.axis_index("groups")
     core = me & 1
     block = grad_ref.shape[2] // 2
@@ -402,6 +412,7 @@
                 src = downs[2 * side + kind]
                 pltpu.make_async_copy(src, places(kind), sems.at[kind]).start()
 
+    read_stores([grad_ref.at[k] for k in range(SPAN)], 2 * half, marks, stores, sems.at[2])
     for kind in range(2):
         pltpu.make_async_copy(downs[kind], places(kind), sems.at[kind]).wait()
     lanes = pl.ds(pl.multiple_of(core * (span - window), 128), window)
@@ -412,8 +423,8 @@
     for mask in range(SPAN):
         for k in range(2):
             out = jnp.dot(
-                turned[store_ref[mask, k]],
-                grad_ref[mask, :, pl.ds(k * block, block)],
+                turned[stores[mask, k * block]],
+                grad_ref[mask, pl.ds(0, 2 * half), pl.ds(k * block, block)],
                 preferred_element_type=jnp.float32,
             )
             at = pl.multiple_of(((mask ^ me) * 2 + k) * block, 128)
@@ -482,13 +493,11 @@
         name="pack",
     )(x_rows, adapt_down)
 
-    slots, slot_rows = pl.pallas_call(
+    own_stores = pl.pallas_call(
         store_kernel,
         in_specs=[smem_spec] * 2,
-        out_specs=[smem_spec, vmem_spec],
-        out_shape=[shape((blocks,), jnp.int32), shape((16, value_width), bf16)],
-        scratch_shapes=[pltpu.VMEM((16, value_width), f32)],
-        compiler_params=params,
+        out_specs=smem_spec,
+        out_shape=shape((blocks,), jnp.int32),
         name="store_rows",
     )(block_tenant, owner_map)
 
@@ -503,83 +512,85 @@
         name="first_pass",
     )(seq_ids, query_rows, key_rows, grad_out)
 
-    up_pair = jnp.concatenate([adapt_up[0], swap(adapt_up[0], 8), slot_rows])
-    x_packs[0], x_packs[1], x_packs[2], down_pack, up_pair = together(*x_packs, down_pack, up_pair)
-    near_up = jnp.stack([up_pair] + [swap(up_pair, 2 * k) for k in range(1, CHIPS)])
+    up_pair = jnp.concatenate([adapt_up, swap(adapt_up, 8)])
+    x_packs[0], x_packs[1], x_packs[2], up_pair = together(*x_packs, up_pair)
+    peers = [[first + 2 * k for k in range(CHIPS)] for first in (0, 1, 8, 9)]
+    near_up = lax.all_to_all(
+        jnp.broadcast_to(up_pair, (CHIPS,) + up_pair.shape), "dp", 0, 0, axis_index_groups=peers
+    )
     near = [swap(x_packs[k], 2 * (k + 1)) for k in range(CHIPS - 1)]
+    down_pack, near_up = together(down_pack, near_up)
     down_own = lax.all_to_all(down_pack, "dp", split_axis=0, concat_axis=0, tiled=True)
-    near[0], near[1], down_own, near_up, dvalues = together(
-        near[0], near[1], down_own, near_up, dvalues
-    )
-    down_other = lax.ppermute(down_own, "groups", [(0, 1), (1, 0)])
-    near_stores = near_up[:, 2 * rank].reshape(CHIPS, 2, -1)[:, :, 0].astype(jnp.int32)
-    all_up = jnp.stack([near_up, swap(near_up, 1)])
-    stores = jnp.stack([near_stores, swap(near_stores, 1)], axis=1).reshape(2 * CHIPS, blocks)
-    stores = jnp.concatenate([stores, swap(stores, 8)])
-    all_up = all_up[:, :, : 2 * rank].reshape((SPAN,) + adapt_up.shape[1:])
+    near[0], near[1], near_up, dvalues = together(near[0], near[1], near_up, dvalues)
+    all_up = jnp.stack([near_up, swap(near_up, 1)]).reshape((SPAN,) + adapt_up.shape[1:])
     me = lax.axis_index("dp")
-    slots = slots ^ me
-    up_slots = 8 * (slots & 1) + 2 * ((slots >> 1) & 3) + (slots >> 3)
+    slots = own_stores ^ me
+    up_slots = 8 * (slots & 1) + (own_stores & 6) + (slots >> 3)
 
     hidden_gradient = pl.pallas_call(
         grad_hidden_kernel,
         grid_spec=pltpu.PrefetchScalarGridSpec(
-            num_scalar_prefetch=1,
+            num_scalar_prefetch=2,
             grid=(blocks,),
             in_specs=[
-                pl.BlockSpec((block, value_width), lambda b, slot: (b, 0)),
-                pl.BlockSpec((1, rank, value_width), lambda b, slot: (slot[b], 0, 0)),
+                pl.BlockSpec((block, value_width), lambda b, slot, store: (b, 0)),
+                pl.BlockSpec((1, rank, value_width), lambda b, slot, store: (slot[b], 0, 0)),
             ],
-            out_specs=pl.BlockSpec((rank, block), lambda b, slot: (0, b)),
+            out_specs=pl.BlockSpec((rank + 16, block), lambda b, slot, store: (0, b)),
         ),
-        out_shape=shape((rank, tok_rows), bf16),
+        out_shape=shape((rank + 16, tok_rows), bf16),
         compiler_params=params,
         cost_estimate=cost(1),
         name="grad_hidden",
-    )(up_slots, dvalues, all_up)
-    far_gradient = swap(hidden_gradient, 8)
-    hidden_gradient, far_gradient, near[2], near_stores, stores, down_other = together(
-        hidden_gradient, far_gradient, near[2], near_stores, stores, down_other
-    )
-    both = jnp.stack([hidden_gradient, far_gradient])
-    near_grad = [both] + [swap(both, 2 * k) for k in range(1, CHIPS)]
-
+    )(up_slots, own_stores, dvalues, all_up)
+    down_own, hidden_gradient = together(down_own, hidden_gradient)
+    near_grad = [hidden_gradient] + [swap(hidden_gradient, 2 * k) for k in range(1, CHIPS)]
+    down_other = lax.ppermute(down_own, "groups", [(0, 1), (1, 0)])
+    down_other, *held = together(down_other, near[2], *near_grad)
     downs = [down_own, down_other, swap(down_own, 1), swap(down_other, 1)]
 
     hidden_parts = pl.pallas_call(
         hidden_kernel,
-        in_specs=[smem_spec] + [any_spec] * (CHIPS + 4),
+        in_specs=[any_spec] + [vmem_spec] * CHIPS + [any_spec] * (CHIPS + 3),
         out_specs=[vmem_spec] * CHIPS,
         out_shape=[shape((rank, tok_rows), f32)] * CHIPS,
         scratch_shapes=[
             pltpu.VMEM((CHIPS, tok_rows, 2 * span), bf16),
             pltpu.VMEM((2 * CHIPS, rank, 2 * span), bf16),
-            pltpu.SemaphoreType.DMA((9 * CHIPS + 1,)),
+            pltpu.VMEM((8, tok_rows), jnp.int32),
+            pltpu.SMEM((8, tok_rows), jnp.int32),
+            pltpu.SemaphoreType.DMA((9 * CHIPS + 2,)),
         ],
         compiler_params=params,
         cost_estimate=cost(3),
         name="hidden",
-    )(near_stores, x_rows, *near, *downs)
+    )(x_rows, *held[1:], near[0], near[1], held[0], *downs)
     own_part = hidden_parts[0]
-    hidden_parts = [own_part] + [swap(hidden_parts[k], 2 * k) for k in range(1, CHIPS)]
+    hidden_parts = [swap(hidden_parts[k], 2 * k) for k in range(1, CHIPS)]
 
     down_keep, down_send = pl.pallas_call(
         grad_down_kernel,
-        in_specs=[smem_spec, any_spec] + [vmem_spec] * CHIPS + [any_spec] * CHIPS,
+        in_specs=[any_spec] + [vmem_spec] * CHIPS + [any_spec] * (CHIPS - 1),
         out_specs=[vmem_spec] * 2,
         out_shape=[shape((SPAN, rank, span), bf16)] * 2,
         scratch_shapes=[
             pltpu.VMEM((CHIPS, tok_rows, 2 * span), bf16),
             pltpu.VMEM((SPAN, rank, 2 * span), f32),
-            pltpu.SemaphoreType.DMA((CHIPS + 1,)),
+            pltpu.VMEM((8, tok_rows), jnp.int32),
+            pltpu.SMEM((8, tok_rows), jnp.int32),
+            pltpu.SemaphoreType.DMA((CHIPS + 2,)),
         ],
         compiler_params=params,
         cost_estimate=cost(3),
         name="grad_down",
-    )(near_stores, x_rows, *near_grad, *near, own_part)
+    )(x_rows, *near_grad, *near)
+    all_grad = jnp.stack(near_grad)
+    far_grad, own_part = together(swap(all_grad, 8), own_part)
+    all_grad = jnp.stack([all_grad, far_grad])
+    down_parts = (down_keep.astype(f32) + swap(down_send, 1).astype(f32)).astype(bf16)
     value_rows, kept, sent = pl.pallas_call(
         values_kernel,
-        in_specs=[smem_spec] * 2 + [vmem_spec] * (3 + CHIPS),
+        in_specs=[smem_spec] * 2 + [vmem_spec] * (3 + CHIPS) + [any_spec],
         out_specs=[vmem_spec] * 3,
         out_shape=[
             shape((tok_rows, value_width), bf16),
@@ -589,11 +600,11 @@
         compiler_params=params,
         cost_estimate=cost(1),
         name="values",
-    )(slots, up_slots, values_base, dvalues, all_up, *hidden_parts)
-
-    down_parts = (down_keep.astype(f32) + swap(down_send, 1).astype(f32)).astype(bf16)
-    down_parts, value_rows, kept, sent = together(down_parts, value_rows, kept, sent)
-    all_grad = jnp.stack(near_grad, axis=1)
+    )(slots, up_slots, values_base, dvalues, all_up, own_part, *hidden_parts, down_parts)
+
+    down_parts, value_rows, kept, sent, all_grad = together(
+        down_parts, value_rows, kept, sent, all_grad
+    )
     all_grad = jnp.stack([all_grad, swap(all_grad, 1)], axis=2)
     all_grad = all_grad.reshape((SPAN,) + hidden_gradient.shape)
     down_parts = lax.all_to_all(down_parts, "dp", split_axis=0, concat_axis=0, tiled=True)
@@ -614,41 +625,21 @@
     window = -(-feats // 128) * 128
     grad_input_t = pl.pallas_call(
         grad_input_kernel,
-        in_specs=[smem_spec, vmem_spec] + [any_spec] * 4,
+        in_specs=[vmem_spec] + [any_spec] * 4,
         out_specs=vmem_spec,
         out_shape=shape((feats, SPAN * tok_rows), bf16),
         scratch_shapes=[
             pltpu.VMEM((SPAN, rank, span), bf16),
             pltpu.VMEM((window, rank), f32),
             pltpu.VMEM((SPAN, feats, rank), bf16),
-            pltpu.SemaphoreType.DMA((2,)),
+            pltpu.VMEM((SPAN, tok_rows), jnp.int32),
+            pltpu.SMEM((SPAN, tok_rows), jnp.int32),
+            pltpu.SemaphoreType.DMA((3,)),
         ],
         compiler_params=params,
         cost_estimate=cost(7),
         name="grad_input",
-    )(stores, all_grad, *downs)
-
-    for mask in (1, 2, 4, 8):
-        if mask == 4:
-            sent, grad_query = together(sent, grad_query)
-        if mask == 8:
-            sent, down_parts, grad_input_t = together(sent, down_parts, grad_input_t)
-        came = swap(sent, mask)
-        count = max(came.shape[0] // 2, 1)
-        outs = [shape((count,) + came.shape[1:], bf16)]
-        if mask < 8:
-            outs = [shape(outs[0].shape, f32)] + outs
-        halves = pl.pallas_call(
-            halve_kernel,
-            in_specs=[vmem_spec] * 2,
-            out_specs=[vmem_spec] * len(outs),
-            out_shape=outs,
-            compiler_params=params,
-            cost_estimate=cost(1),
-            name="halve",
-        )(kept, came)
-        kept, sent = halves[0], halves[-1]
-    grad_up = sent
+    )(all_grad, *downs)
 
     grad_down = pl.pallas_call(
         sum_kernel,
@@ -659,6 +650,29 @@
         cost_estimate=cost(2),
         name="sum_down",
     )(down_parts)
+    for mask in (1, 2, 4, 8):
+        if mask == 4:
+            sent, grad_query = together(sent, grad_query)
+        if mask == 8:
+            sent, grad_input_t = together(sent, grad_input_t)
+        came = swap(sent, mask)
+        last = (grad_down,) if mask == 8 else ()
+        count = max(came.shape[0] // 2, 1)
+        outs = [shape((count,) + came.shape[1:], bf16)]
+        if mask < 8:
+            outs = [shape(outs[0].shape, f32)] + outs
+        halves = pl.pallas_call(
+            functools.partial(halve_kernel, extra=len(last)),
+            in_specs=[vmem_spec] * 2 + [any_spec] * len(last),
+            out_specs=[vmem_spec] * len(outs),
+            out_shape=outs,
+            compiler_params=params,
+            cost_estimate=cost(1),
+            name="halve",
+        )(kept, came, *last)
+        kept, sent = halves[0], halves[-1]
+    grad_up = sent
+
     return (grad_query, grad_input_t, grad_down, grad_up)
 
 

time: 139 us -> 130 us (0.935)
  other arithmetic: 9.94 us -> 4.34 us
  Pallas kernels: 33.2 us -> 30.5 us
  starting transfers between devices: 41.9 us -> 40.4 us
    ppermute x25 -> x20, waiting for transfers between devices: 40.5 us -> 33.9 us  [swap(): return lax.ppermute(value, 'dp', [(i, i ^ mask) for i in range(SPAN)])]
    all_to_all x0 -> x1, waiting for transfers between devices: none -> 6.06 us  [local_clustered(): lax.all_to_all(jnp.broadcast_to(up_pair, (CHIPS,) + up_pair.shape), 'dp',...]
    ppermute x25 -> x20, starting transfers between devices: 30.3 us -> 25.5 us  [swap(): return lax.ppermute(value, 'dp', [(i, i ^ mask) for i in range(SPAN)])]
    all_to_all x0 -> x1, starting transfers between devices: none -> 4.13 us  [local_clustered(): lax.all_to_all(jnp.broadcast_to(up_pair, (CHIPS,) + up_pair.shape), 'dp',...]
    unnamed x41 -> x54, local copies, waits for them, and re-layouts: 6.22 us -> 10.3 us
    pallas_call x8, Pallas kernels: 14.7 us -> 12.1 us  [the longest x1 4.57 us: local_clustered(): pl.pallas_call(grad_input_kernel, in_specs=[vmem_spec] + [any_spec] * 4,...]
    another operation x2 -> x1, other arithmetic: 2.68 us -> 0.06 us  [local_clustered(): all_grad = jnp.stack([all_grad, swap(all_grad, 1)], axis=2)]
    another operation x4 -> x3, other arithmetic: 4.46 us -> 2.09 us  [the longest x1 1.3 us: local_clustered(): jnp.stack([near_up, swap(near_up, 1)]).reshape((SPAN,) + adapt_up.shape[1:])]
  transfers between devices with their start and end apart: 28 -> 24, of which waited for: 15 -> 16; matrix products, arithmetic and copies ran while one was open for 10% -> 3% of each run, Pallas kernels for 21% -> 22%
where the time goes in v2:
time: 130 us; the launch traced here: 129 us
  waiting for transfers between devices  41.3 us (32%)
  starting transfers between devices  40.4 us (31%)
  Pallas kernels  30.5 us (23%)
  local copies, waits for them, and re-layouts  11.2 us (9%)
  other arithmetic  4.34 us (3%)
    ppermute x20, waiting for transfers between devices, swap(): return lax.ppermute(value, 'dp', [(i, i ^ mask) for i in range(SPAN)])  33.9 us
    ppermute x20, starting transfers between devices, swap(): return lax.ppermute(value, 'dp', [(i, i ^ mask) for i in range(SPAN)])  25.5 us
    unnamed x54, local copies, waits for them, and re-layouts  10.3 us
    pallas_call x1, Pallas kernels, local_clustered(): pl.pallas_call(second_kernel, grid=(blocks, heads), in_specs=[vmem_spec,...  6.87 us
    all_to_all x1, waiting for transfers between devices, local_clustered(): lax.all_to_all(jnp.broadcast_to(up_pair, (CHIPS,) + up_pair.shape), 'dp',...  6.06 us
    all_to_all x1, starting transfers between devices, local_clustered(): lax.all_to_all(down_parts, 'dp', split_axis=0, concat_axis=0, tiled=True)  4.95 us
    pallas_call x1, Pallas kernels, local_clustered(): pl.pallas_call(first_kernel, grid=(blocks, heads), in_specs=[vmem_spec, w...  4.67 us
    pallas_call x1, Pallas kernels, local_clustered(): pl.pallas_call(grad_input_kernel, in_specs=[vmem_spec] + [any_spec] * 4,...  4.57 us
  transfers between devices with their start and end apart: 24, of which 16 were waited for; matrix products, arithmetic and copies ran while one was open for 3% of the time, Pallas kernels for 22%

profile of v2, /device:TPU:0, one launch (start us, length us, event | category | flops | bytes accessed | tf_op | source)
XLA Modules:
  0.0 128.8 jit_solution(12742899221793065075)
XLA Ops:
  0.6 4.1 %collective-permute-start = (bf16[1,64,512]{2,1,0:T(8,128)(2,1)}, bf16[1,64,512]{2,1,0:T(8,128)(2,1)S(1)}, u32[]{:S(2)}, u32[]{:S(2)}) collective-permute-start(bf16[1,64,512]{2,1,0:T(8,128)(2,1)} %param.16), channel_id=1, source_target_pairs={{0,8},{1,9},{2,10},{3,11},{4,12},{5,13},{6,14},{7,15},{8,0},{9,1},... | collective-permute-start | bytes 196616 | tf_op jit(solution)/shard_map/ppermute | solution.py:439
  4.7 2.8 %pack.1 = (bf16[16,32,640]{2,1,0:T(8,128)(2,1)}, bf16[256,1280]{1,0:T(8,128)(2,1)}, bf16[256,1280]{1,0:T(8,128)(2,1)}, bf16[256,1280]{1,0:T(8,128)(2,1)}) custom-call(bf16[256,5120]{1,0:T(8,128)(2,1)} %x_ref.5, bf16[1,64,5120]{2,1,0:T(8,128)(2,1)} %down_ref.1), custom_call_target="tpu_custom_call" | custom-call | bytes 82500 | tf_op jit(solution)/shard_map/pack/pallas_call | solution.py:480
  7.6 1.0 collective-permute-done
  8.6 0.8 broadcast_in_dim.3
  9.5 4.1 %all-to-all-start = ((bf16[4,2,64,512]{3,2,1,0:T(8,128)(2,1)}), bf16[4,2,64,512]{3,2,1,0:T(8,128)(2,1)}, u32[]{:S(2)}, u32[]{:S(2)}) async-start(bf16[4,2,64,512]{3,2,1,0:T(8,128)(2,1)} %broadcast_in_dim.3), calls=%async_computation | async-start | bytes 1048576 | tf_op jit(solution)/shard_map/all_to_all | solution.py:518
  13.6 2.0 %collective-permute-start.1 = (bf16[256,1280]{1,0:T(8,128)(2,1)}, bf16[256,1280]{1,0:T(8,128)(2,1)}, u32[]{:S(2)}, u32[]{:S(2)}) collective-permute-start(bf16[256,1280]{1,0:T(8,128)(2,1)} %get-tuple-element.58), channel_id=1, source_target_pairs={{0,2},{1,3},{2,0},{3,1},{4,6},{5,7},{6,4},{7,5},{8,10},{9,11},{10,... | collective-permute-start | bytes 1966088 | tf_op jit(solution)/shard_map/ppermute | solution.py:439
  15.6 1.5 %collective-permute-start.2 = (bf16[256,1280]{1,0:T(8,128)(2,1)}, bf16[256,1280]{1,0:T(8,128)(2,1)}, u32[]{:S(2)}, u32[]{:S(2)}) collective-permute-start(bf16[256,1280]{1,0:T(8,128)(2,1)} %get-tuple-element.59), channel_id=1, source_target_pairs={{0,4},{1,5},{2,6},{3,7},{4,0},{5,1},{6,2},{7,3},{8,12},{9,13},{10,... | collective-permute-start | bytes 1966088 | tf_op jit(solution)/shard_map/ppermute | solution.py:439
  17.1 6.1 %all-to-all-done = bf16[4,2,64,512]{3,2,1,0:T(8,128)(2,1)} async-done(((bf16[4,2,64,512]{3,2,1,0:T(8,128)(2,1)}), bf16[4,2,64,512]{3,2,1,0:T(8,128)(2,1)}, u32[]{:S(2)}, u32[]{:S(2)}) %all-to-all-start) | async-done | bytes 524320 | tf_op jit(solution)/shard_map/all_to_all | solution.py:518
  23.1 4.4 %all-to-all-start.1 = ((bf16[16,32,640]{2,1,0:T(8,128)(2,1)}), bf16[16,32,640]{2,1,0:T(8,128)(2,1)S(1)}, u32[]{:S(2)}, u32[]{:S(2)}) async-start(bf16[16,32,640]{2,1,0:T(8,128)(2,1)} %get-tuple-element.57), calls=%async_computation.1 | async-start | bytes 1310720 | tf_op jit(solution)/shard_map/all_to_all | solution.py:523
  27.5 1.6 %copy-done.5 = bf16[256,4096]{1,0:T(8,128)(2,1)S(1)} copy-done((bf16[256,4096]{1,0:T(8,128)(2,1)S(1)}, bf16[256,4096]{1,0:T(8,128)(2,1)}, u32[]{:S(2)}) %copy-start.5) | copy-done | bytes 2097176
  29.1 4.7 %first_pass.1.dval_ref = bf16[256,512]{1,0:T(8,128)(2,1)S(1)} custom-call(s32[2,128]{1,0:T(2,128)S(1)} %copy-done.22, bf16[256,4096]{1,0:T(8,128)(2,1)S(1)} %copy-done.3, bf16[256,512]{1,0:T(8,128)(2,1)S(1)} %copy-done.14, bf16[256,4096]{1,0:T(8,128)(2,1)S(1)} %copy-done.5), custom_call_target="tpu_custom_call" | custom-call | bytes 231000 | tf_op jit(solution)/shard_map/first_pass/pallas_call | solution.py:504
  33.8 3.9 %collective-permute-done.1.refs_4_ = bf16[256,1280]{1,0:T(8,128)(2,1)} collective-permute-done((bf16[256,1280]{1,0:T(8,128)(2,1)}, bf16[256,1280]{1,0:T(8,128)(2,1)}, u32[]{:S(2)}, u32[]{:S(2)}) %collective-permute-start.1) | collective-permute-done | bytes 655392 | tf_op jit(solution)/shard_map/ppermute | solution.py:439
  37.7 4.1 %collective-permute-done.2.refs_5_ = bf16[256,1280]{1,0:T(8,128)(2,1)} collective-permute-done((bf16[256,1280]{1,0:T(8,128)(2,1)}, bf16[256,1280]{1,0:T(8,128)(2,1)}, u32[]{:S(2)}, u32[]{:S(2)}) %collective-permute-start.2) | collective-permute-done | bytes 655392 | tf_op jit(solution)/shard_map/ppermute | solution.py:439
  41.9 1.2 store_rows.1.store_ref
  43.1 0.7 broadcast_xor_fusion
  43.7 0.4 collective-permute-done.3
  44.1 1.3 %pad_maximum_fusion = bf16[2,4,2,64,512]{4,3,2,1,0:T(8,128)(2,1)S(1)} fusion(bf16[1,4,2,64,512]{4,3,2,1,0:T(8,128)(2,1)} %bitcast.1, bf16[1,4,2,64,512]{4,3,2,1,0:T(8,128)(2,1)} %bitcast), kind=kLoop, calls=%fused_computation.1 | loop fusion | flops 524288 | bytes 2097152 | tf_op jit(solution)/shard_map/stack | solution.py:525
  45.4 0.6 copy-done.23
  46.1 0.9 grad_hidden.1.refs_0_
  47.0 1.0 copy-done.1
  48.0 0.6 copy-done.18
  48.6 1.3 all-to-all-done.1.refs_7_.refs_0_
  49.9 1.5 %collective-permute-start.10 = (bf16[16,32,640]{2,1,0:T(8,128)(2,1)S(1)}, bf16[16,32,640]{2,1,0:T(8,128)(2,1)S(1)}, u32[]{:S(2)}, u32[]{:S(2)}) collective-permute-start(bf16[16,32,640]{2,1,0:T(8,128)(2,1)S(1)} %all-to-all-done.1.refs_7_.refs_0_), channel_id=1, source_target_pairs={{0,16},{16,0},{1,17},{17,1},{2,18},{18,2},{3,19},{19,3},{4,20},{20... | collective-permute-start | bytes 1966088 | tf_op jit(solution)/shard_map/ppermute | solution.py:548
  51.4 1.3 collective-permute-start.6
  52.6 2.2 %collective-permute-start.4 = (bf16[80,256]{1,0:T(8,128)(2,1)}, bf16[80,256]{1,0:T(8,128)(2,1)S(1)}, u32[]{:S(2)}, u32[]{:S(2)}) collective-permute-start(bf16[80,256]{1,0:T(8,128)(2,1)} %copy-done.18), channel_id=1, source_target_pairs={{0,2},{1,3},{2,0},{3,1},{4,6},{5,7},{6,4},{7,5},{8,10},{9,11},{10,... | collective-permute-start | bytes 122888 | tf_op jit(solution)/shard_map/ppermute | solution.py:439
  54.9 6.7 %collective-permute-done.7.refs_6_ = bf16[256,1280]{1,0:T(8,128)(2,1)} collective-permute-done((bf16[256,1280]{1,0:T(8,128)(2,1)}, bf16[256,1280]{1,0:T(8,128)(2,1)}, u32[]{:S(2)}, u32[]{:S(2)}) %collective-permute-start.7) | collective-permute-done | bytes 655392 | tf_op jit(solution)/shard_map/ppermute | solution.py:439
  61.6 0.7 collective-permute-done.6.refs_3_
  62.3 0.4 collective-permute-done.4.refs_1_
  62.8 0.8 copy-done.19
  63.5 2.4 %grad_down.1 = (bf16[16,64,640]{2,1,0:T(8,128)(2,1)S(1)}, bf16[16,64,640]{2,1,0:T(8,128)(2,1)S(1)}) custom-call(bf16[256,5120]{1,0:T(8,128)(2,1)S(1)} %copy-done, bf16[80,256]{1,0:T(8,128)(2,1)S(1)} %copy-done.19, bf16[80,256]{1,0:T(8,128)(2,1)S(1)} %collective-permute-done.4.refs_1_, bf16[80,256]{1,0:T(8,128)(2,1)S(1)} %collective-permute-done.5.refs_2_, ...), custom_call_target="tpu_custom_call" | custom-call | bytes 99000 | tf_op jit(solution)/shard_map/grad_down/pallas_call | solution.py:571
  65.9 0.1 collective-permute-start.8
  66.0 0.5 collective-permute-start.11
  66.5 0.1 collective-permute-start.12
  66.6 3.6 %collective-permute-start.9 = (bf16[4,80,256]{2,1,0:T(8,128)(2,1)S(1)}, bf16[4,80,256]{2,1,0:T(8,128)(2,1)S(1)}, u32[]{:S(2)}, u32[]{:S(2)}) collective-permute-start(bf16[4,80,256]{2,1,0:T(8,128)(2,1)S(1)} %get-tuple-element.101), channel_id=1, source_target_pairs={{0,8},{1,9},{2,10},{3,11},{4,12},{5,13},{6,14},{7,15},{8,0},{9,1},... | collective-permute-start | bytes 491528 | tf_op jit(solution)/shard_map/ppermute | solution.py:439
  70.2 0.7 collective-permute-done.12.refs_10_.refs_3_
  70.9 3.1 %hidden.1 = (f32[64,256]{1,0:T(8,128)S(1)}, f32[64,256]{1,0:T(8,128)S(1)}, f32[64,256]{1,0:T(8,128)S(1)}, f32[64,256]{1,0:T(8,128)S(1)}) custom-call(bf16[256,5120]{1,0:T(8,128)(2,1)S(1)} %copy-done, bf16[80,256]{1,0:T(8,128)(2,1)S(1)} %copy-done.20, bf16[80,256]{1,0:T(8,128)(2,1)S(1)} %collective-permute-done.4.refs_1_, ...), custom_call_target="tpu_custom_call" | custom-call | bytes 99000 | tf_op jit(solution)/shard_map/hidden/pallas_call | solution.py:552
  74.1 3.6 %collective-permute-done.9 = bf16[4,80,256]{2,1,0:T(8,128)(2,1)S(1)} collective-permute-done((bf16[4,80,256]{2,1,0:T(8,128)(2,1)S(1)}, bf16[4,80,256]{2,1,0:T(8,128)(2,1)S(1)}, u32[]{:S(2)}, u32[]{:S(2)}) %collective-permute-start.9) | collective-permute-done | bytes 163872 | tf_op jit(solution)/shard_map/ppermute | solution.py:439
  77.7 0.6 collective-permute-start.13
  78.3 0.6 collective-permute-start.14
  78.9 2.3 %collective-permute-start.15 = (f32[64,256]{1,0:T(8,128)S(1)}, f32[64,256]{1,0:T(8,128)S(1)}, u32[]{:S(2)}, u32[]{:S(2)}) collective-permute-start(f32[64,256]{1,0:T(8,128)S(1)} %get-tuple-element.80), channel_id=1, source_target_pairs={{0,6},{1,7},{2,4},{3,5},{4,2},{5,3},{6,0},{7,1},{8,14},{9,15},{10,... | collective-permute-start | bytes 196616 | tf_op jit(solution)/shard_map/ppermute | solution.py:439
  81.2 0.8 pad_maximum_fusion.2
  81.9 1.5 %add_convert_fusion.refs_4_ = bf16[16,64,640]{2,1,0:T(8,128)(2,1)} fusion(bf16[16,64,640]{2,1,0:T(8,128)(2,1)S(1)} %collective-permute-done.8, bf16[16,64,640]{2,1,0:T(8,128)(2,1)S(1)} %get-tuple-element.67), kind=kLoop, calls=%fused_computation | loop fusion | flops 2621440 | bytes 3932160 | tf_op jit(solution)/shard_map/convert_element_type | solution.py:590
  83.5 0.9 collective-permute-done.15.refs_3_
  84.4 0.9 values.1
  85.3 1.0 copy-done.16
  86.3 0.8 copy-done.24
  87.1 5.0 %all-to-all-start.2 = ((bf16[16,64,640]{2,1,0:T(8,128)(2,1)}), bf16[16,64,640]{2,1,0:T(8,128)(2,1)}, u32[]{:S(2)}, u32[]{:S(2)}) async-start(bf16[16,64,640]{2,1,0:T(8,128)(2,1)} %add_convert_fusion.refs_4_), calls=%async_computation.2 | async-start | bytes 2621440 | tf_op jit(solution)/shard_map/all_to_all | solution.py:610
  92.0 0.4 collective-permute-start.16
  92.4 0.2 collective-permute-start.19
  92.6 1.6 %collective-permute-done.16.came_ref = bf16[8,64,512]{2,1,0:T(8,128)(2,1)S(1)} collective-permute-done((bf16[8,64,512]{2,1,0:T(8,128)(2,1)}, bf16[8,64,512]{2,1,0:T(8,128)(2,1)S(1)}, u32[]{:S(2)}, u32[]{:S(2)}) %collective-permute-start.16) | collective-permute-done | bytes 524320 | tf_op jit(solution)/shard_map/ppermute | solution.py:439
  94.2 1.2 copy-done.17
  95.5 0.1 halve.4
  95.5 1.9 %collective-permute-start.17 = (bf16[4,64,512]{2,1,0:T(8,128)(2,1)S(1)}, bf16[4,64,512]{2,1,0:T(8,128)(2,1)S(1)}, u32[]{:S(2)}, u32[]{:S(2)}) collective-permute-start(bf16[4,64,512]{2,1,0:T(8,128)(2,1)S(1)} %get-tuple-element.88), channel_id=1, source_target_pairs={{0,2},{1,3},{2,0},{3,1},{4,6},{5,7},{6,4},{7,5},{8,10},{9,11},{10,... | collective-permute-start | bytes 786440 | tf_op jit(solution)/shard_map/ppermute | solution.py:439
  97.4 1.6 %copy-done.6 = bf16[256,4096]{1,0:T(8,128)(2,1)S(1)} copy-done((bf16[256,4096]{1,0:T(8,128)(2,1)S(1)}, bf16[256,4096]{1,0:T(8,128)(2,1)}, u32[]{:S(2)}) %copy-start.6) | copy-done | bytes 2097176
  99.0 6.9 %second_pass.1 = bf16[256,4096]{1,0:T(8,128)(2,1)} custom-call(s32[2,128]{1,0:T(2,128)S(1)} %copy-done.22, bf16[256,4096]{1,0:T(8,128)(2,1)S(1)} %copy-done.4, bf16[256,512]{1,0:T(8,128)(2,1)S(1)} %copy-done.15, bf16[256,512]{1,0:T(8,128)(2,1)S(1)} %get-tuple-element.90.value_ref, bf16[256,4096]{1,0:T(8,128)(2,1)S(1)} %copy-done.6), custom_call_target="tpu_custom_call" | custom-call | bytes 297000 | tf_op jit(solution)/shard_map/second_pass/pallas_call | solution.py:613
  105.9 6.1 %collective-permute-done.17.came_ref = bf16[4,64,512]{2,1,0:T(8,128)(2,1)S(1)} collective-permute-done((bf16[4,64,512]{2,1,0:T(8,128)(2,1)S(1)}, bf16[4,64,512]{2,1,0:T(8,128)(2,1)S(1)}, u32[]{:S(2)}, u32[]{:S(2)}) %collective-permute-start.17) | collective-permute-done | bytes 262176 | tf_op jit(solution)/shard_map/ppermute | solution.py:439
  112.0 0.1 collective-permute-start.18
  112.3 4.6 %grad_input.1 = bf16[320,4096]{1,0:T(8,128)(2,1)} custom-call(bf16[16,80,256]{2,1,0:T(8,128)(2,1)S(1)} %bitcast.15, bf16[16,32,640]{2,1,0:T(8,128)(2,1)S(1)} %all-to-all-done.1.refs_7_.refs_0_, bf16[16,32,640]{2,1,0:T(8,128)(2,1)S(1)} %copy-done.9, bf16[16,32,640]{2,1,0:T(8,128)(2,1)S(1)} %copy-done.11, bf16[16,32,640]{2,1,0:T(8,128)(2,1)S(1)} %copy-done.13), custom_call_target="tpu_custom_call" | custom-call | bytes 231000 | tf_op jit(solution)/shard_map/grad_input/pallas_call | solution.py:626
  116.8 0.5 collective-permute-done.18.came_ref
  117.4 4.2 %collective-permute-start.20 = (bf16[1,64,512]{2,1,0:T(8,128)(2,1)S(1)}, bf16[1,64,512]{2,1,0:T(8,128)(2,1)S(1)}, u32[]{:S(2)}, u32[]{:S(2)}) collective-permute-start(bf16[1,64,512]{2,1,0:T(8,128)(2,1)S(1)} %get-tuple-element.99), channel_id=1, source_target_pairs={{0,8},{1,9},{2,10},{3,11},{4,12},{5,13},{6,14},{7,15},{8,0},{9,1},... | collective-permute-start | bytes 196616 | tf_op jit(solution)/shard_map/ppermute | solution.py:439
  121.6 2.3 %sum_down.1.outs_0_ = bf16[1,64,5120]{2,1,0:T(8,128)(2,1)} custom-call(bf16[16,64,640]{2,1,0:T(8,128)(2,1)} %all-to-all-done.2.part_ref), custom_call_target="tpu_custom_call" | custom-call | bytes 66000 | tf_op jit(solution)/shard_map/sum_down/pallas_call | solution.py:644
  123.9 3.1 %collective-permute-done.20.came_ref = bf16[1,64,512]{2,1,0:T(8,128)(2,1)S(1)} collective-permute-done((bf16[1,64,512]{2,1,0:T(8,128)(2,1)S(1)}, bf16[1,64,512]{2,1,0:T(8,128)(2,1)S(1)}, u32[]{:S(2)}, u32[]{:S(2)}) %collective-permute-start.20) | collective-permute-done | bytes 65568 | tf_op jit(solution)/shard_map/ppermute | solution.py:439
  127.0 1.1 copy-done.7
  128.1 0.6 halve.7
  (61 shorter events, 0.3 us)
Async XLA Ops:
  0.6 8.0 %copy-start.26 = (bf16[1,64,512]{2,1,0:T(8,128)(2,1)S(1)}, bf16[1,64,512]{2,1,0:T(8,128)(2,1)}, u32[]{:S(2)}) copy-start(bf16[1,64,512]{2,1,0:T(8,128)(2,1)} %param.16) | copy-start | bytes 196612
  0.6 8.0 %collective-permute-start = (bf16[1,64,512]{2,1,0:T(8,128)(2,1)}, bf16[1,64,512]{2,1,0:T(8,128)(2,1)S(1)}, u32[]{:S(2)}, u32[]{:S(2)}) collective-permute-start(bf16[1,64,512]{2,1,0:T(8,128)(2,1)} %param.16), channel_id=1, source_target_pairs={{0,8},{1,9},{2,10},{3,11},{4,12},{5,13},{6,14},{7,15},{8,0},{9,1},... | collective-permute-start | bytes 196616 | tf_op jit(solution)/shard_map/ppermute | solution.py:439
  7.5 20.0 %copy-start.3 = (bf16[256,4096]{1,0:T(8,128)(2,1)S(1)}, bf16[256,4096]{1,0:T(8,128)(2,1)}, u32[]{:S(2)}) copy-start(bf16[256,4096]{1,0:T(8,128)(2,1)} %query_ref.3) | copy-start | bytes 6291460
  7.5 20.0 %copy-start.14 = (bf16[256,512]{1,0:T(8,128)(2,1)S(1)}, bf16[256,512]{1,0:T(8,128)(2,1)}, u32[]{:S(2)}) copy-start(bf16[256,512]{1,0:T(8,128)(2,1)} %key_ref.3) | copy-start | bytes 786436
  7.6 20.0 %copy-start.22 = (s32[2,128]{1,0:T(2,128)S(1)}, s32[2,128]{1,0:T(2,128)}, u32[]{:S(2)}) copy-start(s32[2,128]{1,0:T(2,128)} %ids_ref.3) | copy-start | bytes 3076
  9.5 13.6 %all-to-all-start = ((bf16[4,2,64,512]{3,2,1,0:T(8,128)(2,1)}), bf16[4,2,64,512]{3,2,1,0:T(8,128)(2,1)}, u32[]{:S(2)}, u32[]{:S(2)}) async-start(bf16[4,2,64,512]{3,2,1,0:T(8,128)(2,1)} %broadcast_in_dim.3), calls=%async_computation | async-start | bytes 1048576 | tf_op jit(solution)/shard_map/all_to_all | solution.py:518
  13.6 24.1 %collective-permute-start.1 = (bf16[256,1280]{1,0:T(8,128)(2,1)}, bf16[256,1280]{1,0:T(8,128)(2,1)}, u32[]{:S(2)}, u32[]{:S(2)}) collective-permute-start(bf16[256,1280]{1,0:T(8,128)(2,1)} %get-tuple-element.58), channel_id=1, source_target_pairs={{0,2},{1,3},{2,0},{3,1},{4,6},{5,7},{6,4},{7,5},{8,10},{9,11},{10,... | collective-permute-start | bytes 1966088 | tf_op jit(solution)/shard_map/ppermute | solution.py:439
  15.6 26.3 %collective-permute-start.2 = (bf16[256,1280]{1,0:T(8,128)(2,1)}, bf16[256,1280]{1,0:T(8,128)(2,1)}, u32[]{:S(2)}, u32[]{:S(2)}) collective-permute-start(bf16[256,1280]{1,0:T(8,128)(2,1)} %get-tuple-element.59), channel_id=1, source_target_pairs={{0,4},{1,5},{2,6},{3,7},{4,0},{5,1},{6,2},{7,3},{8,12},{9,13},{10,... | collective-permute-start | bytes 1966088 | tf_op jit(solution)/shard_map/ppermute | solution.py:439
  23.1 26.8 %all-to-all-start.1 = ((bf16[16,32,640]{2,1,0:T(8,128)(2,1)}), bf16[16,32,640]{2,1,0:T(8,128)(2,1)S(1)}, u32[]{:S(2)}, u32[]{:S(2)}) async-start(bf16[16,32,640]{2,1,0:T(8,128)(2,1)} %get-tuple-element.57), calls=%async_computation.1 | async-start | bytes 1310720 | tf_op jit(solution)/shard_map/all_to_all | solution.py:523
  27.5 1.6 %copy-start.5 = (bf16[256,4096]{1,0:T(8,128)(2,1)S(1)}, bf16[256,4096]{1,0:T(8,128)(2,1)}, u32[]{:S(2)}) copy-start(bf16[256,4096]{1,0:T(8,128)(2,1)} %grad_ref.3) | copy-start | bytes 6291460
  33.8 29.0 %copy-start = (bf16[256,5120]{1,0:T(8,128)(2,1)S(1)}, bf16[256,5120]{1,0:T(8,128)(2,1)}, u32[]{:S(2)}) copy-start(bf16[256,5120]{1,0:T(8,128)(2,1)} %x_ref.5) | copy-start | bytes 7864324
  41.9 2.3 %collective-permute-start.3 = (bf16[4,2,64,512]{3,2,1,0:T(8,128)(2,1)}, bf16[4,2,64,512]{3,2,1,0:T(8,128)(2,1)}, u32[]{:S(2)}, u32[]{:S(2)}) collective-permute-start(bf16[4,2,64,512]{3,2,1,0:T(8,128)(2,1)} %all-to-all-done), channel_id=1, source_target_pairs={{0,1},{1,0},{2,3},{3,2},{4,5},{5,4},{6,7},{7,6},{8,9},{9,8},{10,11... | collective-permute-start | bytes 1572872 | tf_op jit(solution)/shard_map/ppermute | solution.py:439
  41.9 19.7 %collective-permute-start.7 = (bf16[256,1280]{1,0:T(8,128)(2,1)}, bf16[256,1280]{1,0:T(8,128)(2,1)}, u32[]{:S(2)}, u32[]{:S(2)}) collective-permute-start(bf16[256,1280]{1,0:T(8,128)(2,1)} %get-tuple-element.66), channel_id=1, source_target_pairs={{0,6},{1,7},{2,4},{3,5},{4,2},{5,3},{6,0},{7,1},{8,14},{9,15},{10,... | collective-permute-start | bytes 1966088 | tf_op jit(solution)/shard_map/ppermute | solution.py:439
  45.4 0.7 copy-start.23
  47.0 1.0 copy-start.1
  48.0 0.6 copy-start.18
  49.9 16.6 %collective-permute-start.10 = (bf16[16,32,640]{2,1,0:T(8,128)(2,1)S(1)}, bf16[16,32,640]{2,1,0:T(8,128)(2,1)S(1)}, u32[]{:S(2)}, u32[]{:S(2)}) collective-permute-start(bf16[16,32,640]{2,1,0:T(8,128)(2,1)S(1)} %all-to-all-done.1.refs_7_.refs_0_), channel_id=1, source_target_pairs={{0,16},{16,0},{1,17},{17,1},{2,18},{18,2},{3,19},{19,3},{4,20},{20... | collective-permute-start | bytes 1966088 | tf_op jit(solution)/shard_map/ppermute | solution.py:548
  51.4 10.9 %collective-permute-start.6 = (bf16[80,256]{1,0:T(8,128)(2,1)}, bf16[80,256]{1,0:T(8,128)(2,1)S(1)}, u32[]{:S(2)}, u32[]{:S(2)}) collective-permute-start(bf16[80,256]{1,0:T(8,128)(2,1)} %copy-done.18), channel_id=1, source_target_pairs={{0,6},{1,7},{2,4},{3,5},{4,2},{5,3},{6,0},{7,1},{8,14},{9,15},{10,... | collective-permute-start | bytes 122888 | tf_op jit(solution)/shard_map/ppermute | solution.py:439
  52.6 9.7 %collective-permute-start.5 = (bf16[80,256]{1,0:T(8,128)(2,1)}, bf16[80,256]{1,0:T(8,128)(2,1)S(1)}, u32[]{:S(2)}, u32[]{:S(2)}) collective-permute-start(bf16[80,256]{1,0:T(8,128)(2,1)} %copy-done.18), channel_id=1, source_target_pairs={{0,4},{1,5},{2,6},{3,7},{4,0},{5,1},{6,2},{7,3},{8,12},{9,13},{10,... | collective-permute-start | bytes 122888 | tf_op jit(solution)/shard_map/ppermute | solution.py:439
  52.6 10.1 %collective-permute-start.4 = (bf16[80,256]{1,0:T(8,128)(2,1)}, bf16[80,256]{1,0:T(8,128)(2,1)S(1)}, u32[]{:S(2)}, u32[]{:S(2)}) collective-permute-start(bf16[80,256]{1,0:T(8,128)(2,1)} %copy-done.18), channel_id=1, source_target_pairs={{0,2},{1,3},{2,0},{3,1},{4,6},{5,7},{6,4},{7,5},{8,10},{9,11},{10,... | collective-permute-start | bytes 122888 | tf_op jit(solution)/shard_map/ppermute | solution.py:439
  62.8 0.8 copy-start.19
  63.5 7.4 %copy-start.20 = (bf16[80,256]{1,0:T(8,128)(2,1)S(1)}, bf16[80,256]{1,0:T(8,128)(2,1)}, u32[]{:S(2)}) copy-start(bf16[80,256]{1,0:T(8,128)(2,1)} %copy-done.18) | copy-start | bytes 122884
  65.9 16.0 %collective-permute-start.8 = (bf16[16,64,640]{2,1,0:T(8,128)(2,1)S(1)}, bf16[16,64,640]{2,1,0:T(8,128)(2,1)S(1)}, u32[]{:S(2)}, u32[]{:S(2)}) collective-permute-start(bf16[16,64,640]{2,1,0:T(8,128)(2,1)S(1)} %get-tuple-element.68), channel_id=1, source_target_pairs={{0,1},{1,0},{2,3},{3,2},{4,5},{5,4},{6,7},{7,6},{8,9},{9,8},{10,11... | collective-permute-start | bytes 3932168 | tf_op jit(solution)/shard_map/ppermute | solution.py:439
  66.0 4.2 %collective-permute-start.11 = (bf16[16,32,640]{2,1,0:T(8,128)(2,1)S(1)}, bf16[16,32,640]{2,1,0:T(8,128)(2,1)S(1)}, u32[]{:S(2)}, u32[]{:S(2)}) collective-permute-start(bf16[16,32,640]{2,1,0:T(8,128)(2,1)S(1)} %all-to-all-done.1.refs_7_.refs_0_), channel_id=1, source_target_pairs={{0,1},{1,0},{2,3},{3,2},{4,5},{5,4},{6,7},{7,6},{8,9},{9,8},{10,11... | collective-permute-start | bytes 1966088 | tf_op jit(solution)/shard_map/ppermute | solution.py:439
  66.5 7.5 %copy-start.8 = (bf16[16,32,640]{2,1,0:T(8,128)(2,1)}, bf16[16,32,640]{2,1,0:T(8,128)(2,1)S(1)}, u32[]{:S(2)}) copy-start(bf16[16,32,640]{2,1,0:T(8,128)(2,1)S(1)} %collective-permute-done.10.refs_8_.refs_1_) | copy-start | bytes 1966084
  66.5 4.4 %collective-permute-start.12 = (bf16[16,32,640]{2,1,0:T(8,128)(2,1)S(1)}, bf16[16,32,640]{2,1,0:T(8,128)(2,1)S(1)}, u32[]{:S(2)}, u32[]{:S(2)}) collective-permute-start(bf16[16,32,640]{2,1,0:T(8,128)(2,1)S(1)} %collective-permute-done.10.refs_8_.refs_1_), channel_id=1, source_target_pairs={{0,1},{1,0},{2,3},{3,2},{4,5},{5,4},{6,7},{7,6},{8,9},{9,8},{10,11... | collective-permute-start | bytes 1966088 | tf_op jit(solution)/shard_map/ppermute | solution.py:439
  66.6 11.1 %collective-permute-start.9 = (bf16[4,80,256]{2,1,0:T(8,128)(2,1)S(1)}, bf16[4,80,256]{2,1,0:T(8,128)(2,1)S(1)}, u32[]{:S(2)}, u32[]{:S(2)}) collective-permute-start(bf16[4,80,256]{2,1,0:T(8,128)(2,1)S(1)} %get-tuple-element.101), channel_id=1, source_target_pairs={{0,8},{1,9},{2,10},{3,11},{4,12},{5,13},{6,14},{7,15},{8,0},{9,1},... | collective-permute-start | bytes 491528 | tf_op jit(solution)/shard_map/ppermute | solution.py:439
  70.2 3.9 %copy-start.10 = (bf16[16,32,640]{2,1,0:T(8,128)(2,1)}, bf16[16,32,640]{2,1,0:T(8,128)(2,1)S(1)}, u32[]{:S(2)}) copy-start(bf16[16,32,640]{2,1,0:T(8,128)(2,1)S(1)} %collective-permute-done.11.refs_9_.refs_2_) | copy-start | bytes 1966084
  70.9 3.2 %copy-start.12 = (bf16[16,32,640]{2,1,0:T(8,128)(2,1)}, bf16[16,32,640]{2,1,0:T(8,128)(2,1)S(1)}, u32[]{:S(2)}) copy-start(bf16[16,32,640]{2,1,0:T(8,128)(2,1)S(1)} %collective-permute-done.12.refs_10_.refs_3_) | copy-start | bytes 1966084
  77.7 5.8 %collective-permute-start.13 = (f32[64,256]{1,0:T(8,128)S(1)}, f32[64,256]{1,0:T(8,128)S(1)}, u32[]{:S(2)}, u32[]{:S(2)}) collective-permute-start(f32[64,256]{1,0:T(8,128)S(1)} %get-tuple-element.78), channel_id=1, source_target_pairs={{0,2},{1,3},{2,0},{3,1},{4,6},{5,7},{6,4},{7,5},{8,10},{9,11},{10,... | collective-permute-start | bytes 196616 | tf_op jit(solution)/shard_map/ppermute | solution.py:439
  78.3 5.2 %collective-permute-start.14 = (f32[64,256]{1,0:T(8,128)S(1)}, f32[64,256]{1,0:T(8,128)S(1)}, u32[]{:S(2)}, u32[]{:S(2)}) collective-permute-start(f32[64,256]{1,0:T(8,128)S(1)} %get-tuple-element.79), channel_id=1, source_target_pairs={{0,4},{1,5},{2,6},{3,7},{4,0},{5,1},{6,2},{7,3},{8,12},{9,13},{10,... | collective-permute-start | bytes 196616 | tf_op jit(solution)/shard_map/ppermute | solution.py:439
  78.9 5.5 %collective-permute-start.15 = (f32[64,256]{1,0:T(8,128)S(1)}, f32[64,256]{1,0:T(8,128)S(1)}, u32[]{:S(2)}, u32[]{:S(2)}) collective-permute-start(f32[64,256]{1,0:T(8,128)S(1)} %get-tuple-element.80), channel_id=1, source_target_pairs={{0,6},{1,7},{2,4},{3,5},{4,2},{5,3},{6,0},{7,1},{8,14},{9,15},{10,... | collective-permute-start | bytes 196616 | tf_op jit(solution)/shard_map/ppermute | solution.py:439
  81.9 2.4 %copy-start.2 = (bf16[2,4,2,64,512]{4,3,2,1,0:T(8,128)(2,1)S(1)}, bf16[2,4,2,64,512]{4,3,2,1,0:T(8,128)(2,1)}, u32[]{:S(2)}) copy-start(bf16[2,4,2,64,512]{4,3,2,1,0:T(8,128)(2,1)} %copy-done.1) | copy-start | bytes 3145732
  81.9 2.4 %copy-start.21 = (bf16[256,512]{1,0:T(8,128)(2,1)S(1)}, bf16[256,512]{1,0:T(8,128)(2,1)}, u32[]{:S(2)}) copy-start(bf16[256,512]{1,0:T(8,128)(2,1)} %base_ref.1) | copy-start | bytes 786436
  85.3 1.0 copy-start.16
  86.3 0.8 copy-start.24
  87.1 10.3 %copy-start.4 = (bf16[256,4096]{1,0:T(8,128)(2,1)S(1)}, bf16[256,4096]{1,0:T(8,128)(2,1)}, u32[]{:S(2)}) copy-start(bf16[256,4096]{1,0:T(8,128)(2,1)} %query_ref.3) | copy-start | bytes 6291460
  87.1 10.3 %copy-start.15 = (bf16[256,512]{1,0:T(8,128)(2,1)S(1)}, bf16[256,512]{1,0:T(8,128)(2,1)}, u32[]{:S(2)}) copy-start(bf16[256,512]{1,0:T(8,128)(2,1)} %key_ref.3) | copy-start | bytes 786436
  87.1 34.5 %all-to-all-start.2 = ((bf16[16,64,640]{2,1,0:T(8,128)(2,1)}), bf16[16,64,640]{2,1,0:T(8,128)(2,1)}, u32[]{:S(2)}, u32[]{:S(2)}) async-start(bf16[16,64,640]{2,1,0:T(8,128)(2,1)} %add_convert_fusion.refs_4_), calls=%async_computation.2 | async-start | bytes 2621440 | tf_op jit(solution)/shard_map/all_to_all | solution.py:610
  92.0 2.2 %collective-permute-start.16 = (bf16[8,64,512]{2,1,0:T(8,128)(2,1)}, bf16[8,64,512]{2,1,0:T(8,128)(2,1)S(1)}, u32[]{:S(2)}, u32[]{:S(2)}) collective-permute-start(bf16[8,64,512]{2,1,0:T(8,128)(2,1)} %copy-done.24), channel_id=1, source_target_pairs={{0,1},{1,0},{2,3},{3,2},{4,5},{5,4},{6,7},{7,6},{8,9},{9,8},{10,11... | collective-permute-start | bytes 1572872 | tf_op jit(solution)/shard_map/ppermute | solution.py:439
  92.4 19.7 %collective-permute-start.19 = (bf16[2,4,80,256]{3,2,1,0:T(8,128)(2,1)}, bf16[2,4,80,256]{3,2,1,0:T(8,128)(2,1)S(1)}, u32[]{:S(2)}, u32[]{:S(2)}) collective-permute-start(bf16[2,4,80,256]{3,2,1,0:T(8,128)(2,1)} %pad_maximum_fusion.2), channel_id=1, source_target_pairs={{0,1},{1,0},{2,3},{3,2},{4,5},{5,4},{6,7},{7,6},{8,9},{9,8},{10,11... | collective-permute-start | bytes 983048 | tf_op jit(solution)/shard_map/ppermute | solution.py:439
  94.2 1.2 copy-start.17
  95.5 16.4 %collective-permute-start.17 = (bf16[4,64,512]{2,1,0:T(8,128)(2,1)S(1)}, bf16[4,64,512]{2,1,0:T(8,128)(2,1)S(1)}, u32[]{:S(2)}, u32[]{:S(2)}) collective-permute-start(bf16[4,64,512]{2,1,0:T(8,128)(2,1)S(1)} %get-tuple-element.88), channel_id=1, source_target_pairs={{0,2},{1,3},{2,0},{3,1},{4,6},{5,7},{6,4},{7,5},{8,10},{9,11},{10,... | collective-permute-start | bytes 786440 | tf_op jit(solution)/shard_map/ppermute | solution.py:439
  97.4 1.6 %copy-start.6 = (bf16[256,4096]{1,0:T(8,128)(2,1)S(1)}, bf16[256,4096]{1,0:T(8,128)(2,1)}, u32[]{:S(2)}) copy-start(bf16[256,4096]{1,0:T(8,128)(2,1)} %grad_ref.3) | copy-start | bytes 6291460
  99.0 13.1 %copy-start.25 = (bf16[2,4,80,256]{3,2,1,0:T(8,128)(2,1)S(1)}, bf16[2,4,80,256]{3,2,1,0:T(8,128)(2,1)}, u32[]{:S(2)}) copy-start(bf16[2,4,80,256]{3,2,1,0:T(8,128)(2,1)} %pad_maximum_fusion.2) | copy-start | bytes 983044
  105.9 6.3 %copy-start.9 = (bf16[16,32,640]{2,1,0:T(8,128)(2,1)S(1)}, bf16[16,32,640]{2,1,0:T(8,128)(2,1)}, u32[]{:S(2)}) copy-start(bf16[16,32,640]{2,1,0:T(8,128)(2,1)} %copy-done.8) | copy-start | bytes 1966084
  105.9 6.4 %copy-start.11 = (bf16[16,32,640]{2,1,0:T(8,128)(2,1)S(1)}, bf16[16,32,640]{2,1,0:T(8,128)(2,1)}, u32[]{:S(2)}) copy-start(bf16[16,32,640]{2,1,0:T(8,128)(2,1)} %copy-done.10) | copy-start | bytes 1966084
  105.9 6.4 %copy-start.13 = (bf16[16,32,640]{2,1,0:T(8,128)(2,1)S(1)}, bf16[16,32,640]{2,1,0:T(8,128)(2,1)}, u32[]{:S(2)}) copy-start(bf16[16,32,640]{2,1,0:T(8,128)(2,1)} %copy-done.12) | copy-start | bytes 1966084
  112.0 5.4 %collective-permute-start.18 = (bf16[2,64,512]{2,1,0:T(8,128)(2,1)S(1)}, bf16[2,64,512]{2,1,0:T(8,128)(2,1)S(1)}, u32[]{:S(2)}, u32[]{:S(2)}) collective-permute-start(bf16[2,64,512]{2,1,0:T(8,128)(2,1)S(1)} %get-tuple-element.93), channel_id=1, source_target_pairs={{0,4},{1,5},{2,6},{3,7},{4,0},{5,1},{6,2},{7,3},{8,12},{9,13},{10,... | collective-permute-start | bytes 393224 | tf_op jit(solution)/shard_map/ppermute | solution.py:439
  117.4 9.6 %collective-permute-start.20 = (bf16[1,64,512]{2,1,0:T(8,128)(2,1)S(1)}, bf16[1,64,512]{2,1,0:T(8,128)(2,1)S(1)}, u32[]{:S(2)}, u32[]{:S(2)}) collective-permute-start(bf16[1,64,512]{2,1,0:T(8,128)(2,1)S(1)} %get-tuple-element.99), channel_id=1, source_target_pairs={{0,8},{1,9},{2,10},{3,11},{4,12},{5,13},{6,14},{7,15},{8,0},{9,1},... | collective-permute-start | bytes 196616 | tf_op jit(solution)/shard_map/ppermute | solution.py:439
  127.0 1.1 copy-start.7

commit v3 on v2

--- a/solution.py
+++ b/solution.py
@@ -340,25 +340,22 @@
     send_ref[...] = total[:, :, columns(1 - core, span)].astype(jnp.bfloat16)
 
 
-def sum_kernel(part_ref, out_ref):
+def sum_kernel(part_ref, out_ref, token_ref):
     span = part_ref.shape[2]
+    token_ref[...] = jnp.zeros_like(token_ref)
     for part in range(2 * CHIPS):
         one, two = [i for i in range(SPAN) if eighth_of(i) == part]
         out = part_ref[one].astype(jnp.float32) + part_ref[two].astype(jnp.float32)
         out_ref[0, :, pl.ds(part * span, span)] = out.astype(jnp.bfloat16)
 
 
-def values_kernel(slot_ref, up_slot_ref, base_ref, dval_ref, up_ref, *refs):
-    hidden_refs, (val_ref, keep_ref, send_ref) = refs[:CHIPS], refs[CHIPS + 1 :]
-    rank = keep_ref.shape[1]
+def values_kernel(up_slot_ref, base_ref, dval_ref, up_ref, *refs):
+    hidden_refs, (val_ref, term_ref) = refs[:CHIPS], refs[CHIPS + 1 :]
     block = base_ref.shape[0] // 2
     hidden = hidden_refs[0][...]
     for ref in hidden_refs[1:]:
         hidden = hidden + ref[...]
     hidden = hidden.astype(jnp.bfloat16)
-    keep_ref[...] = jnp.zeros_like(keep_ref)
-    send_ref[...] = jnp.zeros_like(send_ref)
-    terms = []
     for k in range(2):
         rows = pl.ds(k * block, block)
         part = hidden[:, k * block : (k + 1) * block]
@@ -371,17 +368,22 @@
         val_ref[rows, :] = (base_ref[rows, :].astype(jnp.float32) + adapter_scale * added).astype(
             jnp.bfloat16
         )
-        terms.append(
-            adapter_scale * jnp.dot(part, dval_ref[rows, :], preferred_element_type=jnp.float32)
-        )
-    same = (slot_ref[0] == slot_ref[1]).astype(jnp.float32)
-    terms[1] = terms[1] + same * terms[0]
-    for k in range(2):
+        term = jnp.dot(part, dval_ref[rows, :], preferred_element_type=jnp.float32)
+        term_ref[k] = (adapter_scale * term).astype(jnp.bfloat16)
+
+
+def place_kernel(slot_ref, own_ref, came_ref, keep_ref, send_ref):
+    keep_ref[...] = jnp.zeros_like(keep_ref)
+    send_ref[...] = jnp.zeros_like(send_ref)
+    for k in range(4):
+        slot = slot_ref[k]
+        term = (own_ref, came_ref)[k // 2][k % 2].astype(jnp.float32)
         for side, ref in enumerate((keep_ref, send_ref)):
 
-            @pl.when((slot_ref[k] & 1) == side)
+            @pl.when((slot & 3) == 2 * side)
             def _():
-                ref[slot_ref[k] >> 1] = terms[k].astype(ref.dtype)
+                place = ref.at[slot >> 2]
+                place[...] = (place[...].astype(jnp.float32) + term).astype(ref.dtype)
 
 
 def halve_kernel(kept_ref, came_ref, *outs, extra=0):
@@ -524,6 +526,7 @@
     near[0], near[1], near_up, dvalues = together(near[0], near[1], near_up, dvalues)
     all_up = jnp.stack([near_up, swap(near_up, 1)]).reshape((SPAN,) + adapt_up.shape[1:])
     me = lax.axis_index("dp")
+    chip_slots = jnp.concatenate([own_stores, swap(own_stores, 1)]) ^ me
     slots = own_stores ^ me
     up_slots = 8 * (slots & 1) + (own_stores & 6) + (slots >> 3)
 
@@ -585,26 +588,23 @@
         name="grad_down",
     )(x_rows, *near_grad, *near)
     all_grad = jnp.stack(near_grad)
-    far_grad, own_part = together(swap(all_grad, 8), own_part)
-    all_grad = jnp.stack([all_grad, far_grad])
+    far_grad, *hidden_parts = together(swap(all_grad, 8), *hidden_parts)
     down_parts = (down_keep.astype(f32) + swap(down_send, 1).astype(f32)).astype(bf16)
-    value_rows, kept, sent = pl.pallas_call(
+    value_rows, terms = pl.pallas_call(
         values_kernel,
-        in_specs=[smem_spec] * 2 + [vmem_spec] * (3 + CHIPS) + [any_spec],
-        out_specs=[vmem_spec] * 3,
+        in_specs=[smem_spec] + [vmem_spec] * (3 + CHIPS) + [any_spec],
+        out_specs=[vmem_spec] * 2,
         out_shape=[
             shape((tok_rows, value_width), bf16),
-            shape((SPAN // 2, rank, value_width), f32),
-            shape((SPAN // 2, rank, value_width), bf16),
+            shape((blocks, rank, value_width), bf16),
         ],
         compiler_params=params,
         cost_estimate=cost(1),
         name="values",
-    )(slots, up_slots, values_base, dvalues, all_up, own_part, *hidden_parts, down_parts)
-
-    down_parts, value_rows, kept, sent, all_grad = together(
-        down_parts, value_rows, kept, sent, all_grad
-    )
+    )(up_slots, values_base, dvalues, all_up, own_part, *hidden_parts, down_parts)
+
+    down_parts, terms, far_grad = together(down_parts, terms, far_grad)
+    all_grad = jnp.stack([all_grad, far_grad])
     all_grad = jnp.stack([all_grad, swap(all_grad, 1)], axis=2)
     all_grad = all_grad.reshape((SPAN,) + hidden_gradient.shape)
     down_parts = lax.all_to_all(down_parts, "dp", split_axis=0, concat_axis=0, tiled=True)
@@ -641,22 +641,34 @@
         name="grad_input",
     )(all_grad, *downs)
 
-    grad_down = pl.pallas_call(
+    grad_down, token = pl.pallas_call(
         sum_kernel,
         in_specs=[vmem_spec],
-        out_specs=vmem_spec,
-        out_shape=shape((1, rank, width), bf16),
+        out_specs=[vmem_spec] * 2,
+        out_shape=[shape((1, rank, width), bf16), shape((8, 128), f32)],
         compiler_params=params,
         cost_estimate=cost(2),
         name="sum_down",
     )(down_parts)
-    for mask in (1, 2, 4, 8):
+    kept, sent = pl.pallas_call(
+        place_kernel,
+        in_specs=[smem_spec] + [vmem_spec] * 2,
+        out_specs=[vmem_spec] * 2,
+        out_shape=[
+            shape((SPAN // 4, rank, value_width), f32),
+            shape((SPAN // 4, rank, value_width), bf16),
+        ],
+        compiler_params=params,
+        cost_estimate=cost(1),
+        name="place",
+    )(chip_slots, terms, swap(terms, 1))
+    for mask in (2, 4, 8):
         if mask == 4:
             sent, grad_query = together(sent, grad_query)
         if mask == 8:
             sent, grad_input_t = together(sent, grad_input_t)
         came = swap(sent, mask)
-        last = (grad_down,) if mask == 8 else ()
+        last = (token,) if mask == 8 else ()
         count = max(came.shape[0] // 2, 1)
         outs = [shape((count,) + came.shape[1:], bf16)]
         if mask < 8:

time: 130 us -> 126 us (0.969)
  local copies, waits for them, and re-layouts: 11.2 us -> 7.99 us
  waiting for transfers between devices: 41.3 us -> 38.3 us
  starting transfers between devices: 40.4 us -> 41.8 us
    ppermute x20 -> x21, waiting for transfers between devices: 33.9 us -> 29.5 us  [swap(): return lax.ppermute(value, 'dp', [(i, i ^ mask) for i in range(SPAN)])]
    unnamed x54 -> x48, local copies, waits for them, and re-layouts: 10.3 us -> 7.11 us
    ppermute x20 -> x21, starting transfers between devices: 25.5 us -> 27 us  [swap(): return lax.ppermute(value, 'dp', [(i, i ^ mask) for i in range(SPAN)])]
    ppermute x1, waiting for transfers between devices: 0.01 us -> 1.47 us  [local_clustered(): down_other = lax.ppermute(down_own, 'groups', [(0, 1), (1, 0)])]
    pallas_call x2 -> x3, Pallas kernels: 3.24 us -> 3.82 us  [the longest x1 2.31 us: local_clustered(): pl.pallas_call(sum_kernel, in_specs=[vmem_spec], out_specs=[vmem_spec] *...]
  transfers between devices with their start and end apart: 24 -> 25, of which waited for: 16 -> 15; matrix products, arithmetic and copies ran while one was open for 3% -> 4% of each run, Pallas kernels for 22% -> 24%
where the time goes in v3:
time: 126 us
  starting transfers between devices  41.8 us (33%)
  waiting for transfers between devices  38.3 us (30%)
  Pallas kernels  31.1 us (25%)
  local copies, waits for them, and re-layouts  7.99 us (6%)
  other arithmetic  5.42 us (4%)
    ppermute x21, waiting for transfers between devices, swap(): return lax.ppermute(value, 'dp', [(i, i ^ mask) for i in range(SPAN)])  29.5 us
    ppermute x21, starting transfers between devices, swap(): return lax.ppermute(value, 'dp', [(i, i ^ mask) for i in range(SPAN)])  27 us
    unnamed x48, local copies, waits for them, and re-layouts  7.11 us
    pallas_call x1, Pallas kernels, local_clustered(): pl.pallas_call(second_kernel, grid=(blocks, heads), in_specs=[vmem_spec,...  6.87 us
    all_to_all x1, waiting for transfers between devices, local_clustered(): lax.all_to_all(jnp.broadcast_to(up_pair, (CHIPS,) + up_pair.shape), 'dp',...  6.06 us
    all_to_all x1, starting transfers between devices, local_clustered(): lax.all_to_all(down_parts, 'dp', split_axis=0, concat_axis=0, tiled=True)  4.74 us
    pallas_call x1, Pallas kernels, local_clustered(): pl.pallas_call(first_kernel, grid=(blocks, heads), in_specs=[vmem_spec, w...  4.68 us
    pallas_call x1, Pallas kernels, local_clustered(): pl.pallas_call(grad_input_kernel, in_specs=[vmem_spec] + [any_spec] * 4,...  4.57 us
  transfers between devices with their start and end apart: 25, of which 15 were waited for; matrix products, arithmetic and copies ran while one was open for 4% of the time, Pallas kernels for 24%

profile of v3, /device:TPU:0, one launch (start us, length us, event | category | flops | bytes accessed | tf_op | source)
XLA Modules:
  0.0 125.6 jit_solution(17494475236468163502)
XLA Ops:
  0.6 4.1 %collective-permute-start.1 = (bf16[1,64,512]{2,1,0:T(8,128)(2,1)}, bf16[1,64,512]{2,1,0:T(8,128)(2,1)S(1)}, u32[]{:S(2)}, u32[]{:S(2)}) collective-permute-start(bf16[1,64,512]{2,1,0:T(8,128)(2,1)} %param.16), channel_id=1, source_target_pairs={{0,8},{1,9},{2,10},{3,11},{4,12},{5,13},{6,14},{7,15},{8,0},{9,1},... | collective-permute-start | bytes 196616 | tf_op jit(solution)/shard_map/ppermute | solution.py:441
  4.7 2.8 %pack.1 = (bf16[16,32,640]{2,1,0:T(8,128)(2,1)}, bf16[256,1280]{1,0:T(8,128)(2,1)}, bf16[256,1280]{1,0:T(8,128)(2,1)}, bf16[256,1280]{1,0:T(8,128)(2,1)}) custom-call(bf16[256,5120]{1,0:T(8,128)(2,1)} %x_ref.5, bf16[1,64,5120]{2,1,0:T(8,128)(2,1)} %down_ref.1), custom_call_target="tpu_custom_call" | custom-call | bytes 82500 | tf_op jit(solution)/shard_map/pack/pallas_call | solution.py:482
  7.6 0.0 copy-start.19
  7.6 1.0 collective-permute-done.1
  8.6 0.8 broadcast_in_dim.3
  9.5 4.1 %all-to-all-start = ((bf16[4,2,64,512]{3,2,1,0:T(8,128)(2,1)}), bf16[4,2,64,512]{3,2,1,0:T(8,128)(2,1)}, u32[]{:S(2)}, u32[]{:S(2)}) async-start(bf16[4,2,64,512]{3,2,1,0:T(8,128)(2,1)} %broadcast_in_dim.3), calls=%async_computation | async-start | bytes 1048576 | tf_op jit(solution)/shard_map/all_to_all | solution.py:520
  13.6 2.0 %collective-permute-start.2 = (bf16[256,1280]{1,0:T(8,128)(2,1)}, bf16[256,1280]{1,0:T(8,128)(2,1)}, u32[]{:S(2)}, u32[]{:S(2)}) collective-permute-start(bf16[256,1280]{1,0:T(8,128)(2,1)} %get-tuple-element.59), channel_id=1, source_target_pairs={{0,2},{1,3},{2,0},{3,1},{4,6},{5,7},{6,4},{7,5},{8,10},{9,11},{10,... | collective-permute-start | bytes 1966088 | tf_op jit(solution)/shard_map/ppermute | solution.py:441
  15.6 1.5 %collective-permute-start.3 = (bf16[256,1280]{1,0:T(8,128)(2,1)}, bf16[256,1280]{1,0:T(8,128)(2,1)}, u32[]{:S(2)}, u32[]{:S(2)}) collective-permute-start(bf16[256,1280]{1,0:T(8,128)(2,1)} %get-tuple-element.60), channel_id=1, source_target_pairs={{0,4},{1,5},{2,6},{3,7},{4,0},{5,1},{6,2},{7,3},{8,12},{9,13},{10,... | collective-permute-start | bytes 1966088 | tf_op jit(solution)/shard_map/ppermute | solution.py:441
  17.0 6.1 %all-to-all-done = bf16[4,2,64,512]{3,2,1,0:T(8,128)(2,1)} async-done(((bf16[4,2,64,512]{3,2,1,0:T(8,128)(2,1)}), bf16[4,2,64,512]{3,2,1,0:T(8,128)(2,1)}, u32[]{:S(2)}, u32[]{:S(2)}) %all-to-all-start) | async-done | bytes 524320 | tf_op jit(solution)/shard_map/all_to_all | solution.py:520
  23.1 4.4 %all-to-all-start.1 = ((bf16[16,32,640]{2,1,0:T(8,128)(2,1)}), bf16[16,32,640]{2,1,0:T(8,128)(2,1)S(1)}, u32[]{:S(2)}, u32[]{:S(2)}) async-start(bf16[16,32,640]{2,1,0:T(8,128)(2,1)} %get-tuple-element.58), calls=%async_computation.1 | async-start | bytes 1310720 | tf_op jit(solution)/shard_map/all_to_all | solution.py:525
  27.5 1.6 %copy-done.5 = bf16[256,4096]{1,0:T(8,128)(2,1)S(1)} copy-done((bf16[256,4096]{1,0:T(8,128)(2,1)S(1)}, bf16[256,4096]{1,0:T(8,128)(2,1)}, u32[]{:S(2)}) %copy-start.5) | copy-done | bytes 2097176
  29.1 4.7 %first_pass.1.dval_ref = bf16[256,512]{1,0:T(8,128)(2,1)S(1)} custom-call(s32[2,128]{1,0:T(2,128)S(1)} %copy-done.19, bf16[256,4096]{1,0:T(8,128)(2,1)S(1)} %copy-done.3, bf16[256,512]{1,0:T(8,128)(2,1)S(1)} %copy-done.13, bf16[256,4096]{1,0:T(8,128)(2,1)S(1)} %copy-done.5), custom_call_target="tpu_custom_call" | custom-call | bytes 231000 | tf_op jit(solution)/shard_map/first_pass/pallas_call | solution.py:506
  33.8 3.9 %collective-permute-done.2.refs_4_ = bf16[256,1280]{1,0:T(8,128)(2,1)} collective-permute-done((bf16[256,1280]{1,0:T(8,128)(2,1)}, bf16[256,1280]{1,0:T(8,128)(2,1)}, u32[]{:S(2)}, u32[]{:S(2)}) %collective-permute-start.2) | collective-permute-done | bytes 655392 | tf_op jit(solution)/shard_map/ppermute | solution.py:441
  37.7 4.1 %collective-permute-done.3.refs_5_ = bf16[256,1280]{1,0:T(8,128)(2,1)} collective-permute-done((bf16[256,1280]{1,0:T(8,128)(2,1)}, bf16[256,1280]{1,0:T(8,128)(2,1)}, u32[]{:S(2)}, u32[]{:S(2)}) %collective-permute-start.3) | collective-permute-done | bytes 655392 | tf_op jit(solution)/shard_map/ppermute | solution.py:441
  41.8 1.2 store_rows.1.store_ref
  43.1 0.7 shift-right-arithmetic_add_fusion.slot_ref.up_slot_ref
  43.7 0.4 collective-permute-done.4
  44.1 1.3 %pad_maximum_fusion = bf16[2,4,2,64,512]{4,3,2,1,0:T(8,128)(2,1)S(1)} fusion(bf16[1,4,2,64,512]{4,3,2,1,0:T(8,128)(2,1)} %bitcast.1, bf16[1,4,2,64,512]{4,3,2,1,0:T(8,128)(2,1)} %bitcast), kind=kLoop, calls=%fused_computation.1 | loop fusion | flops 524288 | bytes 2097152 | tf_op jit(solution)/shard_map/stack | solution.py:527
  45.4 0.7 copy-done.20
  46.1 0.9 grad_hidden.1.refs_0_
  47.0 1.0 copy-done.1
  48.0 0.6 copy-done.15
  48.6 1.3 %all-to-all-done.1.refs_7_.refs_0_ = bf16[16,32,640]{2,1,0:T(8,128)(2,1)S(1)} async-done(((bf16[16,32,640]{2,1,0:T(8,128)(2,1)}), bf16[16,32,640]{2,1,0:T(8,128)(2,1)S(1)}, u32[]{:S(2)}, u32[]{:S(2)}) %all-to-all-start.1) | async-done | bytes 655392 | tf_op jit(solution)/shard_map/all_to_all | solution.py:525
  49.8 1.3 %collective-permute-start.7 = (bf16[80,256]{1,0:T(8,128)(2,1)}, bf16[80,256]{1,0:T(8,128)(2,1)S(1)}, u32[]{:S(2)}, u32[]{:S(2)}) collective-permute-start(bf16[80,256]{1,0:T(8,128)(2,1)} %copy-done.15), channel_id=1, source_target_pairs={{0,6},{1,7},{2,4},{3,5},{4,2},{5,3},{6,0},{7,1},{8,14},{9,15},{10,... | collective-permute-start | bytes 122888 | tf_op jit(solution)/shard_map/ppermute | solution.py:441
  51.1 2.2 %collective-permute-start.5 = (bf16[80,256]{1,0:T(8,128)(2,1)}, bf16[80,256]{1,0:T(8,128)(2,1)S(1)}, u32[]{:S(2)}, u32[]{:S(2)}) collective-permute-start(bf16[80,256]{1,0:T(8,128)(2,1)} %copy-done.15), channel_id=1, source_target_pairs={{0,2},{1,3},{2,0},{3,1},{4,6},{5,7},{6,4},{7,5},{8,10},{9,11},{10,... | collective-permute-start | bytes 122888 | tf_op jit(solution)/shard_map/ppermute | solution.py:441
  53.3 1.5 %collective-permute-start.10 = (bf16[16,32,640]{2,1,0:T(8,128)(2,1)S(1)}, bf16[16,32,640]{2,1,0:T(8,128)(2,1)S(1)}, u32[]{:S(2)}, u32[]{:S(2)}) collective-permute-start(bf16[16,32,640]{2,1,0:T(8,128)(2,1)S(1)} %all-to-all-done.1.refs_7_.refs_0_), channel_id=1, source_target_pairs={{0,16},{16,0},{1,17},{17,1},{2,18},{18,2},{3,19},{19,3},{4,20},{20... | collective-permute-start | bytes 1966088 | tf_op jit(solution)/shard_map/ppermute | solution.py:551
  54.8 6.7 %collective-permute-done.8.refs_6_ = bf16[256,1280]{1,0:T(8,128)(2,1)} collective-permute-done((bf16[256,1280]{1,0:T(8,128)(2,1)}, bf16[256,1280]{1,0:T(8,128)(2,1)}, u32[]{:S(2)}, u32[]{:S(2)}) %collective-permute-start.8) | collective-permute-done | bytes 655392 | tf_op jit(solution)/shard_map/ppermute | solution.py:441
  61.6 0.7 collective-permute-done.7.refs_3_
  62.3 0.4 collective-permute-done.5.refs_1_
  62.7 0.8 copy-done.16
  63.5 2.4 %grad_down.1 = (bf16[16,64,640]{2,1,0:T(8,128)(2,1)S(1)}, bf16[16,64,640]{2,1,0:T(8,128)(2,1)S(1)}) custom-call(bf16[256,5120]{1,0:T(8,128)(2,1)S(1)} %copy-done, bf16[80,256]{1,0:T(8,128)(2,1)S(1)} %copy-done.16, bf16[80,256]{1,0:T(8,128)(2,1)S(1)} %collective-permute-done.5.refs_1_, bf16[80,256]{1,0:T(8,128)(2,1)S(1)} %collective-permute-done.6.refs_2_, ...), custom_call_target="tpu_custom_call" | custom-call | bytes 99000 | tf_op jit(solution)/shard_map/grad_down/pallas_call | solution.py:574
  66.0 0.1 collective-permute-start.9
  66.0 0.5 collective-permute-start.11
  66.5 1.5 %collective-permute-done.10.refs_8_.refs_1_ = bf16[16,32,640]{2,1,0:T(8,128)(2,1)S(1)} collective-permute-done((bf16[16,32,640]{2,1,0:T(8,128)(2,1)S(1)}, bf16[16,32,640]{2,1,0:T(8,128)(2,1)S(1)}, u32[]{:S(2)}, u32[]{:S(2)}) %collective-permute-start.10) | collective-permute-done | bytes 655392 | tf_op jit(solution)/shard_map/ppermute | solution.py:551
  68.0 0.8 fusion.1
  68.8 4.7 %collective-permute-start.13 = (bf16[4,80,256]{2,1,0:T(8,128)(2,1)S(1)}, bf16[4,80,256]{2,1,0:T(8,128)(2,1)S(1)}, u32[]{:S(2)}, u32[]{:S(2)}) collective-permute-start(bf16[4,80,256]{2,1,0:T(8,128)(2,1)S(1)} %get-tuple-element.105), channel_id=1, source_target_pairs={{0,8},{1,9},{2,10},{3,11},{4,12},{5,13},{6,14},{7,15},{8,0},{9,1},... | collective-permute-start | bytes 491528 | tf_op jit(solution)/shard_map/ppermute | solution.py:441
  73.5 3.1 %hidden.1 = (f32[64,256]{1,0:T(8,128)S(1)}, f32[64,256]{1,0:T(8,128)S(1)}, f32[64,256]{1,0:T(8,128)S(1)}, f32[64,256]{1,0:T(8,128)S(1)}) custom-call(bf16[256,5120]{1,0:T(8,128)(2,1)S(1)} %copy-done, bf16[80,256]{1,0:T(8,128)(2,1)S(1)} %copy-done.17, bf16[80,256]{1,0:T(8,128)(2,1)S(1)} %collective-permute-done.5.refs_1_, ...), custom_call_target="tpu_custom_call" | custom-call | bytes 99000 | tf_op jit(solution)/shard_map/hidden/pallas_call | solution.py:555
  76.7 0.8 copy-done.9
  77.5 0.3 collective-permute-start.14
  77.8 0.6 collective-permute-start.15
  78.4 2.6 %collective-permute-start.16 = (f32[64,256]{1,0:T(8,128)S(1)}, f32[64,256]{1,0:T(8,128)S(1)}, u32[]{:S(2)}, u32[]{:S(2)}) collective-permute-start(f32[64,256]{1,0:T(8,128)S(1)} %get-tuple-element.80), channel_id=1, source_target_pairs={{0,6},{1,7},{2,4},{3,5},{4,2},{5,3},{6,0},{7,1},{8,14},{9,15},{10,... | collective-permute-start | bytes 196616 | tf_op jit(solution)/shard_map/ppermute | solution.py:441
  81.0 1.5 %add_convert_fusion.refs_4_ = bf16[16,64,640]{2,1,0:T(8,128)(2,1)} fusion(bf16[16,64,640]{2,1,0:T(8,128)(2,1)S(1)} %collective-permute-done.9, bf16[16,64,640]{2,1,0:T(8,128)(2,1)S(1)} %get-tuple-element.68), kind=kLoop, calls=%fused_computation | loop fusion | flops 2621440 | bytes 3932160 | tf_op jit(solution)/shard_map/convert_element_type | solution.py:592
  82.5 0.5 collective-permute-done.15.refs_2_
  83.0 1.3 %collective-permute-done.16.refs_3_ = f32[64,256]{1,0:T(8,128)S(1)} collective-permute-done((f32[64,256]{1,0:T(8,128)S(1)}, f32[64,256]{1,0:T(8,128)S(1)}, u32[]{:S(2)}, u32[]{:S(2)}) %collective-permute-start.16) | collective-permute-done | bytes 65568 | tf_op jit(solution)/shard_map/ppermute | solution.py:441
  84.3 0.8 values.1
  85.2 4.7 %all-to-all-start.2 = ((bf16[16,64,640]{2,1,0:T(8,128)(2,1)}), bf16[16,64,640]{2,1,0:T(8,128)(2,1)}, u32[]{:S(2)}, u32[]{:S(2)}) async-start(bf16[16,64,640]{2,1,0:T(8,128)(2,1)} %add_convert_fusion.refs_4_), calls=%async_computation.2 | async-start | bytes 2621440 | tf_op jit(solution)/shard_map/all_to_all | solution.py:610
  90.0 0.4 collective-permute-start
  90.4 0.1 collective-permute-start.17
  90.6 1.0 fusion
  91.6 0.4 collective-permute-start.20
  92.0 0.1 add_xor_fusion.slot_ref
  92.1 0.7 place.1
  92.8 1.7 %collective-permute-start.18 = (bf16[4,64,512]{2,1,0:T(8,128)(2,1)S(1)}, bf16[4,64,512]{2,1,0:T(8,128)(2,1)S(1)}, u32[]{:S(2)}, u32[]{:S(2)}) collective-permute-start(bf16[4,64,512]{2,1,0:T(8,128)(2,1)S(1)} %get-tuple-element.88), channel_id=1, source_target_pairs={{0,2},{1,3},{2,0},{3,1},{4,6},{5,7},{6,4},{7,5},{8,10},{9,11},{10,... | collective-permute-start | bytes 786440 | tf_op jit(solution)/shard_map/ppermute | solution.py:441
  94.5 1.6 %copy-done.6 = bf16[256,4096]{1,0:T(8,128)(2,1)S(1)} copy-done((bf16[256,4096]{1,0:T(8,128)(2,1)S(1)}, bf16[256,4096]{1,0:T(8,128)(2,1)}, u32[]{:S(2)}) %copy-start.6) | copy-done | bytes 2097176
  96.1 6.9 %second_pass.1 = bf16[256,4096]{1,0:T(8,128)(2,1)} custom-call(s32[2,128]{1,0:T(2,128)S(1)} %copy-done.19, bf16[256,4096]{1,0:T(8,128)(2,1)S(1)} %copy-done.4, bf16[256,512]{1,0:T(8,128)(2,1)S(1)} %copy-done.14, bf16[256,512]{1,0:T(8,128)(2,1)S(1)} %get-tuple-element.90.value_ref, bf16[256,4096]{1,0:T(8,128)(2,1)S(1)} %copy-done.6), custom_call_target="tpu_custom_call" | custom-call | bytes 297000 | tf_op jit(solution)/shard_map/second_pass/pallas_call | solution.py:613
  103.0 6.2 %collective-permute-done.18.came_ref = bf16[4,64,512]{2,1,0:T(8,128)(2,1)S(1)} collective-permute-done((bf16[4,64,512]{2,1,0:T(8,128)(2,1)S(1)}, bf16[4,64,512]{2,1,0:T(8,128)(2,1)S(1)}, u32[]{:S(2)}, u32[]{:S(2)}) %collective-permute-start.18) | collective-permute-done | bytes 262176 | tf_op jit(solution)/shard_map/ppermute | solution.py:441
  109.2 0.1 collective-permute-start.19
  109.3 0.1 pad_maximum_fusion.1
  109.5 4.6 %grad_input.1 = bf16[320,4096]{1,0:T(8,128)(2,1)} custom-call(bf16[16,80,256]{2,1,0:T(8,128)(2,1)S(1)} %bitcast.16, bf16[16,32,640]{2,1,0:T(8,128)(2,1)S(1)} %all-to-all-done.1.refs_7_.refs_0_, bf16[16,32,640]{2,1,0:T(8,128)(2,1)S(1)} %copy-done.8, bf16[16,32,640]{2,1,0:T(8,128)(2,1)S(1)} %copy-done.10, bf16[16,32,640]{2,1,0:T(8,128)(2,1)S(1)} %copy-done.12), custom_call_target="tpu_custom_call" | custom-call | bytes 231000 | tf_op jit(solution)/shard_map/grad_input/pallas_call | solution.py:626
  114.1 1.0 collective-permute-done.19.came_ref
  115.1 4.4 %collective-permute-start.21 = (bf16[1,64,512]{2,1,0:T(8,128)(2,1)S(1)}, bf16[1,64,512]{2,1,0:T(8,128)(2,1)S(1)}, u32[]{:S(2)}, u32[]{:S(2)}) collective-permute-start(bf16[1,64,512]{2,1,0:T(8,128)(2,1)S(1)} %get-tuple-element.100), channel_id=1, source_target_pairs={{0,8},{1,9},{2,10},{3,11},{4,12},{5,13},{6,14},{7,15},{8,0},{9,1},... | collective-permute-start | bytes 196616 | tf_op jit(solution)/shard_map/ppermute | solution.py:441
  119.5 2.3 %sum_down.1 = (bf16[1,64,5120]{2,1,0:T(8,128)(2,1)}, f32[8,128]{1,0:T(8,128)S(1)}) custom-call(bf16[16,64,640]{2,1,0:T(8,128)(2,1)} %all-to-all-done.2.part_ref), custom_call_target="tpu_custom_call" | custom-call | bytes 66000 | tf_op jit(solution)/shard_map/sum_down/pallas_call | solution.py:644
  121.8 3.1 %collective-permute-done.21.came_ref = bf16[1,64,512]{2,1,0:T(8,128)(2,1)S(1)} collective-permute-done((bf16[1,64,512]{2,1,0:T(8,128)(2,1)S(1)}, bf16[1,64,512]{2,1,0:T(8,128)(2,1)S(1)}, u32[]{:S(2)}, u32[]{:S(2)}) %collective-permute-start.21) | collective-permute-done | bytes 65568 | tf_op jit(solution)/shard_map/ppermute | solution.py:441
  124.9 0.6 halve.5
  (58 shorter events, 0.3 us)
Async XLA Ops:
  0.6 8.0 %copy-start.23 = (bf16[1,64,512]{2,1,0:T(8,128)(2,1)S(1)}, bf16[1,64,512]{2,1,0:T(8,128)(2,1)}, u32[]{:S(2)}) copy-start(bf16[1,64,512]{2,1,0:T(8,128)(2,1)} %param.16) | copy-start | bytes 196612
  0.6 8.0 %collective-permute-start.1 = (bf16[1,64,512]{2,1,0:T(8,128)(2,1)}, bf16[1,64,512]{2,1,0:T(8,128)(2,1)S(1)}, u32[]{:S(2)}, u32[]{:S(2)}) collective-permute-start(bf16[1,64,512]{2,1,0:T(8,128)(2,1)} %param.16), channel_id=1, source_target_pairs={{0,8},{1,9},{2,10},{3,11},{4,12},{5,13},{6,14},{7,15},{8,0},{9,1},... | collective-permute-start | bytes 196616 | tf_op jit(solution)/shard_map/ppermute | solution.py:441
  7.5 19.9 %copy-start.3 = (bf16[256,4096]{1,0:T(8,128)(2,1)S(1)}, bf16[256,4096]{1,0:T(8,128)(2,1)}, u32[]{:S(2)}) copy-start(bf16[256,4096]{1,0:T(8,128)(2,1)} %query_ref.3) | copy-start | bytes 6291460
  7.5 19.9 %copy-start.13 = (bf16[256,512]{1,0:T(8,128)(2,1)S(1)}, bf16[256,512]{1,0:T(8,128)(2,1)}, u32[]{:S(2)}) copy-start(bf16[256,512]{1,0:T(8,128)(2,1)} %key_ref.3) | copy-start | bytes 786436
  7.6 19.9 %copy-start.19 = (s32[2,128]{1,0:T(2,128)S(1)}, s32[2,128]{1,0:T(2,128)}, u32[]{:S(2)}) copy-start(s32[2,128]{1,0:T(2,128)} %ids_ref.3) | copy-start | bytes 3076
  9.5 13.6 %all-to-all-start = ((bf16[4,2,64,512]{3,2,1,0:T(8,128)(2,1)}), bf16[4,2,64,512]{3,2,1,0:T(8,128)(2,1)}, u32[]{:S(2)}, u32[]{:S(2)}) async-start(bf16[4,2,64,512]{3,2,1,0:T(8,128)(2,1)} %broadcast_in_dim.3), calls=%async_computation | async-start | bytes 1048576 | tf_op jit(solution)/shard_map/all_to_all | solution.py:520
  13.6 24.1 %collective-permute-start.2 = (bf16[256,1280]{1,0:T(8,128)(2,1)}, bf16[256,1280]{1,0:T(8,128)(2,1)}, u32[]{:S(2)}, u32[]{:S(2)}) collective-permute-start(bf16[256,1280]{1,0:T(8,128)(2,1)} %get-tuple-element.59), channel_id=1, source_target_pairs={{0,2},{1,3},{2,0},{3,1},{4,6},{5,7},{6,4},{7,5},{8,10},{9,11},{10,... | collective-permute-start | bytes 1966088 | tf_op jit(solution)/shard_map/ppermute | solution.py:441
  15.6 26.3 %collective-permute-start.3 = (bf16[256,1280]{1,0:T(8,128)(2,1)}, bf16[256,1280]{1,0:T(8,128)(2,1)}, u32[]{:S(2)}, u32[]{:S(2)}) collective-permute-start(bf16[256,1280]{1,0:T(8,128)(2,1)} %get-tuple-element.60), channel_id=1, source_target_pairs={{0,4},{1,5},{2,6},{3,7},{4,0},{5,1},{6,2},{7,3},{8,12},{9,13},{10,... | collective-permute-start | bytes 1966088 | tf_op jit(solution)/shard_map/ppermute | solution.py:441
  23.1 26.7 %all-to-all-start.1 = ((bf16[16,32,640]{2,1,0:T(8,128)(2,1)}), bf16[16,32,640]{2,1,0:T(8,128)(2,1)S(1)}, u32[]{:S(2)}, u32[]{:S(2)}) async-start(bf16[16,32,640]{2,1,0:T(8,128)(2,1)} %get-tuple-element.58), calls=%async_computation.1 | async-start | bytes 1310720 | tf_op jit(solution)/shard_map/all_to_all | solution.py:525
  27.5 1.6 %copy-start.5 = (bf16[256,4096]{1,0:T(8,128)(2,1)S(1)}, bf16[256,4096]{1,0:T(8,128)(2,1)}, u32[]{:S(2)}) copy-start(bf16[256,4096]{1,0:T(8,128)(2,1)} %grad_ref.3) | copy-start | bytes 6291460
  33.8 28.9 %copy-start = (bf16[256,5120]{1,0:T(8,128)(2,1)S(1)}, bf16[256,5120]{1,0:T(8,128)(2,1)}, u32[]{:S(2)}) copy-start(bf16[256,5120]{1,0:T(8,128)(2,1)} %x_ref.5) | copy-start | bytes 7864324
  41.8 2.3 %collective-permute-start.4 = (bf16[4,2,64,512]{3,2,1,0:T(8,128)(2,1)}, bf16[4,2,64,512]{3,2,1,0:T(8,128)(2,1)}, u32[]{:S(2)}, u32[]{:S(2)}) collective-permute-start(bf16[4,2,64,512]{3,2,1,0:T(8,128)(2,1)} %all-to-all-done), channel_id=1, source_target_pairs={{0,1},{1,0},{2,3},{3,2},{4,5},{5,4},{6,7},{7,6},{8,9},{9,8},{10,11... | collective-permute-start | bytes 1572872 | tf_op jit(solution)/shard_map/ppermute | solution.py:441
  41.8 19.7 %collective-permute-start.8 = (bf16[256,1280]{1,0:T(8,128)(2,1)}, bf16[256,1280]{1,0:T(8,128)(2,1)}, u32[]{:S(2)}, u32[]{:S(2)}) collective-permute-start(bf16[256,1280]{1,0:T(8,128)(2,1)} %get-tuple-element.67), channel_id=1, source_target_pairs={{0,6},{1,7},{2,4},{3,5},{4,2},{5,3},{6,0},{7,1},{8,14},{9,15},{10,... | collective-permute-start | bytes 1966088 | tf_op jit(solution)/shard_map/ppermute | solution.py:441
  45.4 0.7 copy-start.20
  47.0 1.0 copy-start.1
  48.0 0.6 copy-start.15
  49.8 12.4 %collective-permute-start.7 = (bf16[80,256]{1,0:T(8,128)(2,1)}, bf16[80,256]{1,0:T(8,128)(2,1)S(1)}, u32[]{:S(2)}, u32[]{:S(2)}) collective-permute-start(bf16[80,256]{1,0:T(8,128)(2,1)} %copy-done.15), channel_id=1, source_target_pairs={{0,6},{1,7},{2,4},{3,5},{4,2},{5,3},{6,0},{7,1},{8,14},{9,15},{10,... | collective-permute-start | bytes 122888 | tf_op jit(solution)/shard_map/ppermute | solution.py:441
  51.1 11.1 %collective-permute-start.6 = (bf16[80,256]{1,0:T(8,128)(2,1)}, bf16[80,256]{1,0:T(8,128)(2,1)S(1)}, u32[]{:S(2)}, u32[]{:S(2)}) collective-permute-start(bf16[80,256]{1,0:T(8,128)(2,1)} %copy-done.15), channel_id=1, source_target_pairs={{0,4},{1,5},{2,6},{3,7},{4,0},{5,1},{6,2},{7,3},{8,12},{9,13},{10,... | collective-permute-start | bytes 122888 | tf_op jit(solution)/shard_map/ppermute | solution.py:441
  51.1 11.6 %collective-permute-start.5 = (bf16[80,256]{1,0:T(8,128)(2,1)}, bf16[80,256]{1,0:T(8,128)(2,1)S(1)}, u32[]{:S(2)}, u32[]{:S(2)}) collective-permute-start(bf16[80,256]{1,0:T(8,128)(2,1)} %copy-done.15), channel_id=1, source_target_pairs={{0,2},{1,3},{2,0},{3,1},{4,6},{5,7},{6,4},{7,5},{8,10},{9,11},{10,... | collective-permute-start | bytes 122888 | tf_op jit(solution)/shard_map/ppermute | solution.py:441
  53.3 14.7 %collective-permute-start.10 = (bf16[16,32,640]{2,1,0:T(8,128)(2,1)S(1)}, bf16[16,32,640]{2,1,0:T(8,128)(2,1)S(1)}, u32[]{:S(2)}, u32[]{:S(2)}) collective-permute-start(bf16[16,32,640]{2,1,0:T(8,128)(2,1)S(1)} %all-to-all-done.1.refs_7_.refs_0_), channel_id=1, source_target_pairs={{0,16},{16,0},{1,17},{17,1},{2,18},{18,2},{3,19},{19,3},{4,20},{20... | collective-permute-start | bytes 1966088 | tf_op jit(solution)/shard_map/ppermute | solution.py:551
  62.7 0.8 copy-start.16
  63.5 10.0 %copy-start.17 = (bf16[80,256]{1,0:T(8,128)(2,1)S(1)}, bf16[80,256]{1,0:T(8,128)(2,1)}, u32[]{:S(2)}) copy-start(bf16[80,256]{1,0:T(8,128)(2,1)} %copy-done.15) | copy-start | bytes 122884
  66.0 15.0 %collective-permute-start.9 = (bf16[16,64,640]{2,1,0:T(8,128)(2,1)S(1)}, bf16[16,64,640]{2,1,0:T(8,128)(2,1)S(1)}, u32[]{:S(2)}, u32[]{:S(2)}) collective-permute-start(bf16[16,64,640]{2,1,0:T(8,128)(2,1)S(1)} %get-tuple-element.69), channel_id=1, source_target_pairs={{0,1},{1,0},{2,3},{3,2},{4,5},{5,4},{6,7},{7,6},{8,9},{9,8},{10,11... | collective-permute-start | bytes 3932168 | tf_op jit(solution)/shard_map/ppermute | solution.py:441
  66.0 7.5 %collective-permute-start.11 = (bf16[16,32,640]{2,1,0:T(8,128)(2,1)S(1)}, bf16[16,32,640]{2,1,0:T(8,128)(2,1)S(1)}, u32[]{:S(2)}, u32[]{:S(2)}) collective-permute-start(bf16[16,32,640]{2,1,0:T(8,128)(2,1)S(1)} %all-to-all-done.1.refs_7_.refs_0_), channel_id=1, source_target_pairs={{0,1},{1,0},{2,3},{3,2},{4,5},{5,4},{6,7},{7,6},{8,9},{9,8},{10,11... | collective-permute-start | bytes 1966088 | tf_op jit(solution)/shard_map/ppermute | solution.py:441
  68.0 8.6 %copy-start.7 = (bf16[16,32,640]{2,1,0:T(8,128)(2,1)}, bf16[16,32,640]{2,1,0:T(8,128)(2,1)S(1)}, u32[]{:S(2)}) copy-start(bf16[16,32,640]{2,1,0:T(8,128)(2,1)S(1)} %collective-permute-done.10.refs_8_.refs_1_) | copy-start | bytes 1966084
  68.0 5.5 %collective-permute-start.12 = (bf16[16,32,640]{2,1,0:T(8,128)(2,1)S(1)}, bf16[16,32,640]{2,1,0:T(8,128)(2,1)S(1)}, u32[]{:S(2)}, u32[]{:S(2)}) collective-permute-start(bf16[16,32,640]{2,1,0:T(8,128)(2,1)S(1)} %collective-permute-done.10.refs_8_.refs_1_), channel_id=1, source_target_pairs={{0,1},{1,0},{2,3},{3,2},{4,5},{5,4},{6,7},{7,6},{8,9},{9,8},{10,11... | collective-permute-start | bytes 1966088 | tf_op jit(solution)/shard_map/ppermute | solution.py:441
  68.8 13.7 %collective-permute-start.13 = (bf16[4,80,256]{2,1,0:T(8,128)(2,1)S(1)}, bf16[4,80,256]{2,1,0:T(8,128)(2,1)S(1)}, u32[]{:S(2)}, u32[]{:S(2)}) collective-permute-start(bf16[4,80,256]{2,1,0:T(8,128)(2,1)S(1)} %get-tuple-element.105), channel_id=1, source_target_pairs={{0,8},{1,9},{2,10},{3,11},{4,12},{5,13},{6,14},{7,15},{8,0},{9,1},... | collective-permute-start | bytes 491528 | tf_op jit(solution)/shard_map/ppermute | solution.py:441
  73.5 3.1 %copy-start.11 = (bf16[16,32,640]{2,1,0:T(8,128)(2,1)}, bf16[16,32,640]{2,1,0:T(8,128)(2,1)S(1)}, u32[]{:S(2)}) copy-start(bf16[16,32,640]{2,1,0:T(8,128)(2,1)S(1)} %collective-permute-done.12.refs_10_.refs_3_) | copy-start | bytes 1966084
  76.7 0.8 copy-start.9
  77.5 6.8 %copy-start.2 = (bf16[2,4,2,64,512]{4,3,2,1,0:T(8,128)(2,1)S(1)}, bf16[2,4,2,64,512]{4,3,2,1,0:T(8,128)(2,1)}, u32[]{:S(2)}) copy-start(bf16[2,4,2,64,512]{4,3,2,1,0:T(8,128)(2,1)} %copy-done.1) | copy-start | bytes 3145732
  77.5 6.8 %copy-start.18 = (bf16[256,512]{1,0:T(8,128)(2,1)S(1)}, bf16[256,512]{1,0:T(8,128)(2,1)}, u32[]{:S(2)}) copy-start(bf16[256,512]{1,0:T(8,128)(2,1)} %base_ref.1) | copy-start | bytes 786436
  77.5 5.0 %collective-permute-start.14 = (f32[64,256]{1,0:T(8,128)S(1)}, f32[64,256]{1,0:T(8,128)S(1)}, u32[]{:S(2)}, u32[]{:S(2)}) collective-permute-start(f32[64,256]{1,0:T(8,128)S(1)} %get-tuple-element.78), channel_id=1, source_target_pairs={{0,2},{1,3},{2,0},{3,1},{4,6},{5,7},{6,4},{7,5},{8,10},{9,11},{10,... | collective-permute-start | bytes 196616 | tf_op jit(solution)/shard_map/ppermute | solution.py:441
  77.8 5.2 %collective-permute-start.15 = (f32[64,256]{1,0:T(8,128)S(1)}, f32[64,256]{1,0:T(8,128)S(1)}, u32[]{:S(2)}, u32[]{:S(2)}) collective-permute-start(f32[64,256]{1,0:T(8,128)S(1)} %get-tuple-element.79), channel_id=1, source_target_pairs={{0,4},{1,5},{2,6},{3,7},{4,0},{5,1},{6,2},{7,3},{8,12},{9,13},{10,... | collective-permute-start | bytes 196616 | tf_op jit(solution)/shard_map/ppermute | solution.py:441
  78.4 6.0 %collective-permute-start.16 = (f32[64,256]{1,0:T(8,128)S(1)}, f32[64,256]{1,0:T(8,128)S(1)}, u32[]{:S(2)}, u32[]{:S(2)}) collective-permute-start(f32[64,256]{1,0:T(8,128)S(1)} %get-tuple-element.80), channel_id=1, source_target_pairs={{0,6},{1,7},{2,4},{3,5},{4,2},{5,3},{6,0},{7,1},{8,14},{9,15},{10,... | collective-permute-start | bytes 196616 | tf_op jit(solution)/shard_map/ppermute | solution.py:441
  82.5 2.7 %copy-start.22 = (bf16[4,80,256]{2,1,0:T(8,128)(2,1)}, bf16[4,80,256]{2,1,0:T(8,128)(2,1)S(1)}, u32[]{:S(2)}) copy-start(bf16[4,80,256]{2,1,0:T(8,128)(2,1)S(1)} %collective-permute-done.13) | copy-start | bytes 491524
  85.2 4.8 %copy-start.21 = (s32[2]{0:T(128)S(1)}, s32[2]{0:T(128)}, u32[]{:S(2)}) copy-start(s32[2]{0:T(128)} %store_rows.1.store_ref) | copy-start | bytes 28
  85.2 9.3 %copy-start.4 = (bf16[256,4096]{1,0:T(8,128)(2,1)S(1)}, bf16[256,4096]{1,0:T(8,128)(2,1)}, u32[]{:S(2)}) copy-start(bf16[256,4096]{1,0:T(8,128)(2,1)} %query_ref.3) | copy-start | bytes 6291460
  85.2 9.3 %copy-start.14 = (bf16[256,512]{1,0:T(8,128)(2,1)S(1)}, bf16[256,512]{1,0:T(8,128)(2,1)}, u32[]{:S(2)}) copy-start(bf16[256,512]{1,0:T(8,128)(2,1)} %key_ref.3) | copy-start | bytes 786436
  85.2 34.3 %all-to-all-start.2 = ((bf16[16,64,640]{2,1,0:T(8,128)(2,1)}), bf16[16,64,640]{2,1,0:T(8,128)(2,1)}, u32[]{:S(2)}, u32[]{:S(2)}) async-start(bf16[16,64,640]{2,1,0:T(8,128)(2,1)} %add_convert_fusion.refs_4_), calls=%async_computation.2 | async-start | bytes 2621440 | tf_op jit(solution)/shard_map/all_to_all | solution.py:610
  90.0 2.0 %collective-permute-start = (s32[2]{0:T(128)S(1)}, s32[2]{0:T(128)S(1)}, u32[]{:S(2)}, u32[]{:S(2)}) collective-permute-start(s32[2]{0:T(128)S(1)} %copy-done.21), channel_id=1, source_target_pairs={{0,1},{1,0},{2,3},{3,2},{4,5},{5,4},{6,7},{7,6},{8,9},{9,8},{10,11... | collective-permute-start | bytes 32 | tf_op jit(solution)/shard_map/ppermute | solution.py:441
  90.4 1.7 %collective-permute-start.17 = (bf16[2,64,512]{2,1,0:T(8,128)(2,1)S(1)}, bf16[2,64,512]{2,1,0:T(8,128)(2,1)S(1)}, u32[]{:S(2)}, u32[]{:S(2)}) collective-permute-start(bf16[2,64,512]{2,1,0:T(8,128)(2,1)S(1)} %get-tuple-element.86.own_ref), channel_id=1, source_target_pairs={{0,1},{1,0},{2,3},{3,2},{4,5},{5,4},{6,7},{7,6},{8,9},{9,8},{10,11... | collective-permute-start | bytes 393224 | tf_op jit(solution)/shard_map/ppermute | solution.py:441
  91.6 17.7 %collective-permute-start.20 = (bf16[2,4,80,256]{3,2,1,0:T(8,128)(2,1)S(1)}, bf16[2,4,80,256]{3,2,1,0:T(8,128)(2,1)S(1)}, u32[]{:S(2)}, u32[]{:S(2)}) collective-permute-start(bf16[2,4,80,256]{3,2,1,0:T(8,128)(2,1)S(1)} %get-tuple-element.103), channel_id=1, source_target_pairs={{0,1},{1,0},{2,3},{3,2},{4,5},{5,4},{6,7},{7,6},{8,9},{9,8},{10,11... | collective-permute-start | bytes 983048 | tf_op jit(solution)/shard_map/ppermute | solution.py:441
  92.8 16.4 %collective-permute-start.18 = (bf16[4,64,512]{2,1,0:T(8,128)(2,1)S(1)}, bf16[4,64,512]{2,1,0:T(8,128)(2,1)S(1)}, u32[]{:S(2)}, u32[]{:S(2)}) collective-permute-start(bf16[4,64,512]{2,1,0:T(8,128)(2,1)S(1)} %get-tuple-element.88), channel_id=1, source_target_pairs={{0,2},{1,3},{2,0},{3,1},{4,6},{5,7},{6,4},{7,5},{8,10},{9,11},{10,... | collective-permute-start | bytes 786440 | tf_op jit(solution)/shard_map/ppermute | solution.py:441
  94.5 1.6 %copy-start.6 = (bf16[256,4096]{1,0:T(8,128)(2,1)S(1)}, bf16[256,4096]{1,0:T(8,128)(2,1)}, u32[]{:S(2)}) copy-start(bf16[256,4096]{1,0:T(8,128)(2,1)} %grad_ref.3) | copy-start | bytes 6291460
  103.0 6.5 %copy-start.8 = (bf16[16,32,640]{2,1,0:T(8,128)(2,1)S(1)}, bf16[16,32,640]{2,1,0:T(8,128)(2,1)}, u32[]{:S(2)}) copy-start(bf16[16,32,640]{2,1,0:T(8,128)(2,1)} %copy-done.7) | copy-start | bytes 1966084
  103.0 6.5 %copy-start.10 = (bf16[16,32,640]{2,1,0:T(8,128)(2,1)S(1)}, bf16[16,32,640]{2,1,0:T(8,128)(2,1)}, u32[]{:S(2)}) copy-start(bf16[16,32,640]{2,1,0:T(8,128)(2,1)} %copy-done.9) | copy-start | bytes 1966084
  103.0 6.5 %copy-start.12 = (bf16[16,32,640]{2,1,0:T(8,128)(2,1)S(1)}, bf16[16,32,640]{2,1,0:T(8,128)(2,1)}, u32[]{:S(2)}) copy-start(bf16[16,32,640]{2,1,0:T(8,128)(2,1)} %copy-done.11) | copy-start | bytes 1966084
  109.2 5.8 %collective-permute-start.19 = (bf16[2,64,512]{2,1,0:T(8,128)(2,1)S(1)}, bf16[2,64,512]{2,1,0:T(8,128)(2,1)S(1)}, u32[]{:S(2)}, u32[]{:S(2)}) collective-permute-start(bf16[2,64,512]{2,1,0:T(8,128)(2,1)S(1)} %get-tuple-element.93), channel_id=1, source_target_pairs={{0,4},{1,5},{2,6},{3,7},{4,0},{5,1},{6,2},{7,3},{8,12},{9,13},{10,... | collective-permute-start | bytes 393224 | tf_op jit(solution)/shard_map/ppermute | solution.py:441
  115.1 9.8 %collective-permute-start.21 = (bf16[1,64,512]{2,1,0:T(8,128)(2,1)S(1)}, bf16[1,64,512]{2,1,0:T(8,128)(2,1)S(1)}, u32[]{:S(2)}, u32[]{:S(2)}) collective-permute-start(bf16[1,64,512]{2,1,0:T(8,128)(2,1)S(1)} %get-tuple-element.100), channel_id=1, source_target_pairs={{0,8},{1,9},{2,10},{3,11},{4,12},{5,13},{6,14},{7,15},{8,0},{9,1},... | collective-permute-start | bytes 196616 | tf_op jit(solution)/shard_map/ppermute | solution.py:441
